TPU v7x, 128 devices: a whole 4x4x4 slice. The times are simulated.
128 devices in a mesh: wide: 16 (over x, z), mid: 8 (over y, core).
Axes of the slice: x: 4, y: 4, z: 4, core: 2. Of those that a mesh axis runs over, the one named last changes fastest.
Arguments:
- noise: float32 [512, 256, 512], P('wide', 'mid'), may hold values from -6 to 6
- spectrum: float32 [512], replicated, may hold values from 0.3 to 1.2
- send_core: int32 [16, 8, 16], P('wide', 'mid'), may hold values from -1 to 127, as said below
- recv_source: int32 [16, 8, 8], P('wide', 'mid'), may hold values from 0 to 15, as said below
Outputs:
- coefficient: float32 [512, 256, 512], P('wide', 'mid')
- corrector: float32 [16, 8, 8, 48, 2304], P('wide', 'mid')
Inputs may be any that keep to these rules, and one draw needn't show every extreme that they name: Every owner has exactly 8 patches, whose sources are distinct devices of its own mid row; device (s, m) sends a core to owner (d, m) exactly when s is among recv_source[d, m], never the same core to two owners, and send_core is -1 otherwise. `recv_source`: listed in no particular order.
All inputs are finite; a program needn't handle non-finite values.
Results may differ from a plain program's by a relative error of at most 0.0003.
Values sent between devices are 32-bit elements; how exact they have to be, the bound alone decides.
No kernel may reach another device: no remote copies, remote signals or barrier semaphores. Data moves between devices by JAX's collectives and lax.ppermute only.
A program may use at most 256 MiB of HBM per device.

v0:
```python
import math

import jax
import jax.numpy as jnp
from jax import lax
from jax.sharding import PartitionSpec as P

CORE = 16
LAYER = 16
PATCH_DEV = 8
ITERS = 2
EDGE = 48


REACTION = 1.0
TINY = 1e-06


def with_halo(block, sides, width):
    for axis, dim in sides:
        count = lax.axis_size(axis)
        forward = [(i, i + 1) for i in range(count - 1)]
        backward = [(target, source) for source, target in forward]
        low = lax.ppermute(
            lax.slice_in_dim(block, block.shape[dim] - width, None, axis=dim), axis, forward
        )
        high = lax.ppermute(lax.slice_in_dim(block, 0, width, axis=dim), axis, backward)
        block = jnp.concatenate([low, block, high], axis=dim)
    return block


def up_x(values):
    return jnp.concatenate([values[:, 1:, :], jnp.zeros_like(values[:, :1, :])], axis=1)


def down_x(values):
    return jnp.concatenate([jnp.zeros_like(values[:, :1, :]), values[:, :-1, :]], axis=1)


def up_y(values):
    return jnp.concatenate([values[:, :, EDGE:], jnp.zeros_like(values[:, :, :EDGE])], axis=2)


def down_y(values):
    return jnp.concatenate([jnp.zeros_like(values[:, :, :EDGE]), values[:, :, :-EDGE]], axis=2)


def up_z(values, upper_mask):
    return (
        jnp.concatenate([values[:, :, 1:], jnp.zeros_like(values[:, :, :1])], axis=2) * upper_mask
    )


def down_z(values, lower_mask):
    return (
        jnp.concatenate([jnp.zeros_like(values[:, :, :1]), values[:, :, :-1]], axis=2) * lower_mask
    )


def neighbour_set(values, masks):
    return (
        up_x(values),
        down_x(values),
        up_y(values),
        down_y(values),
        up_z(values, masks[0]),
        down_z(values, masks[1]),
    )


def patch_sum(values):
    return jnp.sum(values, axis=(1, 2), keepdims=True)


def apply_operator(field, faces, masks):
    nearby = neighbour_set(field, masks)
    diagonal = REACTION + faces[0] + faces[1] + faces[2] + faces[3] + faces[4] + faces[5]
    couple = faces[0] * nearby[0] + faces[1] * nearby[1] + faces[2] * nearby[2]
    couple = couple + faces[3] * nearby[3] + faces[4] * nearby[4] + faces[5] * nearby[5]
    return diagonal * field - couple


def solve_patches(conduct):
    column = jnp.arange(EDGE * EDGE, dtype=jnp.int32) % EDGE
    masks = ((column != EDGE - 1).astype(jnp.float32), (column != 0).astype(jnp.float32))
    nearby = neighbour_set(conduct, masks)
    faces = tuple((0.5 * (conduct + other) for other in nearby))
    residual = faces[0] - faces[1]
    direction = residual
    solution = jnp.zeros_like(conduct)
    norm_now = patch_sum(residual * residual)
    for sweep_index in range(ITERS):
        image = apply_operator(direction, faces, masks)
        alpha = norm_now / (patch_sum(direction * image) + TINY)
        solution = solution + alpha * direction
        residual = residual - alpha * image
        norm_next = patch_sum(residual * residual)
        direction = residual + norm_next / (norm_now + TINY) * direction
        norm_now = norm_next
    return solution


def on_device(noise, spectrum, send_core, recv_source):
    pencil = lax.all_to_all(noise, "wide", split_axis=2, concat_axis=0, tiled=True)
    length, cells_y, slab_z = pencil.shape
    flat = pencil.reshape(length, cells_y * slab_z)
    freqs = jnp.arange(length, dtype=jnp.int32)
    phase = freqs[:, None] * freqs[None, :] % length
    angle = phase.astype(jnp.float32) * (2.0 * math.pi / length)
    cosine = jnp.cos(angle)
    sine = jnp.sin(angle)
    forward = jnp.dot(
        jnp.concatenate([cosine, sine], axis=0),
        flat,
        precision=lax.Precision.HIGHEST,
        preferred_element_type=jnp.float32,
    )
    weights = jnp.concatenate([spectrum, spectrum])[:, None]
    logfield = (
        jnp.dot(
            jnp.concatenate([cosine, sine], axis=1),
            forward * weights,
            precision=lax.Precision.HIGHEST,
            preferred_element_type=jnp.float32,
        )
        / length
    )
    coeff_pencil = jnp.exp(logfield).reshape(length, cells_y, slab_z)
    coefficient = lax.all_to_all(coeff_pencil, "wide", split_axis=0, concat_axis=2, tiled=True)
    depth_z = coefficient.shape[2]
    extended = with_halo(coefficient, (("wide", 0), ("mid", 1)), LAYER)
    cores_y = cells_y // CORE
    cores_z = depth_z // CORE
    depth_ids = jnp.arange(depth_z, dtype=jnp.int32)
    window_ids = jnp.arange(EDGE, dtype=jnp.int32)

    def cut_block(core_id):
        core_id = jnp.maximum(core_id, 0)
        index_x = core_id // (cores_y * cores_z)
        index_y = core_id // cores_z % cores_y
        index_z = core_id % cores_z
        column_block = lax.dynamic_slice(
            extended, (index_x * CORE, index_y * CORE, jnp.int32(0)), (EDGE, EDGE, depth_z)
        )
        selector = (depth_ids[:, None] == index_z * CORE - LAYER + window_ids[None, :]).astype(
            jnp.float32
        )
        block = jnp.einsum(
            "xyz,zj->xyj",
            column_block,
            selector,
            precision=lax.Precision.HIGHEST,
            preferred_element_type=jnp.float32,
        )
        return block.reshape(EDGE, EDGE * EDGE)

    outgoing = jax.vmap(cut_block)(send_core.reshape(-1))
    sources = recv_source.reshape(-1)
    incoming = lax.all_to_all(outgoing, "wide", split_axis=0, concat_axis=0, tiled=True)
    solved = solve_patches(jnp.take(incoming, sources, axis=0))
    return (coefficient, solved.reshape(1, 1, PATCH_DEV, EDGE, EDGE * EDGE))


def solution(mesh):
    in_specs = (P("wide", "mid", None), P(), P("wide", "mid", None), P("wide", "mid", None))
    out_specs = (P("wide", "mid", None), P("wide", "mid", None, None, None))
    return jax.shard_map(
        on_device, mesh=mesh, in_specs=in_specs, out_specs=out_specs, check_vma=False
    )
```

profile of v0, /device:TPU:77, one launch (start us, length us, event | category | flops | bytes accessed | tf_op | source)
XLA Modules:
  0.0 668.2 jit_solution(1540959118340942390)
XLA Ops:
  0.6 8.4 %copy.12 = f32[32,32,512]{1,0,2:T(8,128)} copy(f32[32,32,512]{2,1,0:T(8,128)} %param.4) | data formatting | bytes 4194304 | tf_op args[0]
  9.0 8.6 %reshape.308 = f32[16,1,32768]{2,1,0:T(1,128)} reshape(f32[512,32,32]{2,1,0:T(8,128)} %bitcast.68) | data formatting | bytes 4194304
  17.6 7.0 %all-to-all-start = ((f32[16,1,32768]{2,1,0:T(1,128)}), f32[16,1,32768]{2,1,0:T(1,128)}, u32[]{:S(2)}, u32[]{:S(2)}) async-start(f32[16,1,32768]{2,1,0:T(1,128)} %reshape.308), calls=%async_computation | async-start | bytes 4194304 | tf_op jit(solution)/shard_map/all_to_all | solution.py:104
  28.7 21.1 %all-to-all-done = f32[16,1,32768]{2,1,0:T(1,128)} async-done(((f32[16,1,32768]{2,1,0:T(1,128)}), f32[16,1,32768]{2,1,0:T(1,128)}, u32[]{:S(2)}, u32[]{:S(2)}) %all-to-all-start) | async-done | bytes 2097184 | tf_op jit(solution)/shard_map/all_to_all | solution.py:104
  50.3 8.6 %reduce = f32[16,32768]{1,0:T(8,128)} reduce(f32[16,1,32768]{2,1,0:T(1,128)} %all-to-all-done, f32[]{:T(128)} %broadcast.495), dimensions={1}, to_apply=%all_to_all.27.reduce_sub_computation | reduce | bytes 4194308 | tf_op jit(solution)/shard_map/all_to_all | solution.py:104
  58.9 6.0 reshape.309
  64.9 10.2 %copy.13 = f32[32,32,16,32]{3,1,0,2:T(8,128)} copy(f32[32,32,16,32]{1,0,3,2:T(8,128)} %bitcast.69) | data formatting | bytes 4194304 | tf_op jit(solution)/shard_map/all_to_all | solution.py:104
  75.1 8.0 %reshape.270 = f32[512,1024]{1,0:T(8,128)} reshape(f32[16,32,32,32]{3,2,1,0:T(8,128)} %bitcast.70) | data formatting | bytes 4194304 | tf_op jit(solution)/shard_map/reshape | solution.py:106
  83.1 8.9 %fusion.5 = f32[1024,1024]{1,0:T(8,128)S(1)} fusion(f32[512,1024]{1,0:T(8,128)} %reshape.270, f32[512,512]{1,0:T(8,128)S(1)} %get-tuple-element.47, f32[512,512]{1,0:T(8,128)S(1)} %get-tuple-element.48), kind=kOutput, calls=%fused_computation.24 | convolution fusion | flops 6442975232 | bytes 8388608 | tf_op jit(solution)/shard_map/dot_general | solution.py:112
  92.0 8.7 %multiply_exponential_fusion = f32[512,1024]{1,0:T(8,128)} fusion(f32[1024,1024]{1,0:T(8,128)S(1)} %fusion.5, f32[1024]{0:T(1024)S(1)} %pad_maximum_fusion.1, f32[512,512]{1,0:T(8,128)S(1)} %get-tuple-element.47, f32[512,512]{1,0:T(8,128)S(1)} %get-tuple-element.48), kind=kOutput, calls=%fused_computation.28 | convolution fusion | flops 6444548096 | bytes 8392704 | tf_op jit(solution)/shard_map/dot_general | solution.py:120
  102.7 7.6 %copy.15 = f32[512,32,32]{2,1,0:T(8,128)} copy(f32[512,32,32]{0,2,1:T(8,128)S(1)} %bitcast.71) | data formatting | bytes 4194304 | tf_op jit(solution)/shard_map/reshape | solution.py:128
  110.3 7.4 %reshape.310 = f32[16,1,32768]{2,1,0:T(1,128)S(1)} reshape(f32[512,32,32]{2,1,0:T(8,128)} %copy.15) | data formatting | bytes 4194304
  117.7 28.3 %all_to_all.38 = f32[16,1,32768]{2,1,0:T(1,128)} all-to-all(f32[16,1,32768]{2,1,0:T(1,128)S(1)} %reshape.310), channel_id=1, replica_groups=mesh['wide'=16,'mid'=8] {'wide'}, dimensions={0} | all-to-all | bytes 4194304 | tf_op jit(solution)/shard_map/all_to_all | solution.py:129
  146.0 7.3 %reduce.1 = f32[16,32768]{1,0:T(8,128)S(1)} reduce(f32[16,1,32768]{2,1,0:T(1,128)} %all_to_all.38, f32[]{:T(128)} %broadcast.495), dimensions={1}, to_apply=%all_to_all.30.reduce_sub_computation | reduce | bytes 4194308 | tf_op jit(solution)/shard_map/all_to_all | solution.py:129
  153.3 4.8 reshape.311
  158.1 6.7 fusion.42
  164.8 5.2 copy.17
  176.4 7.4 %copy.18 = f32[16,32,16,32]{3,2,1,0:T(8,128)} copy(f32[16,32,16,32]{3,1,0,2:T(8,128)} %get-tuple-element.23) | data formatting | bytes 2097152 | tf_op jit(solution)/shard_map/slice | solution.py:27
  190.9 14.2 %copy.16 = f32[32,32,16,32]{3,2,1,0:T(8,128)} copy(f32[32,32,16,32]{3,1,0,2:T(8,128)} %bitcast.67) | data formatting | bytes 4194304 | tf_op jit(solution)/shard_map/all_to_all | solution.py:129
  205.1 6.2 all_to_all.33
  218.4 7.7 %collective-permute-start.2 = (f32[64,16,512]{2,1,0:T(8,128)}, f32[64,16,512]{2,1,0:T(8,128)S(1)}, u32[]{:S(2)}, u32[]{:S(2)}) collective-permute-start(f32[64,16,512]{2,1,0:T(8,128)} %get-tuple-element.25), channel_id=1, source_target_pairs={{0,1},{1,2},{2,3},{3,4},{4,5},{5,6},{6,7},{8,9},{9,10},{10,11},{11... | collective-permute-start | bytes 6291464 | tf_op jit(solution)/shard_map/ppermute | solution.py:24
  228.7 20.7 %collective-permute-done.2 = f32[64,16,512]{2,1,0:T(8,128)S(1)} collective-permute-done((f32[64,16,512]{2,1,0:T(8,128)}, f32[64,16,512]{2,1,0:T(8,128)S(1)}, u32[]{:S(2)}, u32[]{:S(2)}) %collective-permute-start.2) | collective-permute-done | bytes 2097184 | tf_op jit(solution)/shard_map/ppermute | solution.py:24
  249.4 4.4 collective-permute-done.3
  253.8 5.9 pad_maximum_fusion
  259.8 118.5 %while.1 = (s32[]{:T(128)}, f32[64,64,512]{2,1,0:T(8,128)}, s32[16,3]{0,1:T(4,128)S(1)}, f32[16,48,48,512]{3,2,1,0:T(8,128)}, s32[]{:T(128)}) while((s32[]{:T(128)}, f32[64,64,512]{2,1,0:T(8,128)}, s32[16,3]{0,1:T(4,128)S(1)}, f32[16,48,48,512]{3,2,1,0:T(8,128)}, s32[]{:T(128)}) %tuple.39), condition=%wide.while_cond, body=%wide.while_body.sunk | while | flops 2 | bytes 9438825 | solution.py:142
  260.4 6.8 %bitcast_dynamic-update-slice_fusion.2 = f32[16,48,48,512]{3,2,1,0:T(8,128)} fusion(f32[16,48,48,512]{3,2,1,0:T(8,128)} %get-tuple-element.88, s32[]{:T(128)} %get-tuple-element.85, f32[64,64,512]{2,1,0:T(8,128)} %get-tuple-element.91, s32[]{:T(128)} %bitcast.64, s32[]{:T(128)} %bitcast.65), kind=kLoop, calls=%fused_computation.1.clone.1 | loop fusion | bytes 9438720 | tf_op jit(solution)/shard_map/vmap()/gather
  267.8 6.9 %bitcast_dynamic-update-slice_fusion.2 = f32[16,48,48,512]{3,2,1,0:T(8,128)} fusion(f32[16,48,48,512]{3,2,1,0:T(8,128)} %get-tuple-element.88, s32[]{:T(128)} %get-tuple-element.85, f32[64,64,512]{2,1,0:T(8,128)} %get-tuple-element.91, s32[]{:T(128)} %bitcast.64, s32[]{:T(128)} %bitcast.65), kind=kLoop, calls=%fused_computation.1.clone.1 | loop fusion | bytes 9438720 | tf_op jit(solution)/shard_map/vmap()/gather
  275.3 6.9 %bitcast_dynamic-update-slice_fusion.2 = f32[16,48,48,512]{3,2,1,0:T(8,128)} fusion(f32[16,48,48,512]{3,2,1,0:T(8,128)} %get-tuple-element.88, s32[]{:T(128)} %get-tuple-element.85, f32[64,64,512]{2,1,0:T(8,128)} %get-tuple-element.91, s32[]{:T(128)} %bitcast.64, s32[]{:T(128)} %bitcast.65), kind=kLoop, calls=%fused_computation.1.clone.1 | loop fusion | bytes 9438720 | tf_op jit(solution)/shard_map/vmap()/gather
  282.8 6.6 bitcast_dynamic-update-slice_fusion.2
  290.0 6.9 %bitcast_dynamic-update-slice_fusion.2 = f32[16,48,48,512]{3,2,1,0:T(8,128)} fusion(f32[16,48,48,512]{3,2,1,0:T(8,128)} %get-tuple-element.88, s32[]{:T(128)} %get-tuple-element.85, f32[64,64,512]{2,1,0:T(8,128)} %get-tuple-element.91, s32[]{:T(128)} %bitcast.64, s32[]{:T(128)} %bitcast.65), kind=kLoop, calls=%fused_computation.1.clone.1 | loop fusion | bytes 9438720 | tf_op jit(solution)/shard_map/vmap()/gather
  297.5 6.9 %bitcast_dynamic-update-slice_fusion.2 = f32[16,48,48,512]{3,2,1,0:T(8,128)} fusion(f32[16,48,48,512]{3,2,1,0:T(8,128)} %get-tuple-element.88, s32[]{:T(128)} %get-tuple-element.85, f32[64,64,512]{2,1,0:T(8,128)} %get-tuple-element.91, s32[]{:T(128)} %bitcast.64, s32[]{:T(128)} %bitcast.65), kind=kLoop, calls=%fused_computation.1.clone.1 | loop fusion | bytes 9438720 | tf_op jit(solution)/shard_map/vmap()/gather
  305.0 6.8 %bitcast_dynamic-update-slice_fusion.2 = f32[16,48,48,512]{3,2,1,0:T(8,128)} fusion(f32[16,48,48,512]{3,2,1,0:T(8,128)} %get-tuple-element.88, s32[]{:T(128)} %get-tuple-element.85, f32[64,64,512]{2,1,0:T(8,128)} %get-tuple-element.91, s32[]{:T(128)} %bitcast.64, s32[]{:T(128)} %bitcast.65), kind=kLoop, calls=%fused_computation.1.clone.1 | loop fusion | bytes 9438720 | tf_op jit(solution)/shard_map/vmap()/gather
  312.4 6.9 %bitcast_dynamic-update-slice_fusion.2 = f32[16,48,48,512]{3,2,1,0:T(8,128)} fusion(f32[16,48,48,512]{3,2,1,0:T(8,128)} %get-tuple-element.88, s32[]{:T(128)} %get-tuple-element.85, f32[64,64,512]{2,1,0:T(8,128)} %get-tuple-element.91, s32[]{:T(128)} %bitcast.64, s32[]{:T(128)} %bitcast.65), kind=kLoop, calls=%fused_computation.1.clone.1 | loop fusion | bytes 9438720 | tf_op jit(solution)/shard_map/vmap()/gather
  320.0 6.6 bitcast_dynamic-update-slice_fusion.2
  327.2 6.7 %bitcast_dynamic-update-slice_fusion.2 = f32[16,48,48,512]{3,2,1,0:T(8,128)} fusion(f32[16,48,48,512]{3,2,1,0:T(8,128)} %get-tuple-element.88, s32[]{:T(128)} %get-tuple-element.85, f32[64,64,512]{2,1,0:T(8,128)} %get-tuple-element.91, s32[]{:T(128)} %bitcast.64, s32[]{:T(128)} %bitcast.65), kind=kLoop, calls=%fused_computation.1.clone.1 | loop fusion | bytes 9438720 | tf_op jit(solution)/shard_map/vmap()/gather
  334.5 6.8 %bitcast_dynamic-update-slice_fusion.2 = f32[16,48,48,512]{3,2,1,0:T(8,128)} fusion(f32[16,48,48,512]{3,2,1,0:T(8,128)} %get-tuple-element.88, s32[]{:T(128)} %get-tuple-element.85, f32[64,64,512]{2,1,0:T(8,128)} %get-tuple-element.91, s32[]{:T(128)} %bitcast.64, s32[]{:T(128)} %bitcast.65), kind=kLoop, calls=%fused_computation.1.clone.1 | loop fusion | bytes 9438720 | tf_op jit(solution)/shard_map/vmap()/gather
  341.9 6.8 %bitcast_dynamic-update-slice_fusion.2 = f32[16,48,48,512]{3,2,1,0:T(8,128)} fusion(f32[16,48,48,512]{3,2,1,0:T(8,128)} %get-tuple-element.88, s32[]{:T(128)} %get-tuple-element.85, f32[64,64,512]{2,1,0:T(8,128)} %get-tuple-element.91, s32[]{:T(128)} %bitcast.64, s32[]{:T(128)} %bitcast.65), kind=kLoop, calls=%fused_computation.1.clone.1 | loop fusion | bytes 9438720 | tf_op jit(solution)/shard_map/vmap()/gather
  349.3 6.9 %bitcast_dynamic-update-slice_fusion.2 = f32[16,48,48,512]{3,2,1,0:T(8,128)} fusion(f32[16,48,48,512]{3,2,1,0:T(8,128)} %get-tuple-element.88, s32[]{:T(128)} %get-tuple-element.85, f32[64,64,512]{2,1,0:T(8,128)} %get-tuple-element.91, s32[]{:T(128)} %bitcast.64, s32[]{:T(128)} %bitcast.65), kind=kLoop, calls=%fused_computation.1.clone.1 | loop fusion | bytes 9438720 | tf_op jit(solution)/shard_map/vmap()/gather
  356.8 6.9 %bitcast_dynamic-update-slice_fusion.2 = f32[16,48,48,512]{3,2,1,0:T(8,128)} fusion(f32[16,48,48,512]{3,2,1,0:T(8,128)} %get-tuple-element.88, s32[]{:T(128)} %get-tuple-element.85, f32[64,64,512]{2,1,0:T(8,128)} %get-tuple-element.91, s32[]{:T(128)} %bitcast.64, s32[]{:T(128)} %bitcast.65), kind=kLoop, calls=%fused_computation.1.clone.1 | loop fusion | bytes 9438720 | tf_op jit(solution)/shard_map/vmap()/gather
  364.2 6.8 %bitcast_dynamic-update-slice_fusion.2 = f32[16,48,48,512]{3,2,1,0:T(8,128)} fusion(f32[16,48,48,512]{3,2,1,0:T(8,128)} %get-tuple-element.88, s32[]{:T(128)} %get-tuple-element.85, f32[64,64,512]{2,1,0:T(8,128)} %get-tuple-element.91, s32[]{:T(128)} %bitcast.64, s32[]{:T(128)} %bitcast.65), kind=kLoop, calls=%fused_computation.1.clone.1 | loop fusion | bytes 9438720 | tf_op jit(solution)/shard_map/vmap()/gather
  371.6 6.6 bitcast_dynamic-update-slice_fusion.2
  378.2 44.7 %fusion.15 = f32[16,48,48,48]{3,2,1,0:T(8,128)} fusion(f32[16,48,48,512]{3,2,1,0:T(8,128)} %get-tuple-element.9, pred[16,512,48,1]{1,2,3,0:T(8,128)(4,1)S(1)} %fusion.58), kind=kOutput, calls=%fused_computation.36 | convolution fusion | flops 10871635968 | bytes 82968576 | tf_op jit(solution)/shard_map/vmap(xyz,zj->xyj)/dot_general | solution.py:148
  423.0 15.7 %reshape.273 = f32[16,48,2304]{2,1,0:T(8,128)} reshape(f32[16,48,48,48]{3,2,1,0:T(8,128)} %fusion.15) | data formatting | bytes 14155776 | tf_op jit(solution)/shard_map/vmap()/reshape | solution.py:155
  438.7 9.2 %all-to-all-start.2 = ((f32[16,48,2304]{2,1,0:T(8,128)}), f32[16,48,2304]{2,1,0:T(8,128)}, u32[]{:S(2)}, u32[]{:S(2)}) async-start(f32[16,48,2304]{2,1,0:T(8,128)} %reshape.273), calls=%async_computation.2 | async-start | bytes 14155776 | tf_op jit(solution)/shard_map/all_to_all | solution.py:159
  449.1 126.9 %all-to-all-done.2 = f32[16,48,2304]{2,1,0:T(8,128)} async-done(((f32[16,48,2304]{2,1,0:T(8,128)}), f32[16,48,2304]{2,1,0:T(8,128)}, u32[]{:S(2)}, u32[]{:S(2)}) %all-to-all-start.2) | async-done | bytes 7077920 | tf_op jit(solution)/shard_map/all_to_all | solution.py:159
  582.3 5.6 fusion.40
  607.6 19.8 %multiply_reduce_fusion.2 = (f32[8]{0:T(128)}, f32[8]{0:T(128)}, f32[8,48,2304]{2,1,0:T(8,128)}) fusion(f32[8,48,2304]{2,1,0:T(8,128)S(1)} %fusion.40, f32[8,48,2303]{2,1,0:T(8,128)} %get-tuple-element.42, f32[8,48,2303]{2,1,0:T(8,128)} %get-tuple-element.41, f32[8,48,2256]{2,1,0:T(8,128)} %get-tuple-element.40, f32[8,48,2256]{2,1,0:T(8,128)} %get-tuple-element.39, ...), kind=kLoop, calls=%fused_computation.11 | loop fusion | flops 35389424 | bytes 52506696 | tf_op jit(solution)/shard_map/reduce_sum | solution.py:72
  644.2 18.6 %multiply_reduce_fusion = f32[8]{0:T(128)} fusion(f32[8,48,2304]{2,1,0:T(8,128)} %copy-done, f32[8,48,2303]{2,1,0:T(8,128)} %get-tuple-element.32, f32[8,48,2303]{2,1,0:T(8,128)} %get-tuple-element.31, f32[8,48,2256]{2,1,0:T(8,128)} %get-tuple-element.30, f32[8,48,2256]{2,1,0:T(8,128)} %get-tuple-element.29, f32[8,47,2304]{2,1,0:T(8,128)} %get-tuple-element.28, ...), kind=kLoop, calls=%fused_computation.7 | loop fusion | flops 33619960 | bytes 48967720 | tf_op jit(solution)/shard_map/reduce_sum | solution.py:72
  (101 shorter events, 88.0 us)
Async XLA Ops:
  17.6 7.0 %copy-start.8 = (f32[512]{0:T(512)S(1)}, f32[512]{0:T(512)}, u32[]{:S(2)}) copy-start(f32[512]{0:T(512)} %param.5) | copy-start | bytes 6148
  17.6 32.2 %all-to-all-start = ((f32[16,1,32768]{2,1,0:T(1,128)}), f32[16,1,32768]{2,1,0:T(1,128)}, u32[]{:S(2)}, u32[]{:S(2)}) async-start(f32[16,1,32768]{2,1,0:T(1,128)} %reshape.308), calls=%async_computation | async-start | bytes 4194304 | tf_op jit(solution)/shard_map/all_to_all | solution.py:104
  173.9 37.5 %collective-permute-start = (f32[16,32,512]{2,1,0:T(8,128)S(1)}, f32[16,32,512]{2,1,0:T(8,128)}, u32[]{:S(2)}, u32[]{:S(2)}) collective-permute-start(f32[16,32,512]{2,1,0:T(8,128)S(1)} %slice.73), channel_id=1, source_target_pairs={{0,8},{8,16},{16,24},{24,32},{32,40},{40,48},{48,56},{56,64},{64,7... | collective-permute-start | bytes 3145736 | tf_op jit(solution)/shard_map/ppermute | solution.py:24
  188.2 25.5 %collective-permute-start.1 = (f32[16,32,512]{2,1,0:T(8,128)}, f32[16,32,512]{2,1,0:T(8,128)}, u32[]{:S(2)}, u32[]{:S(2)}) collective-permute-start(f32[16,32,512]{2,1,0:T(8,128)} %slice.75), channel_id=1, source_target_pairs={{8,0},{16,8},{24,16},{32,24},{40,32},{48,40},{56,48},{64,56},{72,6... | collective-permute-start | bytes 3145736 | tf_op jit(solution)/shard_map/ppermute | solution.py:27
  211.4 3.7 copy-start.6
  215.1 3.4 copy-start.5
  215.1 13.2 %copy-start.11 = (s32[1,1,16]{2,1,0:T(1,128)S(1)}, s32[1,1,16]{2,1,0:T(1,128)}, u32[]{:S(2)}) copy-start(s32[1,1,16]{2,1,0:T(1,128)} %param.6) | copy-start | bytes 196
  218.4 31.0 %collective-permute-start.2 = (f32[64,16,512]{2,1,0:T(8,128)}, f32[64,16,512]{2,1,0:T(8,128)S(1)}, u32[]{:S(2)}, u32[]{:S(2)}) collective-permute-start(f32[64,16,512]{2,1,0:T(8,128)} %get-tuple-element.25), channel_id=1, source_target_pairs={{0,1},{1,2},{2,3},{3,4},{4,5},{5,6},{6,7},{8,9},{9,10},{10,11},{11... | collective-permute-start | bytes 6291464 | tf_op jit(solution)/shard_map/ppermute | solution.py:24
  226.1 27.7 %collective-permute-start.3 = (f32[64,16,512]{2,1,0:T(8,128)}, f32[64,16,512]{2,1,0:T(8,128)}, u32[]{:S(2)}, u32[]{:S(2)}) collective-permute-start(f32[64,16,512]{2,1,0:T(8,128)} %get-tuple-element.26), channel_id=1, source_target_pairs={{1,0},{2,1},{3,2},{4,3},{5,4},{6,5},{7,6},{9,8},{10,9},{11,10},{12... | collective-permute-start | bytes 6291464 | tf_op jit(solution)/shard_map/ppermute | solution.py:27
  438.7 9.2 %copy-start.12 = (s32[1,1,8]{2,1,0:T(1,128)S(1)}, s32[1,1,8]{2,1,0:T(1,128)}, u32[]{:S(2)}) copy-start(s32[1,1,8]{2,1,0:T(1,128)} %param.7) | copy-start | bytes 100
  438.7 137.3 %all-to-all-start.2 = ((f32[16,48,2304]{2,1,0:T(8,128)}), f32[16,48,2304]{2,1,0:T(8,128)}, u32[]{:S(2)}, u32[]{:S(2)}) async-start(f32[16,48,2304]{2,1,0:T(8,128)} %reshape.273), calls=%async_computation.2 | async-start | bytes 14155776 | tf_op jit(solution)/shard_map/all_to_all | solution.py:159
  579.9 1.8 copy-start.1
  582.3 5.6 copy-start.2
  582.3 5.6 copy-start.3
  628.1 3.4 copy-start.7
  628.1 3.4 copy-start.9
  628.1 3.4 copy-start.4
  631.0 0.6 copy-start.10
  632.1 7.9 %copy-start = (f32[8,48,2304]{2,1,0:T(8,128)}, f32[8,48,2304]{2,1,0:T(8,128)S(1)}, u32[]{:S(2)}) copy-start(f32[8,48,2304]{2,1,0:T(8,128)S(1)} %multiply_add_fusion) | copy-start | bytes 10616836
where the time goes:
time: 681 us; the launch traced here: 668 us
  local copies, waits for them, and re-layouts  291 us (43%)
  waiting for transfers between devices  173 us (25%)
  other arithmetic  80.9 us (12%)
  matrix products  62.4 us (9%)
  starting transfers between devices  31.2 us (5%)
  blocking collectives  28.3 us (4%)
    all_to_all x1, waiting for transfers between devices, on_device(): lax.all_to_all(outgoing, 'wide', split_axis=0, concat_axis=0, tiled=True)  127 us
    gather x48, local copies, waits for them, and re-layouts  118 us
    dot_general x1, matrix products, cut_block(): jnp.einsum('xyz,zj->xyj', column_block, selector, precision=lax.Precision...  44.7 us
    reduce_sum x3, other arithmetic, patch_sum(): return jnp.sum(values, axis=(1, 2), keepdims=True)  41.3 us
    unnamed x33, local copies, waits for them, and re-layouts  40.1 us
    all_to_all x1, blocking collectives, on_device(): lax.all_to_all(coeff_pencil, 'wide', split_axis=0, concat_axis=2, tiled=T...  28.3 us
    all_to_all x1, waiting for transfers between devices, on_device(): lax.all_to_all(noise, 'wide', split_axis=2, concat_axis=0, tiled=True)  21.1 us
    ppermute x2, waiting for transfers between devices, with_halo(): lax.ppermute(lax.slice_in_dim(block, block.shape[dim] - width, None, axis...  20.7 us
  transfers between devices with their start and end apart: 6, of which 4 were waited for; matrix products, arithmetic and copies ran while one was open for 5% of the time, Pallas kernels for 0%

commit v1 on v0

v1 whole, which is shorter than its diff:
```python
import math

import jax
import jax.numpy as jnp
import numpy as np
from jax import lax
from jax.experimental import pallas as pl
from jax.experimental.pallas import tpu as pltpu
from jax.sharding import PartitionSpec as P

NX = 512
NZ = 512
CY = 32
CX = 32
CORE = 16
LAYER = 16
WIDE = 16
PATCH_DEV = 8
EDGE = 48
TAPS = 3
LANES = PATCH_DEV * EDGE
SIDE = 128
TINY = 1e-06
F32 = jnp.float32
VMEM_LIMIT = 56 * 1024 * 1024


def params():
    return pltpu.CompilerParams(vmem_limit_bytes=VMEM_LIMIT)


def full(shape):
    return jax.ShapeDtypeStruct(shape, F32)


def split_kernel(in_ref, low_ref, high_ref):
    for w in range(WIDE):
        for t, out_ref in enumerate((low_ref, high_ref)):
            out_ref[w * CX:(w + 1) * CX, :] = in_ref[pl.ds(t * WIDE + w, CX, stride=CY), :]


def split_rows(block):
    return pl.pallas_call(
        split_kernel,
        grid=(NZ // SIDE,),
        in_specs=[pl.BlockSpec((CX * CY, SIDE), lambda j: (0, j))],
        out_specs=[pl.BlockSpec((NX, SIDE), lambda j: (0, j))] * 2,
        out_shape=[full((NX, NZ))] * 2,
        compiler_params=params(),
        cost_estimate=pl.CostEstimate(flops=0, bytes_accessed=8 << 20, transcendentals=0),
        name="split_rows",
    )(block.reshape(CX * CY, NZ))


def join_kernel(low_ref, high_ref, out_ref):
    for w in range(WIDE):
        for t, in_ref in enumerate((low_ref, high_ref)):
            out_ref[pl.ds(t * WIDE + w, CX, stride=CY), :] = in_ref[w * CX:(w + 1) * CX, :]


def join_rows(low, high):
    joined = pl.pallas_call(
        join_kernel,
        grid=(NZ // SIDE,),
        in_specs=[pl.BlockSpec((NX, SIDE), lambda j: (0, j))] * 2,
        out_specs=pl.BlockSpec((CX * CY, SIDE), lambda j: (0, j)),
        out_shape=full((CX * CY, NZ)),
        compiler_params=params(),
        cost_estimate=pl.CostEstimate(flops=0, bytes_accessed=8 << 20, transcendentals=0),
        name="join_rows",
    )(low, high)
    return joined.reshape(CX, CY, NZ)


def filter_kernel(matrix_ref, in_ref, out_ref):
    out_ref[...] = jnp.exp(
        jnp.dot(
            matrix_ref[...],
            in_ref[...],
            precision=lax.Precision.HIGHEST,
            preferred_element_type=F32,
        )
    )


def filter_exp(matrix, lines):
    half = NZ // 2
    return pl.pallas_call(
        filter_kernel,
        grid=(2,),
        in_specs=[
            pl.BlockSpec((NX, NX), lambda j: (0, 0)),
            pl.BlockSpec((NX, half), lambda j: (0, j)),
        ],
        out_specs=pl.BlockSpec((NX, half), lambda j: (0, j)),
        out_shape=full((NX, NZ)),
        compiler_params=params(),
        cost_estimate=pl.CostEstimate(
            flops=12 * NX * NX * NZ, bytes_accessed=3 << 20, transcendentals=NX * NZ
        ),
        name="filter_exp",
    )(matrix, lines)


def window_kernel(table_ref, p0_ref, p1_ref, p2_ref, p3_ref, out_ref, held, sems):
    owner = pl.program_id(0)

    @pl.when(owner == 0)
    def _():
        copies = [
            pltpu.make_async_copy(
                src, held.at[t, pl.ds(LAYER, NX), pl.ds(SIDE, NZ)], sems.at[t]
            )
            for t, src in enumerate((p0_ref, p1_ref, p2_ref, p3_ref))
        ]
        for copy in copies:
            copy.start()
        for t in range(4):
            held[t, 0:LAYER, :] = jnp.zeros((LAYER, NZ + 2 * SIDE), F32)
            held[t, LAYER + NX:, :] = jnp.zeros((LAYER, NZ + 2 * SIDE), F32)
            held[t, LAYER:LAYER + NX, 0:SIDE] = jnp.zeros((NX, SIDE), F32)
            held[t, LAYER:LAYER + NX, SIDE + NZ:] = jnp.zeros((NX, SIDE), F32)
        for copy in copies:
            copy.wait()

    places = []
    for p in range(PATCH_DEV):
        source = table_ref[owner, WIDE + p]
        core = jnp.maximum(table_ref[source, owner], 0)
        x_at = source * CX + (core >> 6) * CORE
        t_at = (core >> 5) & 1
        z_at = (core & 31) * CORE + (SIDE - LAYER)
        tile = pl.multiple_of((z_at >> 7) * SIDE, SIDE)
        offset = z_at & (SIDE - 1)
        turn = ((p * EDGE) % SIDE - offset) & (SIDE - 1)
        places.append((pl.multiple_of(x_at, CORE), t_at, tile, offset, turn))
    lane = lax.broadcasted_iota(jnp.int32, (EDGE, SIDE), 1)
    for t in range(TAPS):
        tiles = [None] * 3
        for p, (x_at, t_at, tile, offset, turn) in enumerate(places):
            rows = pl.ds(x_at, EDGE)
            first = held[t_at + t, rows, pl.ds(tile, SIDE)]
            second = held[t_at + t, rows, pl.ds(pl.multiple_of(tile + SIDE, SIDE), SIDE)]
            moved = pltpu.roll(jnp.where(lane >= offset, first, second), turn, 1)
            at = (p * EDGE) % SIDE
            q = (p * EDGE) // SIDE
            tiles[q] = moved if at == 0 else jnp.where(lane >= at, moved, tiles[q])
            if at + EDGE > SIDE:
                tiles[q + 1] = moved
        for q in range(3):
            out_ref[t * EDGE:(t + 1) * EDGE, q * SIDE:(q + 1) * SIDE] = tiles[q]


def windows(table, planes):
    rows = TAPS * EDGE
    return pl.pallas_call(
        window_kernel,
        grid_spec=pltpu.PrefetchScalarGridSpec(
            num_scalar_prefetch=1,
            grid=(WIDE,),
            in_specs=[pl.BlockSpec(memory_space=pl.ANY)] * 4,
            out_specs=pl.BlockSpec((None, rows, LANES), lambda d, table: (d, 0, 0)),
            scratch_shapes=[
                pltpu.VMEM((4, NX + 2 * LAYER, NZ + 2 * SIDE), F32),
                pltpu.SemaphoreType.DMA((4,)),
            ],
        ),
        out_shape=full((WIDE, rows, LANES)),
        compiler_params=params(),
        cost_estimate=pl.CostEstimate(flops=0, bytes_accessed=16 << 20, transcendentals=0),
        name="patch_windows",
    )(table, *planes)


def solve_kernel(kappa_ref, out_ref, first, image):
    row = lax.broadcasted_iota(jnp.int32, (EDGE, LANES), 0)
    lane = lax.broadcasted_iota(jnp.int32, (EDGE, LANES), 1)
    depth = lane - ((lane * 1366) >> 16) * EDGE
    x_low, x_high = row == 0, row == EDGE - 1
    z_low, z_high = depth == 0, depth == EDGE - 1
    zero = jnp.zeros((EDGE, LANES), F32)

    def above_x(v):
        return jnp.where(x_high, 0.0, pltpu.roll(v, EDGE - 1, 0))

    def above_z(v):
        return jnp.where(z_high, 0.0, pltpu.roll(v, LANES - 1, 1))

    def half_kappa(y):
        t, w = y >> 4, y & 15
        rows = pl.ds(pl.multiple_of(t * EDGE, EDGE), EDGE)
        return 0.5 * kappa_ref[w, rows, :]

    def upper(y):
        above = half_kappa(jnp.minimum(y + 1, EDGE - 1))
        return jnp.where(y + 1 < EDGE, above, 0.0)

    def rhs_of(h):
        below = jnp.where(x_low, 0.0, pltpu.roll(h, 1, 0))
        return above_x(h) - below

    def fold(v):
        return jnp.sum(v.reshape(EDGE // 8, 8, LANES), axis=0)

    seg_a = (lax.broadcasted_iota(jnp.int32, (LANES, LANES), 0) * 1366) >> 16
    seg_b = (lax.broadcasted_iota(jnp.int32, (LANES, LANES), 1) * 1366) >> 16
    same = jnp.where(seg_a == seg_b, 1.0, 0.0).astype(F32)

    def patch_total(part):
        spread = jnp.dot(part, same, precision=lax.Precision.HIGHEST, preferred_element_type=F32)
        return jnp.sum(spread, axis=0, keepdims=True)

    none = jnp.zeros((8, LANES), F32)

    def first_pass(y, carry):
        flux_low, h, v, rr, dq = carry
        h_up = upper(y)
        v_up = rhs_of(h_up)
        flux_y = (h + h_up) * (v_up - v)
        flux_x = (h + above_x(h)) * (above_x(v) - v)
        flux_z = (h + above_z(h)) * (above_z(v) - v)
        edge = h * v
        low_x = jnp.where(x_low, edge, pltpu.roll(flux_x, 1, 0))
        low_z = jnp.where(z_low, edge, pltpu.roll(flux_z, 1, 1))
        q = v - (flux_x - low_x) - (flux_y - flux_low) - (flux_z - low_z)
        first[y] = v
        image[y] = q
        return flux_y, h_up, v_up, rr + fold(v * v), dq + fold(v * q)

    h0 = half_kappa(0)
    v0 = rhs_of(h0)
    carry = lax.fori_loop(0, EDGE, first_pass, (h0 * v0, h0, v0, none, none))
    rr = patch_total(carry[3])
    alpha = rr / (patch_total(carry[4]) + TINY)

    def second_pass(y, total):
        left = first[y] - alpha * image[y]
        return total + fold(left * left)

    new = patch_total(lax.fori_loop(0, EDGE, second_pass, none))
    beta = new / (rr + TINY)

    def direction(y):
        return (first[y] - alpha * image[y]) + beta * first[y]

    def third_pass(y, carry):
        h, v, total = carry
        h_up = upper(y)
        v_up = jnp.where(y + 1 < EDGE, direction(jnp.minimum(y + 1, EDGE - 1)), 0.0)
        step_x = above_x(v) - v
        step_y = v_up - v
        step_z = above_z(v) - v
        edges = jnp.where(x_low, h, 0.0) + jnp.where(z_low, h, 0.0) + jnp.where(y == 0, h, 0.0)
        energy = (1.0 + edges) * (v * v)
        energy = energy + (h + above_x(h)) * (step_x * step_x)
        energy = energy + (h + h_up) * (step_y * step_y)
        energy = energy + (h + above_z(h)) * (step_z * step_z)
        return h_up, v_up, total + fold(energy)

    carry = lax.fori_loop(0, EDGE, third_pass, (h0, direction(0), none))
    alpha_next = new / (patch_total(carry[2]) + TINY)
    on_first = alpha + alpha_next * (1.0 + beta)
    on_image = -(alpha_next * alpha)

    chunk = (lax.broadcasted_iota(jnp.int32, (8, LANES), 1) * 1366) >> 16
    bits = [(chunk & (1 << b)) != 0 for b in range(3)]

    def last_pass(step, _):
        group, tile = step // 6, step % 6
        rows = pl.ds(pl.multiple_of(tile * 8, 8), 8)
        lines = []
        for j in range(8):
            y = group * 8 + j
            lines.append(on_first * first[y, rows, :] + on_image * image[y, rows, :])
        for b in range(3):
            hop = EDGE << b
            fresh = [None] * 8
            for j in range(8):
                if j & (1 << b):
                    continue
                k = j | (1 << b)
                fresh[j] = jnp.where(bits[b], pltpu.roll(lines[k], hop, 1), lines[j])
                fresh[k] = jnp.where(bits[b], lines[k], pltpu.roll(lines[j], LANES - hop, 1))
            lines = fresh
        columns = pl.ds(pl.multiple_of(group * LANES, LANES), LANES)
        for p in range(8):
            out_ref[p, rows, columns] = lines[p]
        return 0

    lax.fori_loop(0, 36, last_pass, 0)


def solve(kappa):
    return pl.pallas_call(
        solve_kernel,
        in_specs=[pl.BlockSpec(memory_space=pltpu.VMEM)],
        out_specs=pl.BlockSpec(memory_space=pltpu.VMEM),
        out_shape=full((PATCH_DEV, EDGE, EDGE * EDGE)),
        scratch_shapes=[pltpu.VMEM((EDGE, EDGE, LANES), F32)] * 2,
        compiler_params=params(),
        cost_estimate=pl.CostEstimate(
            flops=60 * EDGE**3 * PATCH_DEV, bytes_accessed=32 << 20, transcendentals=0
        ),
        name="solve_patches",
    )(kappa)


def wave_tables():
    index = np.arange(NX, dtype=np.int64)
    angle = (index[:, None] * index[None, :] % NX) * (2.0 * math.pi / NX)
    waves = np.concatenate([np.cos(angle), np.sin(angle)], axis=0)
    return waves.astype(np.float32)


def on_device(noise, spectrum, send_core, recv_source):
    swap = lambda v: lax.all_to_all(
        v.reshape(WIDE, v.shape[0] // WIDE, v.shape[1]), "wide", split_axis=0, concat_axis=0
    ).reshape(v.shape)
    mine = jnp.concatenate([send_core.reshape(1, WIDE), recv_source.reshape(1, PATCH_DEV)], axis=1)
    table = lax.all_gather(mine, "wide", axis=0, tiled=True)
    low, high = split_rows(noise)
    low, high = swap(low), swap(high)
    waves = jnp.asarray(wave_tables())
    weights = jnp.concatenate([spectrum, spectrum])[:, None] / NX
    matrix = lax.dot_general(
        waves,
        waves * weights,
        (((0,), (0,)), ((), ())),
        precision=lax.Precision.HIGHEST,
        preferred_element_type=F32,
    )
    count = lax.axis_size("mid")
    forward = [(i, i + 1) for i in range(count - 1)]
    backward = [(i + 1, i) for i in range(count - 1)]
    low = filter_exp(matrix, low)
    above = lax.ppermute(low, "mid", backward)
    high = filter_exp(matrix, high)
    below = lax.ppermute(high, "mid", forward)
    out_low, out_high = swap(low), swap(high)
    outgoing = windows(table, (below, low, high, above))
    incoming = lax.all_to_all(outgoing, "wide", split_axis=0, concat_axis=0)
    coefficient = join_rows(out_low, out_high)
    solved = solve(incoming)
    return coefficient, solved.reshape(1, 1, PATCH_DEV, EDGE, EDGE * EDGE)


def solution(mesh):
    in_specs = (P("wide", "mid", None), P(), P("wide", "mid", None), P("wide", "mid", None))
    out_specs = (P("wide", "mid", None), P("wide", "mid", None, None, None))
    return jax.shard_map(
        on_device, mesh=mesh, in_specs=in_specs, out_specs=out_specs, check_vma=False
    )
```

time: 681 us -> 195 us (0.29)
  the two profiles are of different devices: /device:TPU:77 before, /device:TPU:0 now
where the time goes in v1:
time: 195 us; the launch traced here: 193 us
  Pallas kernels  59.7 us (31%)
  blocking collectives  53.2 us (27%)
  waiting for transfers between devices  51.6 us (26%)
  starting transfers between devices  20.3 us (10%)
  matrix products  4.93 us (3%)
  local copies, waits for them, and re-layouts  2.76 us (1%)
    all_to_all x1, waiting for transfers between devices, on_device(): incoming = lax.all_to_all(outgoing, 'wide', split_axis=0, concat_axis=0)  37.7 us
    pallas_call x1, Pallas kernels, solve(): pl.pallas_call(solve_kernel, in_specs=[pl.BlockSpec(memory_space=pltpu.VM...  31 us
    all_gather x1, blocking collectives, on_device(): table = lax.all_gather(mine, 'wide', axis=0, tiled=True)  28.2 us
    all_to_all x1, blocking collectives, on_device(): lax.all_to_all(v.reshape(WIDE, v.shape[0] // WIDE, v.shape[1]), 'wide', s...  25 us
    all_to_all x3, waiting for transfers between devices, on_device(): lax.all_to_all(v.reshape(WIDE, v.shape[0] // WIDE, v.shape[1]), 'wide', s...  14 us
    all_to_all x3, starting transfers between devices, on_device(): lax.all_to_all(v.reshape(WIDE, v.shape[0] // WIDE, v.shape[1]), 'wide', s...  11.2 us
    pallas_call x1, Pallas kernels, windows(): pl.pallas_call(window_kernel, grid_spec=pltpu.PrefetchScalarGridSpec(num_...  10.8 us
    pallas_call x2, Pallas kernels, filter_exp(): pl.pallas_call(filter_kernel, grid=(2,), in_specs=[pl.BlockSpec((NX, NX),...  8.97 us
  transfers between devices with their start and end apart: 6, of which 3 were waited for; matrix products, arithmetic and copies ran while one was open for 3% of the time, Pallas kernels for 13%

profile of v1, /device:TPU:0, one launch (start us, length us, event | category | flops | bytes accessed | tf_op | source)
XLA Modules:
  0.0 193.4 jit_solution(1542991901876306217)
XLA Ops:
  0.6 4.3 %split_rows.1 = (f32[512,512]{1,0:T(8,128)}, f32[512,512]{1,0:T(8,128)}) custom-call(f32[1024,512]{1,0:T(8,128)} %bitcast.22), custom_call_target="tpu_custom_call" | custom-call | bytes 8388608 | tf_op jit(solution)/shard_map/split_rows/pallas_call | solution.py:43
  4.9 0.0 copy-start.6
  4.9 0.0 copy-start.1
  4.9 25.0 %all_to_all.25 = f32[16,32,512]{2,1,0:T(8,128)} all-to-all(f32[16,32,512]{2,1,0:T(8,128)} %bitcast.27), channel_id=1, replica_groups=mesh['wide'=16,'mid'=8] {'wide'}, dimensions={0} | all-to-all | bytes 2097152 | tf_op jit(solution)/shard_map/all_to_all | solution.py:316
  30.0 3.8 %all-to-all-start.2 = ((f32[16,32,512]{2,1,0:T(8,128)}), f32[16,32,512]{2,1,0:T(8,128)S(1)}, u32[]{:S(2)}, u32[]{:S(2)}) async-start(f32[16,32,512]{2,1,0:T(8,128)} %bitcast.25), calls=%async_computation.2 | async-start | bytes 2097152 | tf_op jit(solution)/shard_map/all_to_all | solution.py:316
  33.8 0.0 copy-done.6
  33.9 0.0 copy-done.1
  33.9 4.9 %fusion.matrix_ref = f32[512,512]{1,0:T(8,128)} fusion(f32[1024,512]{1,0:T(8,128)S(1)} %copy-done.1, f32[1024]{0:T(1024)S(1)} %maximum_multiply_fusion), kind=kOutput, calls=%fused_computation | convolution fusion | flops 3221749760 | bytes 3149824 | tf_op jit(solution)/shard_map/dot_general | solution.py:325
  38.8 4.4 %filter_exp.2.p1_ref = f32[512,512]{1,0:T(8,128)} custom-call(f32[512,512]{1,0:T(8,128)} %fusion.matrix_ref, f32[512,512]{1,0:T(8,128)} %bitcast.26), custom_call_target="tpu_custom_call" | custom-call | flops 1610612736 | bytes 3145728 | tf_op jit(solution)/shard_map/filter_exp/pallas_call | solution.py:88
  43.2 6.5 %all-to-all-done.2 = f32[16,32,512]{2,1,0:T(8,128)S(1)} async-done(((f32[16,32,512]{2,1,0:T(8,128)}), f32[16,32,512]{2,1,0:T(8,128)S(1)}, u32[]{:S(2)}, u32[]{:S(2)}) %all-to-all-start.2) | async-done | bytes 1048608 | tf_op jit(solution)/shard_map/all_to_all | solution.py:316
  49.8 0.0 copy-start.5
  49.8 3.7 %all-to-all-start.1 = ((f32[16,32,512]{2,1,0:T(8,128)}), f32[16,32,512]{2,1,0:T(8,128)S(1)}, u32[]{:S(2)}, u32[]{:S(2)}) async-start(f32[16,32,512]{2,1,0:T(8,128)} %bitcast.18), calls=%async_computation.1 | async-start | bytes 2097152 | tf_op jit(solution)/shard_map/all_to_all | solution.py:316
  53.4 0.0 copy-done.5
  53.4 0.0 copy-start.3
  53.4 4.5 %filter_exp.3.p2_ref = f32[512,512]{1,0:T(8,128)} custom-call(f32[512,512]{1,0:T(8,128)} %fusion.matrix_ref, f32[512,512]{1,0:T(8,128)} %bitcast.24), custom_call_target="tpu_custom_call" | custom-call | flops 1610612736 | bytes 3145728 | tf_op jit(solution)/shard_map/filter_exp/pallas_call | solution.py:88
  58.0 0.0 copy-start.7
  58.0 0.0 copy-start.8
  58.0 2.4 %collective-permute-start = (f32[512,512]{1,0:T(8,128)}, f32[512,512]{1,0:T(8,128)}, u32[]{:S(2)}, u32[]{:S(2)}) collective-permute-start(f32[512,512]{1,0:T(8,128)} %filter_exp.3.p2_ref), channel_id=1, source_target_pairs={{0,1},{1,2},{2,3},{3,4},{4,5},{5,6},{6,7},{8,9},{9,10},{10,11},{11... | collective-permute-start | bytes 3145736 | tf_op jit(solution)/shard_map/ppermute | solution.py:338
  60.4 0.0 copy-done.3
  60.4 1.3 collective-permute-start.1
  61.7 7.4 %all-to-all-done.1 = f32[16,32,512]{2,1,0:T(8,128)S(1)} async-done(((f32[16,32,512]{2,1,0:T(8,128)}), f32[16,32,512]{2,1,0:T(8,128)S(1)}, u32[]{:S(2)}, u32[]{:S(2)}) %all-to-all-start.1) | async-done | bytes 1048608 | tf_op jit(solution)/shard_map/all_to_all | solution.py:316
  69.1 0.0 copy-start.2
  69.1 3.7 %all-to-all-start.3 = ((f32[16,32,512]{2,1,0:T(8,128)}), f32[16,32,512]{2,1,0:T(8,128)S(1)}, u32[]{:S(2)}, u32[]{:S(2)}) async-start(f32[16,32,512]{2,1,0:T(8,128)} %bitcast.19), calls=%async_computation.3 | async-start | bytes 2097152 | tf_op jit(solution)/shard_map/all_to_all | solution.py:316
  72.8 0.0 copy-done.7
  72.8 0.0 copy-done.8
  72.8 0.1 add_bitcast_fusion
  72.9 28.2 %all-gather = s32[16,1,24]{2,1,0:T(1,128)} all-gather(s32[1,1,24]{2,1,0:T(1,128)S(1)} %add_bitcast_fusion), channel_id=1, replica_groups=mesh['wide'=16,'mid'=8] {'wide'}, dimensions={0}, use_global_device_ids=true | all-gather | bytes 1632 | tf_op jit(solution)/shard_map/all_gather | solution.py:320
  101.1 0.0 collective-permute-done.p0_ref
  101.1 0.0 collective-permute-done.1.p3_ref
  101.1 10.8 %patch_windows.1 = f32[16,144,384]{2,1,0:T(8,128)} custom-call(s32[16,24]{1,0:T(8,128)} %bitcast.28, f32[512,512]{1,0:T(8,128)} %collective-permute-done.p0_ref, f32[512,512]{1,0:T(8,128)} %filter_exp.2.p1_ref, f32[512,512]{1,0:T(8,128)} %filter_exp.3.p2_ref, f32[512,512]{1,0:T(8,128)} %collective-permute-done.1.p3_ref), custom_call_target="tpu_custom_call" | custom-call | bytes 16777216 | tf_op jit(solution)/shard_map/patch_windows/pallas_call | solution.py:156
  111.9 0.0 copy-done.2
  111.9 0.0 all-to-all-done.3
  111.9 0.0 copy-start.4
  111.9 1.0 copy-done.4
  112.9 5.4 %all-to-all-start.4 = ((f32[16,144,384]{2,1,0:T(8,128)}), f32[16,144,384]{2,1,0:T(8,128)S(1)}, u32[]{:S(2)}, u32[]{:S(2)}) async-start(f32[16,144,384]{2,1,0:T(8,128)} %patch_windows.1), calls=%async_computation.4 | async-start | bytes 7077888 | tf_op jit(solution)/shard_map/all_to_all | solution.py:341
  118.3 4.7 %join_rows.1 = f32[1024,512]{1,0:T(8,128)} custom-call(f32[512,512]{1,0:T(8,128)} %bitcast.17, f32[512,512]{1,0:T(8,128)} %bitcast.20), custom_call_target="tpu_custom_call" | custom-call | bytes 8388608 | tf_op jit(solution)/shard_map/join_rows/pallas_call | solution.py:62
  123.0 37.7 %all-to-all-done.4.kappa_ref = f32[16,144,384]{2,1,0:T(8,128)S(1)} async-done(((f32[16,144,384]{2,1,0:T(8,128)}), f32[16,144,384]{2,1,0:T(8,128)S(1)}, u32[]{:S(2)}, u32[]{:S(2)}) %all-to-all-start.4) | async-done | bytes 3538976 | tf_op jit(solution)/shard_map/all_to_all | solution.py:341
  160.7 0.0 copy-start
  160.7 1.8 copy-done
  162.4 31.0 %solve_patches.1 = f32[8,48,2304]{2,1,0:T(8,128)} custom-call(f32[16,144,384]{2,1,0:T(8,128)} %copy-done), custom_call_target="tpu_custom_call" | custom-call | flops 53084160 | bytes 33554432 | tf_op jit(solution)/shard_map/solve_patches/pallas_call | solution.py:294
  (1 shorter events, 0.0 us)
Async XLA Ops:
  4.9 28.9 %copy-start.6 = (f32[512]{0:T(512)S(1)}, f32[512]{0:T(512)}, u32[]{:S(2)}) copy-start(f32[512]{0:T(512)} %param.6) | copy-start | bytes 6148
  4.9 28.9 %copy-start.1 = (f32[1024,512]{1,0:T(8,128)S(1)}, f32[1024,512]{1,0:T(8,128)}, u32[]{:S(2)}) copy-start(f32[1024,512]{1,0:T(8,128)} %constant.5.clone) | copy-start | bytes 6291460
  30.0 19.8 %all-to-all-start.2 = ((f32[16,32,512]{2,1,0:T(8,128)}), f32[16,32,512]{2,1,0:T(8,128)S(1)}, u32[]{:S(2)}, u32[]{:S(2)}) async-start(f32[16,32,512]{2,1,0:T(8,128)} %bitcast.25), calls=%async_computation.2 | async-start | bytes 2097152 | tf_op jit(solution)/shard_map/all_to_all | solution.py:316
  49.8 3.7 %copy-start.5 = (f32[16,32,512]{2,1,0:T(8,128)}, f32[16,32,512]{2,1,0:T(8,128)S(1)}, u32[]{:S(2)}) copy-start(f32[16,32,512]{2,1,0:T(8,128)S(1)} %all-to-all-done.2) | copy-start | bytes 3145732
  49.8 19.4 %all-to-all-start.1 = ((f32[16,32,512]{2,1,0:T(8,128)}), f32[16,32,512]{2,1,0:T(8,128)S(1)}, u32[]{:S(2)}, u32[]{:S(2)}) async-start(f32[16,32,512]{2,1,0:T(8,128)} %bitcast.18), calls=%async_computation.1 | async-start | bytes 2097152 | tf_op jit(solution)/shard_map/all_to_all | solution.py:316
  53.4 7.0 %copy-start.3 = (f32[512,512]{1,0:T(8,128)S(1)}, f32[512,512]{1,0:T(8,128)}, u32[]{:S(2)}) copy-start(f32[512,512]{1,0:T(8,128)} %filter_exp.2.p1_ref) | copy-start | bytes 3145732
  58.0 14.8 %copy-start.7 = (s32[1,1,8]{2,1,0:T(1,128)S(1)}, s32[1,1,8]{2,1,0:T(1,128)}, u32[]{:S(2)}) copy-start(s32[1,1,8]{2,1,0:T(1,128)} %param.8) | copy-start | bytes 100
  58.0 14.8 %copy-start.8 = (s32[1,1,16]{2,1,0:T(1,128)S(1)}, s32[1,1,16]{2,1,0:T(1,128)}, u32[]{:S(2)}) copy-start(s32[1,1,16]{2,1,0:T(1,128)} %param.7) | copy-start | bytes 196
  58.0 43.1 %collective-permute-start = (f32[512,512]{1,0:T(8,128)}, f32[512,512]{1,0:T(8,128)}, u32[]{:S(2)}, u32[]{:S(2)}) collective-permute-start(f32[512,512]{1,0:T(8,128)} %filter_exp.3.p2_ref), channel_id=1, source_target_pairs={{0,1},{1,2},{2,3},{3,4},{4,5},{5,6},{6,7},{8,9},{9,10},{10,11},{11... | collective-permute-start | bytes 3145736 | tf_op jit(solution)/shard_map/ppermute | solution.py:338
  60.4 40.7 %collective-permute-start.1 = (f32[512,512]{1,0:T(8,128)S(1)}, f32[512,512]{1,0:T(8,128)}, u32[]{:S(2)}, u32[]{:S(2)}) collective-permute-start(f32[512,512]{1,0:T(8,128)S(1)} %copy-done.3), channel_id=1, source_target_pairs={{1,0},{2,1},{3,2},{4,3},{5,4},{6,5},{7,6},{9,8},{10,9},{11,10},{12... | collective-permute-start | bytes 3145736 | tf_op jit(solution)/shard_map/ppermute | solution.py:336
  69.1 42.7 %copy-start.2 = (f32[16,32,512]{2,1,0:T(8,128)}, f32[16,32,512]{2,1,0:T(8,128)S(1)}, u32[]{:S(2)}) copy-start(f32[16,32,512]{2,1,0:T(8,128)S(1)} %all-to-all-done.1) | copy-start | bytes 3145732
  69.1 42.7 %all-to-all-start.3 = ((f32[16,32,512]{2,1,0:T(8,128)}), f32[16,32,512]{2,1,0:T(8,128)S(1)}, u32[]{:S(2)}, u32[]{:S(2)}) async-start(f32[16,32,512]{2,1,0:T(8,128)} %bitcast.19), calls=%async_computation.3 | async-start | bytes 2097152 | tf_op jit(solution)/shard_map/all_to_all | solution.py:316
  111.9 1.0 copy-start.4
  112.9 47.8 %all-to-all-start.4 = ((f32[16,144,384]{2,1,0:T(8,128)}), f32[16,144,384]{2,1,0:T(8,128)S(1)}, u32[]{:S(2)}, u32[]{:S(2)}) async-start(f32[16,144,384]{2,1,0:T(8,128)} %patch_windows.1), calls=%async_computation.4 | async-start | bytes 7077888 | tf_op jit(solution)/shard_map/all_to_all | solution.py:341
  160.7 1.8 copy-start

commit v2 on v1

--- a/solution.py
+++ b/solution.py
@@ -20,6 +20,8 @@
 TAPS = 3
 LANES = PATCH_DEV * EDGE
 SIDE = 128
+TILES = NZ // SIDE
+ROWS = 2 * TILES * CX
 TINY = 1e-06
 F32 = jnp.float32
 VMEM_LIMIT = 56 * 1024 * 1024
@@ -33,70 +35,96 @@
     return jax.ShapeDtypeStruct(shape, F32)
 
 
-def split_kernel(in_ref, low_ref, high_ref):
+def part_rows(t):
+    return pl.ds(pl.multiple_of((t * TILES + pl.program_id(0)) * CX, CX), CX)
+
+
+def split_kernel(in_ref, table_ref, out_ref):
     for w in range(WIDE):
-        for t, out_ref in enumerate((low_ref, high_ref)):
-            out_ref[w * CX:(w + 1) * CX, :] = in_ref[pl.ds(t * WIDE + w, CX, stride=CY), :]
-
-
-def split_rows(block):
+        for t in range(2):
+            out_ref[w, part_rows(t), :] = in_ref[pl.ds(t * WIDE + w, CX, stride=CY), :]
+        out_ref[w, ROWS:, :] = table_ref[...]
+
+
+def split_rows(block, table):
     return pl.pallas_call(
         split_kernel,
-        grid=(NZ // SIDE,),
-        in_specs=[pl.BlockSpec((CX * CY, SIDE), lambda j: (0, j))],
-        out_specs=[pl.BlockSpec((NX, SIDE), lambda j: (0, j))] * 2,
-        out_shape=[full((NX, NZ))] * 2,
+        grid=(TILES,),
+        in_specs=[
+            pl.BlockSpec((CX * CY, SIDE), lambda j: (0, j)),
+            pl.BlockSpec((8, SIDE), lambda j: (0, 0)),
+        ],
+        out_specs=pl.BlockSpec((WIDE, ROWS + 8, SIDE), lambda j: (0, 0, 0)),
+        out_shape=full((WIDE, ROWS + 8, SIDE)),
         compiler_params=params(),
         cost_estimate=pl.CostEstimate(flops=0, bytes_accessed=8 << 20, transcendentals=0),
         name="split_rows",
-    )(block.reshape(CX * CY, NZ))
-
-
-def join_kernel(low_ref, high_ref, out_ref):
+    )(block.reshape(CX * CY, NZ), table)
+
+
+def join_kernel(in_ref, out_ref):
     for w in range(WIDE):
-        for t, in_ref in enumerate((low_ref, high_ref)):
-            out_ref[pl.ds(t * WIDE + w, CX, stride=CY), :] = in_ref[w * CX:(w + 1) * CX, :]
-
-
-def join_rows(low, high):
+        for t in range(2):
+            out_ref[pl.ds(t * WIDE + w, CX, stride=CY), :] = in_ref[w, part_rows(t), :]
+
+
+def join_rows(parts):
     joined = pl.pallas_call(
         join_kernel,
-        grid=(NZ // SIDE,),
-        in_specs=[pl.BlockSpec((NX, SIDE), lambda j: (0, j))] * 2,
+        grid=(TILES,),
+        in_specs=[pl.BlockSpec((WIDE, ROWS, SIDE), lambda j: (0, 0, 0))],
         out_specs=pl.BlockSpec((CX * CY, SIDE), lambda j: (0, j)),
         out_shape=full((CX * CY, NZ)),
         compiler_params=params(),
         cost_estimate=pl.CostEstimate(flops=0, bytes_accessed=8 << 20, transcendentals=0),
         name="join_rows",
-    )(low, high)
+    )(parts)
     return joined.reshape(CX, CY, NZ)
 
 
-def filter_kernel(matrix_ref, in_ref, out_ref):
-    out_ref[...] = jnp.exp(
+def filter_kernel(matrix_ref, in_ref, parts_ref, low_ref, high_ref):
+    step = pl.program_id(0)
+    lines = jnp.concatenate(
+        [in_ref[:, 0:CX, :].reshape(NX, SIDE), in_ref[:, CX:, :].reshape(NX, SIDE)], axis=1
+    )
+    value = jnp.exp(
         jnp.dot(
             matrix_ref[...],
-            in_ref[...],
+            lines,
             precision=lax.Precision.HIGHEST,
             preferred_element_type=F32,
         )
     )
+    left, right = value[:, :SIDE], value[:, SIDE:]
+    parts_ref[:, 0:CX, :] = left.reshape(WIDE, CX, SIDE)
+    parts_ref[:, CX:, :] = right.reshape(WIDE, CX, SIDE)
+
+    @pl.when(step < 2)
+    def _():
+        low_ref[0] = left
+        low_ref[1] = right
+
+    @pl.when(step >= 2)
+    def _():
+        high_ref[0] = left
+        high_ref[1] = right
 
 
 def filter_exp(matrix, lines):
-    half = NZ // 2
+    block = pl.BlockSpec((WIDE, 2 * CX, SIDE), lambda i: (0, i, 0))
     return pl.pallas_call(
         filter_kernel,
-        grid=(2,),
-        in_specs=[
-            pl.BlockSpec((NX, NX), lambda j: (0, 0)),
-            pl.BlockSpec((NX, half), lambda j: (0, j)),
+        grid=(4,),
+        in_specs=[pl.BlockSpec((NX, NX), lambda i: (0, 0)), block],
+        out_specs=[
+            block,
+            pl.BlockSpec((2, NX, SIDE), lambda i: (jnp.minimum(i, 1), 0, 0)),
+            pl.BlockSpec((2, NX, SIDE), lambda i: (jnp.maximum(i - 2, 0), 0, 0)),
         ],
-        out_specs=pl.BlockSpec((NX, half), lambda j: (0, j)),
-        out_shape=full((NX, NZ)),
+        out_shape=[full((WIDE, ROWS, SIDE)), full((TILES, NX, SIDE)), full((TILES, NX, SIDE))],
         compiler_params=params(),
         cost_estimate=pl.CostEstimate(
-            flops=12 * NX * NX * NZ, bytes_accessed=3 << 20, transcendentals=NX * NZ
+            flops=24 * NX * NX * NZ, bytes_accessed=7 << 20, transcendentals=2 * NX * NZ
         ),
         name="filter_exp",
     )(matrix, lines)
@@ -109,17 +137,19 @@
     def _():
         copies = [
             pltpu.make_async_copy(
-                src, held.at[t, pl.ds(LAYER, NX), pl.ds(SIDE, NZ)], sems.at[t]
+                src, held.at[t, pl.ds(1, TILES), pl.ds(LAYER, NX), :], sems.at[t]
             )
             for t, src in enumerate((p0_ref, p1_ref, p2_ref, p3_ref))
         ]
         for copy in copies:
             copy.start()
+        side = jnp.zeros((NX + 2 * LAYER, SIDE), F32)
         for t in range(4):
-            held[t, 0:LAYER, :] = jnp.zeros((LAYER, NZ + 2 * SIDE), F32)
-            held[t, LAYER + NX:, :] = jnp.zeros((LAYER, NZ + 2 * SIDE), F32)
-            held[t, LAYER:LAYER + NX, 0:SIDE] = jnp.zeros((NX, SIDE), F32)
-            held[t, LAYER:LAYER + NX, SIDE + NZ:] = jnp.zeros((NX, SIDE), F32)
+            held[t, 0] = side
+            held[t, TILES + 1] = side
+            for j in range(TILES):
+                held[t, 1 + j, 0:LAYER, :] = side[:LAYER]
+                held[t, 1 + j, LAYER + NX:, :] = side[:LAYER]
         for copy in copies:
             copy.wait()
 
@@ -130,7 +160,7 @@
         x_at = source * CX + (core >> 6) * CORE
         t_at = (core >> 5) & 1
         z_at = (core & 31) * CORE + (SIDE - LAYER)
-        tile = pl.multiple_of((z_at >> 7) * SIDE, SIDE)
+        tile = z_at >> 7
         offset = z_at & (SIDE - 1)
         turn = ((p * EDGE) % SIDE - offset) & (SIDE - 1)
         places.append((pl.multiple_of(x_at, CORE), t_at, tile, offset, turn))
@@ -139,8 +169,8 @@
         tiles = [None] * 3
         for p, (x_at, t_at, tile, offset, turn) in enumerate(places):
             rows = pl.ds(x_at, EDGE)
-            first = held[t_at + t, rows, pl.ds(tile, SIDE)]
-            second = held[t_at + t, rows, pl.ds(pl.multiple_of(tile + SIDE, SIDE), SIDE)]
+            first = held[t_at + t, tile, rows, :]
+            second = held[t_at + t, tile + 1, rows, :]
             moved = pltpu.roll(jnp.where(lane >= offset, first, second), turn, 1)
             at = (p * EDGE) % SIDE
             q = (p * EDGE) // SIDE
@@ -161,7 +191,7 @@
             in_specs=[pl.BlockSpec(memory_space=pl.ANY)] * 4,
             out_specs=pl.BlockSpec((None, rows, LANES), lambda d, table: (d, 0, 0)),
             scratch_shapes=[
-                pltpu.VMEM((4, NX + 2 * LAYER, NZ + 2 * SIDE), F32),
+                pltpu.VMEM((4, TILES + 2, NX + 2 * LAYER, SIDE), F32),
                 pltpu.SemaphoreType.DMA((4,)),
             ],
         ),
@@ -313,13 +343,11 @@
 
 
 def on_device(noise, spectrum, send_core, recv_source):
-    swap = lambda v: lax.all_to_all(
-        v.reshape(WIDE, v.shape[0] // WIDE, v.shape[1]), "wide", split_axis=0, concat_axis=0
-    ).reshape(v.shape)
+    swap = lambda v: lax.all_to_all(v, "wide", split_axis=0, concat_axis=0)
     mine = jnp.concatenate([send_core.reshape(1, WIDE), recv_source.reshape(1, PATCH_DEV)], axis=1)
-    table = lax.all_gather(mine, "wide", axis=0, tiled=True)
-    low, high = split_rows(noise)
-    low, high = swap(low), swap(high)
+    mine = jnp.pad(mine.astype(F32), ((0, 7), (0, SIDE - mine.shape[1])))
+    lines = swap(split_rows(noise, mine))
+    table = lines[:, ROWS, :WIDE + PATCH_DEV].astype(jnp.int32)
     waves = jnp.asarray(wave_tables())
     weights = jnp.concatenate([spectrum, spectrum])[:, None] / NX
     matrix = lax.dot_general(
@@ -332,14 +360,12 @@
     count = lax.axis_size("mid")
     forward = [(i, i + 1) for i in range(count - 1)]
     backward = [(i + 1, i) for i in range(count - 1)]
-    low = filter_exp(matrix, low)
+    parts, low, high = filter_exp(matrix, lines)
     above = lax.ppermute(low, "mid", backward)
-    high = filter_exp(matrix, high)
     below = lax.ppermute(high, "mid", forward)
-    out_low, out_high = swap(low), swap(high)
+    coefficient = join_rows(swap(parts))
     outgoing = windows(table, (below, low, high, above))
-    incoming = lax.all_to_all(outgoing, "wide", split_axis=0, concat_axis=0)
-    coefficient = join_rows(out_low, out_high)
+    incoming = swap(outgoing)
     solved = solve(incoming)
     return coefficient, solved.reshape(1, 1, PATCH_DEV, EDGE, EDGE * EDGE)
 

time: 195 us -> 181 us (0.928)
  the two profiles are of different devices: /device:TPU:0 before, /device:TPU:77 now
where the time goes in v2:
time: 181 us
  waiting for transfers between devices  81.3 us (45%)
  Pallas kernels  58 us (32%)
  starting transfers between devices  29 us (16%)
  local copies, waits for them, and re-layouts  5.52 us (3%)
  matrix products  4.92 us (3%)
    all_to_all x3, waiting for transfers between devices, on_device(): swap = lambda v: lax.all_to_all(v, 'wide', split_axis=0, concat_axis=0)  68.3 us
    pallas_call x1, Pallas kernels, solve(): pl.pallas_call(solve_kernel, in_specs=[pl.BlockSpec(memory_space=pltpu.VM...  31 us
    all_to_all x3, starting transfers between devices, on_device(): swap = lambda v: lax.all_to_all(v, 'wide', split_axis=0, concat_axis=0)  20.4 us
    pallas_call x1, Pallas kernels, windows(): pl.pallas_call(window_kernel, grid_spec=pltpu.PrefetchScalarGridSpec(num_...  10.6 us
    ppermute x1, waiting for transfers between devices, on_device(): below = lax.ppermute(high, 'mid', forward)  8.65 us
    pallas_call x1, Pallas kernels, filter_exp(): pl.pallas_call(filter_kernel, grid=(4,), in_specs=[pl.BlockSpec((NX, NX),...  7.39 us
    ppermute x1, starting transfers between devices, on_device(): below = lax.ppermute(high, 'mid', forward)  6.66 us
    dot_general x1, matrix products, on_device(): lax.dot_general(waves, waves * weights, (((0,), (0,)), ((), ())), precisi...  4.92 us
  transfers between devices with their start and end apart: 5, of which 4 were waited for; matrix products, arithmetic and copies ran while one was open for 4% of the time, Pallas kernels for 8%

profile of v2, /device:TPU:77, one launch (start us, length us, event | category | flops | bytes accessed | tf_op | source)
XLA Modules:
  0.0 180.9 jit_solution(14141067328011733758)
XLA Ops:
  0.6 0.7 add_convert_fusion
  1.4 0.6 pad.4.table_ref
  2.0 4.4 %split_rows.1 = f32[16,264,128]{2,1,0:T(8,128)} custom-call(f32[1024,512]{1,0:T(8,128)} %bitcast.10, f32[8,128]{1,0:T(8,128)} %pad.4.table_ref), custom_call_target="tpu_custom_call" | custom-call | bytes 8388608 | tf_op jit(solution)/shard_map/split_rows/pallas_call | solution.py:50
  6.4 0.0 copy-start.6
  6.4 0.0 copy-start.2
  6.4 7.0 %all-to-all-start = ((f32[16,264,128]{2,1,0:T(8,128)}), f32[16,264,128]{2,1,0:T(8,128)}, u32[]{:S(2)}, u32[]{:S(2)}) async-start(f32[16,264,128]{2,1,0:T(8,128)} %split_rows.1), calls=%async_computation | async-start | bytes 4325376 | tf_op jit(solution)/shard_map/all_to_all | solution.py:346
  13.4 0.0 copy-done.6
  13.4 0.0 copy-done.2
  13.4 4.9 %fusion.matrix_ref = f32[512,512]{1,0:T(8,128)} fusion(f32[1024,512]{1,0:T(8,128)S(1)} %copy-done.2, f32[1024]{0:T(1024)S(1)} %maximum_multiply_fusion), kind=kOutput, calls=%fused_computation | convolution fusion | flops 3221749760 | bytes 3149824 | tf_op jit(solution)/shard_map/dot_general | solution.py:353
  18.3 21.0 %all-to-all-done.in_ref = f32[16,264,128]{2,1,0:T(8,128)} async-done(((f32[16,264,128]{2,1,0:T(8,128)}), f32[16,264,128]{2,1,0:T(8,128)}, u32[]{:S(2)}, u32[]{:S(2)}) %all-to-all-start) | async-done | bytes 2162720 | tf_op jit(solution)/shard_map/all_to_all | solution.py:346
  39.3 7.4 %filter_exp.1 = (f32[16,256,128]{2,1,0:T(8,128)}, f32[4,512,128]{2,1,0:T(8,128)}, f32[4,512,128]{2,1,0:T(8,128)}) custom-call(f32[512,512]{1,0:T(8,128)} %fusion.matrix_ref, f32[16,264,128]{2,1,0:T(8,128)} %all-to-all-done.in_ref), custom_call_target="tpu_custom_call" | custom-call | flops 3221225472 | bytes 7340032 | tf_op jit(solution)/shard_map/filter_exp/pallas_call | solution.py:115
  46.7 0.0 copy-start.3
  46.7 6.8 %all-to-all-start.1 = ((f32[16,256,128]{2,1,0:T(8,128)}), f32[16,256,128]{2,1,0:T(8,128)S(1)}, u32[]{:S(2)}, u32[]{:S(2)}) async-start(f32[16,256,128]{2,1,0:T(8,128)} %get-tuple-element.5), calls=%async_computation.1 | async-start | bytes 4194304 | tf_op jit(solution)/shard_map/all_to_all | solution.py:346
  53.5 6.7 %collective-permute-start = (f32[4,512,128]{2,1,0:T(8,128)}, f32[4,512,128]{2,1,0:T(8,128)S(1)}, u32[]{:S(2)}, u32[]{:S(2)}) collective-permute-start(f32[4,512,128]{2,1,0:T(8,128)} %get-tuple-element.6.p2_ref), channel_id=1, source_target_pairs={{0,1},{1,2},{2,3},{3,4},{4,5},{5,6},{6,7},{8,9},{9,10},{10,11},{11... | collective-permute-start | bytes 3145736 | tf_op jit(solution)/shard_map/ppermute | solution.py:365
  60.2 0.0 copy-done.3
  60.2 1.9 %collective-permute-start.1 = (f32[4,512,128]{2,1,0:T(8,128)S(1)}, f32[4,512,128]{2,1,0:T(8,128)S(1)}, u32[]{:S(2)}, u32[]{:S(2)}) collective-permute-start(f32[4,512,128]{2,1,0:T(8,128)S(1)} %copy-done.3), channel_id=1, source_target_pairs={{1,0},{2,1},{3,2},{4,3},{5,4},{6,5},{7,6},{9,8},{10,9},{11,10},{12... | collective-permute-start | bytes 3145736 | tf_op jit(solution)/shard_map/ppermute | solution.py:364
  62.1 0.8 slice.4
  63.0 0.6 convert_bitcast_fusion.table_ref
  63.6 8.7 %collective-permute-done.p0_ref = f32[4,512,128]{2,1,0:T(8,128)S(1)} collective-permute-done((f32[4,512,128]{2,1,0:T(8,128)}, f32[4,512,128]{2,1,0:T(8,128)S(1)}, u32[]{:S(2)}, u32[]{:S(2)}) %collective-permute-start) | collective-permute-done | bytes 1048608 | tf_op jit(solution)/shard_map/ppermute | solution.py:365
  72.2 0.0 copy-start.4
  72.2 4.4 %collective-permute-done.1.p3_ref = f32[4,512,128]{2,1,0:T(8,128)S(1)} collective-permute-done((f32[4,512,128]{2,1,0:T(8,128)S(1)}, f32[4,512,128]{2,1,0:T(8,128)S(1)}, u32[]{:S(2)}, u32[]{:S(2)}) %collective-permute-start.1) | collective-permute-done | bytes 1048608 | tf_op jit(solution)/shard_map/ppermute | solution.py:364
  76.6 0.0 copy-done.4
  76.6 0.0 copy-start.5
  76.6 1.0 copy-done.5
  77.6 10.6 %patch_windows.1 = f32[16,144,384]{2,1,0:T(8,128)} custom-call(s32[16,24]{1,0:T(8,128)} %convert_bitcast_fusion.table_ref, f32[4,512,128]{2,1,0:T(8,128)} %copy-done.4, f32[4,512,128]{2,1,0:T(8,128)} %get-tuple-element.7.p1_ref, f32[4,512,128]{2,1,0:T(8,128)} %get-tuple-element.6.p2_ref, f32[4,512,128]{2,1,0:T(8,128)} %copy-done.5), custom_call_target="tpu_custom_call" | custom-call | bytes 16777216 | tf_op jit(solution)/shard_map/patch_windows/pallas_call | solution.py:186
  88.2 0.0 all-to-all-done.1.in_ref
  88.2 0.0 copy-start.1
  88.2 1.3 copy-done.1
  89.5 6.7 %all-to-all-start.2 = ((f32[16,144,384]{2,1,0:T(8,128)}), f32[16,144,384]{2,1,0:T(8,128)S(1)}, u32[]{:S(2)}, u32[]{:S(2)}) async-start(f32[16,144,384]{2,1,0:T(8,128)} %patch_windows.1), calls=%async_computation.2 | async-start | bytes 7077888 | tf_op jit(solution)/shard_map/all_to_all | solution.py:346
  96.2 4.7 %join_rows.1 = f32[1024,512]{1,0:T(8,128)} custom-call(f32[16,256,128]{2,1,0:T(8,128)} %copy-done.1), custom_call_target="tpu_custom_call" | custom-call | bytes 8388608 | tf_op jit(solution)/shard_map/join_rows/pallas_call | solution.py:72
  100.9 47.3 %all-to-all-done.2.kappa_ref = f32[16,144,384]{2,1,0:T(8,128)S(1)} async-done(((f32[16,144,384]{2,1,0:T(8,128)}), f32[16,144,384]{2,1,0:T(8,128)S(1)}, u32[]{:S(2)}, u32[]{:S(2)}) %all-to-all-start.2) | async-done | bytes 3538976 | tf_op jit(solution)/shard_map/all_to_all | solution.py:346
  148.2 0.0 copy-start
  148.2 1.7 copy-done
  149.9 31.0 %solve_patches.1 = f32[8,48,2304]{2,1,0:T(8,128)} custom-call(f32[16,144,384]{2,1,0:T(8,128)} %copy-done), custom_call_target="tpu_custom_call" | custom-call | flops 53084160 | bytes 33554432 | tf_op jit(solution)/shard_map/solve_patches/pallas_call | solution.py:324
  (1 shorter events, 0.0 us)
Async XLA Ops:
  6.4 7.0 %copy-start.6 = (f32[512]{0:T(512)S(1)}, f32[512]{0:T(512)}, u32[]{:S(2)}) copy-start(f32[512]{0:T(512)} %param.6) | copy-start | bytes 6148
  6.4 7.0 %copy-start.2 = (f32[1024,512]{1,0:T(8,128)S(1)}, f32[1024,512]{1,0:T(8,128)}, u32[]{:S(2)}) copy-start(f32[1024,512]{1,0:T(8,128)} %constant.8.clone) | copy-start | bytes 6291460
  6.4 32.9 %all-to-all-start = ((f32[16,264,128]{2,1,0:T(8,128)}), f32[16,264,128]{2,1,0:T(8,128)}, u32[]{:S(2)}, u32[]{:S(2)}) async-start(f32[16,264,128]{2,1,0:T(8,128)} %split_rows.1), calls=%async_computation | async-start | bytes 4325376 | tf_op jit(solution)/shard_map/all_to_all | solution.py:346
  46.7 13.5 %copy-start.3 = (f32[4,512,128]{2,1,0:T(8,128)S(1)}, f32[4,512,128]{2,1,0:T(8,128)}, u32[]{:S(2)}) copy-start(f32[4,512,128]{2,1,0:T(8,128)} %get-tuple-element.7.p1_ref) | copy-start | bytes 3145732
  46.7 41.5 %all-to-all-start.1 = ((f32[16,256,128]{2,1,0:T(8,128)}), f32[16,256,128]{2,1,0:T(8,128)S(1)}, u32[]{:S(2)}, u32[]{:S(2)}) async-start(f32[16,256,128]{2,1,0:T(8,128)} %get-tuple-element.5), calls=%async_computation.1 | async-start | bytes 4194304 | tf_op jit(solution)/shard_map/all_to_all | solution.py:346
  53.5 18.7 %collective-permute-start = (f32[4,512,128]{2,1,0:T(8,128)}, f32[4,512,128]{2,1,0:T(8,128)S(1)}, u32[]{:S(2)}, u32[]{:S(2)}) collective-permute-start(f32[4,512,128]{2,1,0:T(8,128)} %get-tuple-element.6.p2_ref), channel_id=1, source_target_pairs={{0,1},{1,2},{2,3},{3,4},{4,5},{5,6},{6,7},{8,9},{9,10},{10,11},{11... | collective-permute-start | bytes 3145736 | tf_op jit(solution)/shard_map/ppermute | solution.py:365
  60.2 16.4 %collective-permute-start.1 = (f32[4,512,128]{2,1,0:T(8,128)S(1)}, f32[4,512,128]{2,1,0:T(8,128)S(1)}, u32[]{:S(2)}, u32[]{:S(2)}) collective-permute-start(f32[4,512,128]{2,1,0:T(8,128)S(1)} %copy-done.3), channel_id=1, source_target_pairs={{1,0},{2,1},{3,2},{4,3},{5,4},{6,5},{7,6},{9,8},{10,9},{11,10},{12... | collective-permute-start | bytes 3145736 | tf_op jit(solution)/shard_map/ppermute | solution.py:364
  72.2 4.4 %copy-start.4 = (f32[4,512,128]{2,1,0:T(8,128)}, f32[4,512,128]{2,1,0:T(8,128)S(1)}, u32[]{:S(2)}) copy-start(f32[4,512,128]{2,1,0:T(8,128)S(1)} %collective-permute-done.p0_ref) | copy-start | bytes 3145732
  76.6 1.0 copy-start.5
  88.2 1.3 copy-start.1
  89.5 58.6 %all-to-all-start.2 = ((f32[16,144,384]{2,1,0:T(8,128)}), f32[16,144,384]{2,1,0:T(8,128)S(1)}, u32[]{:S(2)}, u32[]{:S(2)}) async-start(f32[16,144,384]{2,1,0:T(8,128)} %patch_windows.1), calls=%async_computation.2 | async-start | bytes 7077888 | tf_op jit(solution)/shard_map/all_to_all | solution.py:346
  148.2 1.7 copy-start

commit v3 on v2

v3 whole, which is shorter than its diff:
```python
import math

import jax
import jax.numpy as jnp
import numpy as np
from jax import lax
from jax.experimental import pallas as pl
from jax.experimental.pallas import tpu as pltpu
from jax.sharding import PartitionSpec as P

NX = 512
NZ = 512
CY = 32
CX = 32
CORE = 16
LAYER = 16
WIDE = 16
PATCH_DEV = 8
EDGE = 48
TAPS = 3
LANES = PATCH_DEV * EDGE
SIDE = 128
TILES = NZ // SIDE
ROWS = 2 * TILES * CX
TINY = 1e-06
F32 = jnp.float32
VMEM_LIMIT = 56 * 1024 * 1024


def params():
    return pltpu.CompilerParams(vmem_limit_bytes=VMEM_LIMIT)


def full(shape):
    return jax.ShapeDtypeStruct(shape, F32)


def exchange(pieces):
    row = lax.broadcasted_iota(jnp.int32, pieces[0].shape, 0)
    pieces = list(pieces)
    for bit in (4, 2, 1):
        upper = (row & bit) != 0
        for i in range(8):
            k = i | bit
            if i == k:
                continue
            pieces[i], pieces[k] = (
                jnp.where(upper, pltpu.roll(pieces[k], bit, 0), pieces[i]),
                jnp.where(upper, pieces[k], pltpu.roll(pieces[i], 8 - bit, 0)),
            )
    return pieces


def split_kernel(in_ref, send_ref, source_ref, out_ref, held, sems):
    j = pl.program_id(0)

    def leave(t, tile):
        rows = pl.ds(pl.multiple_of((t * TILES + tile) * CX, CX), CX)
        return pltpu.make_async_copy(held.at[:, rows, :], out_ref.at[:, rows, :], sems.at[t, tile])

    def leave_tables():
        rows = pl.ds(ROWS, 8)
        return pltpu.make_async_copy(held.at[:, rows, :], out_ref.at[:, rows, :], sems.at[2, 0])

    @pl.when(j == 0)
    def _():
        for w in range(WIDE):
            held[w, ROWS:ROWS + 1, 0:WIDE] = send_ref[...].astype(F32)
            held[w, ROWS + 1:ROWS + 2, 0:PATCH_DEV] = source_ref[...].astype(F32)
        leave_tables().start()

    for t in range(2):
        first = pl.multiple_of((t * TILES + j) * CX, CX)
        for x in range(0, CX, 8):
            for y in range(0, WIDE, 8):
                at = t * WIDE + y
                pieces = exchange([in_ref[x + i, at:at + 8, :] for i in range(8)])
                for i in range(8):
                    held[y + i, pl.ds(first + x, 8), :] = pieces[i]
        leave(t, j).start()

    @pl.when(j == TILES - 1)
    def _():
        leave_tables().wait()
        for t in range(2):
            for tile in range(TILES):
                leave(t, tile).wait()


def split_rows(block, send, source):
    return pl.pallas_call(
        split_kernel,
        grid=(TILES,),
        in_specs=[
            pl.BlockSpec((CX, CY, SIDE), lambda j: (0, 0, j)),
            pl.BlockSpec((1, WIDE), lambda j: (0, 0)),
            pl.BlockSpec((1, PATCH_DEV), lambda j: (0, 0)),
        ],
        out_specs=pl.BlockSpec(memory_space=pl.ANY),
        out_shape=full((WIDE, ROWS + 8, SIDE)),
        scratch_shapes=[
            pltpu.VMEM((WIDE, ROWS + 8, SIDE), F32),
            pltpu.SemaphoreType.DMA((3, TILES)),
        ],
        compiler_params=params(),
        cost_estimate=pl.CostEstimate(flops=0, bytes_accessed=8 << 20, transcendentals=0),
        name="split_rows",
    )(block, send, source)


def join_kernel(in_ref, *refs):
    out_ref = refs[-1]
    for x in range(0, CX, 8):
        for y in range(0, WIDE, 8):
            pieces = exchange([in_ref[y + i, x:x + 8, :] for i in range(8)])
            for i in range(8):
                out_ref[x + i, y:y + 8, :] = pieces[i]


def join_rows(t, parts, *others):
    return pl.pallas_call(
        join_kernel,
        grid=(TILES,),
        in_specs=[pl.BlockSpec((WIDE, CX, SIDE), lambda j: (0, j, 0))]
        + [pl.BlockSpec(memory_space=pl.ANY)] * len(others),
        out_specs=pl.BlockSpec((CX, WIDE, SIDE), lambda j: (0, t, j)),
        out_shape=full((CX, CY, NZ)),
        input_output_aliases={1: 0} if others else {},
        compiler_params=params(),
        cost_estimate=pl.CostEstimate(flops=0, bytes_accessed=4 << 20, transcendentals=0),
        name="join_rows",
    )(parts, *others)


def pair_kernel(in_ref, high_ref, low_ref):
    value = in_ref[...]
    high = value.astype(jnp.bfloat16)
    high_ref[...] = high
    low_ref[...] = (value - high.astype(F32)).astype(jnp.bfloat16)


def bf16_pair(matrix):
    return pl.pallas_call(
        pair_kernel,
        out_shape=[jax.ShapeDtypeStruct((NX, NX), jnp.bfloat16)] * 2,
        compiler_params=params(),
        cost_estimate=pl.CostEstimate(flops=0, bytes_accessed=2 << 20, transcendentals=0),
        name="bf16_pair",
    )(matrix)


def filter_kernel(high_ref, low_ref, in_ref, parts_ref, plane_ref):
    lines = jnp.concatenate(
        [in_ref[:, 0:CX, :].reshape(NX, SIDE), in_ref[:, CX:, :].reshape(NX, SIDE)], axis=1
    )
    high = lines.astype(jnp.bfloat16)
    low = (lines - high.astype(F32)).astype(jnp.bfloat16)
    dot = lambda a, b: jnp.dot(a, b, preferred_element_type=F32)
    small = dot(high_ref[...], low) + dot(low_ref[...], high)
    value = jnp.exp(dot(high_ref[...], high) + small)
    for k in range(2):
        side = value[:, k * SIDE:(k + 1) * SIDE]
        parts_ref[:, k * CX:(k + 1) * CX, :] = side.reshape(WIDE, CX, SIDE)
        plane_ref[k] = 0.5 * side


def filter_exp(t, pair, lines):
    whole = pl.BlockSpec((NX, NX), lambda i: (0, 0))
    return pl.pallas_call(
        filter_kernel,
        grid=(2,),
        in_specs=[whole, whole, pl.BlockSpec((WIDE, 2 * CX, SIDE), lambda i: (0, 2 * t + i, 0))],
        out_specs=[
            pl.BlockSpec((WIDE, 2 * CX, SIDE), lambda i: (0, i, 0)),
            pl.BlockSpec((2, NX, SIDE), lambda i: (i, 0, 0)),
        ],
        out_shape=[full((WIDE, TILES * CX, SIDE)), full((TILES, NX, SIDE))],
        compiler_params=params(),
        cost_estimate=pl.CostEstimate(
            flops=6 * NX * NX * NZ, bytes_accessed=4 << 20, transcendentals=NX * NZ
        ),
        name="filter_exp",
    )(*pair, lines)


def window_kernel(table_ref, p0_ref, p1_ref, p2_ref, p3_ref, out_ref, held, sems):
    owner = pl.program_id(0)

    @pl.when(owner == 0)
    def _():
        copies = [
            pltpu.make_async_copy(
                src, held.at[t, pl.ds(1, TILES), pl.ds(LAYER, NX), :], sems.at[t]
            )
            for t, src in enumerate((p0_ref, p1_ref, p2_ref, p3_ref))
        ]
        for copy in copies:
            copy.start()
        side = jnp.zeros((NX + 2 * LAYER, SIDE), F32)
        for t in range(4):
            held[t, 0] = side
            held[t, TILES + 1] = side
            for j in range(TILES):
                held[t, 1 + j, 0:LAYER, :] = side[:LAYER]
                held[t, 1 + j, LAYER + NX:, :] = side[:LAYER]
        for copy in copies:
            copy.wait()

    places = []
    for p in range(PATCH_DEV):
        source = table_ref[owner, WIDE + p]
        core = jnp.maximum(table_ref[source, owner], 0)
        x_at = source * CX + (core >> 6) * CORE
        t_at = (core >> 5) & 1
        z_at = (core & 31) * CORE + (SIDE - LAYER)
        tile = z_at >> 7
        offset = z_at & (SIDE - 1)
        turn = ((p * EDGE) % SIDE - offset) & (SIDE - 1)
        places.append((pl.multiple_of(x_at, CORE), t_at, tile, offset, turn))
    lane = lax.broadcasted_iota(jnp.int32, (EDGE, SIDE), 1)
    for t in range(TAPS):
        tiles = [None] * 3
        for p, (x_at, t_at, tile, offset, turn) in enumerate(places):
            rows = pl.ds(x_at, EDGE)
            first = held[t_at + t, tile, rows, :]
            second = held[t_at + t, tile + 1, rows, :]
            moved = pltpu.roll(jnp.where(lane >= offset, first, second), turn, 1)
            at = (p * EDGE) % SIDE
            q = (p * EDGE) // SIDE
            tiles[q] = moved if at == 0 else jnp.where(lane >= at, moved, tiles[q])
            if at + EDGE > SIDE:
                tiles[q + 1] = moved
        for q in range(3):
            out_ref[t * EDGE:(t + 1) * EDGE, q * SIDE:(q + 1) * SIDE] = tiles[q]


def windows(table, planes):
    rows = TAPS * EDGE
    return pl.pallas_call(
        window_kernel,
        grid_spec=pltpu.PrefetchScalarGridSpec(
            num_scalar_prefetch=1,
            grid=(WIDE,),
            in_specs=[pl.BlockSpec(memory_space=pl.ANY)] * 4,
            out_specs=pl.BlockSpec((None, rows, LANES), lambda d, table: (d, 0, 0)),
            scratch_shapes=[
                pltpu.VMEM((4, TILES + 2, NX + 2 * LAYER, SIDE), F32),
                pltpu.SemaphoreType.DMA((4,)),
            ],
        ),
        out_shape=full((WIDE, rows, LANES)),
        compiler_params=params(),
        cost_estimate=pl.CostEstimate(flops=0, bytes_accessed=16 << 20, transcendentals=0),
        name="patch_windows",
    )(table, *planes)


STRIPS = EDGE // 8
GROUPS = EDGE // 8
PIECES = [(i, q) for i in range(STRIPS) for q in range(3)]


def piece(i, q):
    return (pl.ds(8 * i, 8), pl.ds(SIDE * q, SIDE))


def solve_kernel(half_ref, out_ref, half, first, image, heavy, face_x, face_y, face_z, ready, arrive, leave):
    arrivals = [
        pltpu.make_async_copy(
            half_ref.at[:, pl.ds(t * EDGE, EDGE), :], half.at[pl.ds(1 + t * WIDE, WIDE)], arrive.at[t]
        )
        for t in range(TAPS)
    ]
    for copy in arrivals:
        copy.start()
    none = jnp.zeros((8, SIDE), F32)
    for at in PIECES:
        half[0, *piece(*at)] = none
        half[EDGE + 1, *piece(*at)] = none
        first[EDGE, *piece(*at)] = none
        image[EDGE, *piece(*at)] = none

    row = lax.broadcasted_iota(jnp.int32, (8, SIDE), 0)
    lane = lax.broadcasted_iota(jnp.int32, (8, SIDE), 1)
    row_low, row_high = row == 0, row == 7
    lane_low, lane_high = lane == 0, lane == SIDE - 1
    depth = []
    for q in range(3):
        place = lane + q * SIDE
        depth.append(place - ((place * 1366) >> 16) * EDGE)
    z_low = [d == 0 for d in depth]
    z_high = [d == EDGE - 1 for d in depth]

    def above_x(slab):
        turned = {at: pltpu.roll(slab[at], 7, 0) for at in PIECES}
        return {
            (i, q): jnp.where(row_high, turned[i + 1, q] if i < STRIPS - 1 else 0.0, turned[i, q])
            for i, q in PIECES
        }

    def below_x(slab):
        turned = {at: pltpu.roll(slab[at], 1, 0) for at in PIECES}
        return {
            (i, q): jnp.where(row_low, turned[i - 1, q] if i else 0.0, turned[i, q])
            for i, q in PIECES
        }

    def above_z(strip):
        turned = [pltpu.roll(v, SIDE - 1, 1) for v in strip]
        return [
            jnp.where(lane_high, turned[1], turned[0]),
            jnp.where(lane_high, turned[2], turned[1]),
            turned[2],
        ]

    def below_z(strip):
        turned = [pltpu.roll(v, 1, 1) for v in strip]
        return [
            jnp.where(lane_low, 0.0, turned[0]),
            jnp.where(lane_low, turned[0], turned[1]),
            jnp.where(lane_low, turned[1], turned[2]),
        ]

    def load(ref, y):
        return {at: ref[y, *piece(*at)] for at in PIECES}

    def strip(slab, i):
        return [slab[i, q] for q in range(3)]

    same = jnp.where(
        ((lax.broadcasted_iota(jnp.int32, (LANES, LANES), 0) * 1366) >> 16)
        == ((lax.broadcasted_iota(jnp.int32, (LANES, LANES), 1) * 1366) >> 16),
        1.0,
        0.0,
    ).astype(jnp.bfloat16)

    def patch_total(parts):
        part = jnp.concatenate(parts, axis=1)
        high = part.astype(jnp.bfloat16).astype(F32)
        middle = (part - high).astype(jnp.bfloat16).astype(F32)
        low = part - high - middle
        stack = jnp.concatenate([high, middle, low, jnp.zeros_like(low)], axis=0)
        spread = jnp.dot(stack.astype(jnp.bfloat16), same, preferred_element_type=F32)
        total = jnp.sum(spread, axis=0, keepdims=True)
        return [
            jnp.broadcast_to(total[:, SIDE * q:SIDE * (q + 1)], (8, SIDE)) for q in range(3)
        ]

    def divide(top, bottom):
        return [t / (b + TINY) for t, b in zip(top, bottom)]

    nothing = (none, none, none)

    def faces_of(y, rr):
        rr = list(rr)
        h = load(half, y + 1)
        h_up = above_x(h)
        h_down = below_x(h)
        for i in range(STRIPS):
            ups, downs = above_z(strip(h, i)), below_z(strip(h, i))
            for q in range(3):
                here, to = h[i, q], piece(i, q)
                v = h_up[i, q] - h_down[i, q]
                z_up = jnp.where(z_high[q], 0.0, ups[q])
                z_down = jnp.where(z_low[q], 0.0, downs[q])
                y_up = half[y + 2, *to]
                y_down = half[y, *to]
                across = here + h_up[i, q]
                if i == STRIPS - 1:
                    across = jnp.where(row_high, 0.0, across)
                heavy[y, *to] = (
                    (1.0 + 6.0 * here) + (h_up[i, q] + h_down[i, q])
                    + ((y_up + y_down) + (z_up + z_down))
                )
                face_x[y, *to] = across
                face_y[y, *to] = here + y_up
                face_z[y, *to] = jnp.where(z_high[q], 0.0, here + z_up)
                first[y, *to] = v
                rr[q] = rr[q] + v * v
        return tuple(rr)

    rr = nothing
    for t in range(TAPS):
        arrivals[t].wait()
        start = 0 if t == 0 else t * WIDE - 1
        stop = EDGE if t == TAPS - 1 else (t + 1) * WIDE - 1
        rr = lax.fori_loop(start, stop, faces_of, rr)
    for at in PIECES:
        face_y[EDGE - 1, *piece(*at)] = none
        ready[0, *piece(*at)] = none
    rr = patch_total(rr)

    def image_of(y, total):
        total = list(total)
        v = load(first, y)
        v_up = above_x(v)
        across = load(face_x, y)
        from_x = below_x({at: across[at] * v[at] for at in PIECES})
        for i in range(STRIPS):
            deep = [face_z[y, *piece(i, q)] for q in range(3)]
            ups = above_z(strip(v, i))
            downs = below_z([deep[q] * v[i, q] for q in range(3)])
            for q in range(3):
                to = piece(i, q)
                along = face_y[y, *to]
                couple = across[i, q] * v_up[i, q] + from_x[i, q]
                couple = couple + (along * first[y + 1, *to] + ready[0, *to])
                couple = couple + (deep[q] * ups[q] + downs[q])
                result = heavy[y, *to] * v[i, q] - couple
                ready[0, *to] = along * v[i, q]
                image[y, *to] = result
                total[q] = total[q] + v[i, q] * result
        return tuple(total)

    alpha = divide(rr, patch_total(lax.fori_loop(0, EDGE, image_of, nothing)))

    def residual_of(y, total):
        total = list(total)
        for i, q in PIECES:
            left = first[y, *piece(i, q)] - alpha[q] * image[y, *piece(i, q)]
            total[q] = total[q] + left * left
        return tuple(total)

    new = patch_total(lax.fori_loop(0, EDGE, residual_of, nothing))
    beta = divide(new, rr)

    def direction(y, i, q):
        v = first[y, *piece(i, q)]
        return (v - alpha[q] * image[y, *piece(i, q)]) + beta[q] * v

    for at in PIECES:
        ready[0, *piece(*at)] = direction(0, *at)

    def energy_of(y, total):
        total = list(total)
        v = load(ready, 0)
        v_up = above_x(v)
        for i in range(STRIPS):
            ups = above_z(strip(v, i))
            for q in range(3):
                to = piece(i, q)
                y_up = direction(y + 1, i, q)
                ready[0, *to] = y_up
                couple = face_x[y, *to] * v_up[i, q]
                couple = couple + face_y[y, *to] * y_up
                couple = couple + face_z[y, *to] * ups[q]
                total[q] = total[q] + v[i, q] * (heavy[y, *to] * v[i, q] - 2.0 * couple)
        return tuple(total)

    alpha_next = divide(new, patch_total(lax.fori_loop(0, EDGE, energy_of, nothing)))
    on_first = [alpha[q] + alpha_next[q] * (1.0 + beta[q]) for q in range(3)]
    on_image = [-(alpha_next[q] * alpha[q]) for q in range(3)]

    ends = [lane < end for end in (48, 96, 16, 64, 112, 32, 80)]
    departures = []
    for group in range(GROUPS):

        def correct(i, _):
            rows = pl.ds(8*i,8)
            chunks = []
            for j in range(8):
                line = []
                for q in range(3):
                    at = (8 * group + j, rows, pl.ds(SIDE * q, SIDE))
                    line.append(on_first[q] * first[*at] + on_image[q] * image[*at])
                a, b, c = line
                cut = [a, a, jnp.where(ends[1], b, a), b, b, jnp.where(ends[4], c, b), c, c]
                chunks.append(cut)
            for p in range(PATCH_DEV):
                c = []
                for j in range(8):
                    turn = (EDGE * (j - p)) % SIDE
                    c.append(pltpu.roll(chunks[j][p], turn, 1) if turn else chunks[j][p])
                tiles = (
                    jnp.where(ends[0], c[0], jnp.where(ends[1], c[1], c[2])),
                    jnp.where(ends[2], c[2], jnp.where(ends[3], c[3], jnp.where(ends[4], c[4], c[5]))),
                    jnp.where(ends[5], c[5], jnp.where(ends[6], c[6], c[7])),
                )
                for q in range(3):
                    heavy[8 * group + p, rows, pl.ds(SIDE * q, SIDE)] = tiles[q]
            return 0

        [correct(i,0) for i in range(STRIPS)]
        departures.append(
            pltpu.make_async_copy(
                heavy.at[pl.ds(8 * group, PATCH_DEV)],
                out_ref.at[:, :, pl.ds(group * LANES, LANES)],
                leave.at[group],
            )
        )
        departures[-1].start()
    for copy in departures:
        copy.wait()


def solve(half):
    cube = pltpu.VMEM((EDGE, EDGE, LANES), F32)
    longer = pltpu.VMEM((EDGE + 1, EDGE, LANES), F32)
    return pl.pallas_call(
        solve_kernel,
        in_specs=[pl.BlockSpec(memory_space=pl.ANY)],
        out_specs=pl.BlockSpec(memory_space=pl.ANY),
        out_shape=full((PATCH_DEV, EDGE, EDGE * EDGE)),
        scratch_shapes=[
            pltpu.VMEM((EDGE + 2, EDGE, LANES), F32),
            longer,
            longer,
            cube,
            cube,
            cube,
            cube,
            pltpu.VMEM((1, EDGE, LANES), F32),
            pltpu.SemaphoreType.DMA((TAPS,)),
            pltpu.SemaphoreType.DMA((GROUPS,)),
        ],
        compiler_params=params(),
        cost_estimate=pl.CostEstimate(
            flops=60 * EDGE**3 * PATCH_DEV, bytes_accessed=32 << 20, transcendentals=0
        ),
        name="solve_patches",
    )(half)


def wave_tables():
    index = np.arange(NX, dtype=np.int64)
    angle = (index[:, None] * index[None, :] % NX) * (2.0 * math.pi / NX)
    waves = np.concatenate([np.cos(angle), np.sin(angle)], axis=0)
    return waves.astype(np.float32)


def on_device(noise, spectrum, send_core, recv_source):
    swap = lambda v: lax.all_to_all(v, "wide", split_axis=0, concat_axis=0)
    lines = swap(
        split_rows(noise, send_core.reshape(1, WIDE), recv_source.reshape(1, PATCH_DEV))
    )
    table = jnp.concatenate(
        [lines[:, ROWS, :WIDE], lines[:, ROWS + 1, :PATCH_DEV]], axis=1
    ).astype(jnp.int32)
    waves = jnp.asarray(wave_tables())
    weights = jnp.concatenate([spectrum, spectrum])[:, None] / NX
    matrix = lax.dot_general(
        waves,
        waves * weights,
        (((0,), (0,)), ((), ())),
        precision=lax.Precision.HIGHEST,
        preferred_element_type=F32,
    )
    count = lax.axis_size("mid")
    forward = [(i, i + 1) for i in range(count - 1)]
    backward = [(i + 1, i) for i in range(count - 1)]
    pair = bf16_pair(matrix)
    parts_low, low = filter_exp(0, pair, lines)
    parts_high, high = filter_exp(1, pair, lines)
    above = lax.ppermute(low, "mid", backward)
    below = lax.ppermute(high, "mid", forward)
    back_low = swap(parts_low)
    outgoing = windows(table, (below, low, high, above))
    incoming = swap(outgoing)
    coefficient = join_rows(0, back_low)
    incoming, parts_high = lax.optimization_barrier((incoming, parts_high))
    back_high = swap(parts_high)
    solved = solve(incoming)
    coefficient = join_rows(1, back_high, coefficient)
    return coefficient, solved.reshape(1, 1, PATCH_DEV, EDGE, EDGE * EDGE)


def solution(mesh):
    in_specs = (P("wide", "mid", None), P(), P("wide", "mid", None), P("wide", "mid", None))
    out_specs = (P("wide", "mid", None), P("wide", "mid", None, None, None))
    return jax.shard_map(
        on_device, mesh=mesh, in_specs=in_specs, out_specs=out_specs, check_vma=False
    )
```

time: 181 us -> 183 us (1.011)
  the two profiles are of different devices: /device:TPU:77 before, /device:TPU:10 now
where the time goes in v3:
time: 183 us; the launch traced here: 182 us
  Pallas kernels  51.7 us (28%)
  blocking collectives  49.3 us (27%)
  waiting for transfers between devices  43.8 us (24%)
  starting transfers between devices  23.7 us (13%)
  matrix products  7.13 us (4%)
  local copies, waits for them, and re-layouts  5 us (3%)
    all_to_all x1, blocking collectives, on_device(): swap = lambda v: lax.all_to_all(v, 'wide', split_axis=0, concat_axis=0)  49.3 us
    all_to_all x3, waiting for transfers between devices, on_device(): swap = lambda v: lax.all_to_all(v, 'wide', split_axis=0, concat_axis=0)  32.3 us
    pallas_call x1, Pallas kernels, solve(): pl.pallas_call(solve_kernel, in_specs=[pl.BlockSpec(memory_space=pl.ANY)]...  21.2 us
    all_to_all x3, starting transfers between devices, on_device(): swap = lambda v: lax.all_to_all(v, 'wide', split_axis=0, concat_axis=0)  19.4 us
    pallas_call x1, Pallas kernels, windows(): pl.pallas_call(window_kernel, grid_spec=pltpu.PrefetchScalarGridSpec(num_...  10.6 us
    ppermute x1, waiting for transfers between devices, on_device(): below = lax.ppermute(high, 'mid', forward)  7.28 us
    dot_general x1, matrix products, on_device(): lax.dot_general(waves, waves * weights, (((0,), (0,)), ((), ())), precisi...  7.13 us
    pallas_call x2, Pallas kernels, filter_exp(): pl.pallas_call(filter_kernel, grid=(2,), in_specs=[whole, whole, pl.Block...  7.12 us
  transfers between devices with their start and end apart: 5, of which 4 were waited for; matrix products, arithmetic and copies ran while one was open for 5% of the time, Pallas kernels for 17%

profile of v3, /device:TPU:10, one launch (start us, length us, event | category | flops | bytes accessed | tf_op | source)
XLA Modules:
  0.0 182.0 jit_solution(2523843277078998765)
XLA Ops:
  0.6 3.7 %split_rows.1 = f32[16,264,128]{2,1,0:T(8,128)} custom-call(f32[32,32,512]{2,1,0:T(8,128)} %in_ref.1, s32[1,16]{1,0:T(1,128)} %bitcast.14, s32[1,8]{1,0:T(1,128)} %bitcast.15), custom_call_target="tpu_custom_call" | custom-call | bytes 8388608 | tf_op jit(solution)/shard_map/split_rows/pallas_call | solution.py:91
  4.3 0.0 copy-start.5
  4.3 8.3 %all-to-all-start = ((f32[16,264,128]{2,1,0:T(8,128)}), f32[16,264,128]{2,1,0:T(8,128)S(1)}, u32[]{:S(2)}, u32[]{:S(2)}) async-start(f32[16,264,128]{2,1,0:T(8,128)} %split_rows.1), calls=%async_computation | async-start | bytes 4325376 | tf_op jit(solution)/shard_map/all_to_all | solution.py:532
  12.7 0.0 copy-done.5
  12.7 7.1 %fusion.in_ref = f32[512,512]{1,0:T(8,128)} fusion(f32[1024,512]{1,0:T(8,128)} %constant.5.clone, f32[1024]{0:T(1024)S(1)} %maximum_multiply_fusion), kind=kOutput, calls=%fused_computation | convolution fusion | flops 3221749760 | bytes 3149824 | tf_op jit(solution)/shard_map/dot_general | solution.py:541
  19.8 2.3 %bf16_pair.1 = (bf16[512,512]{1,0:T(8,128)(2,1)}, bf16[512,512]{1,0:T(8,128)(2,1)}) custom-call(f32[512,512]{1,0:T(8,128)} %fusion.in_ref), custom_call_target="tpu_custom_call" | custom-call | bytes 2097152 | tf_op jit(solution)/shard_map/bf16_pair/pallas_call | solution.py:143
  22.1 18.5 %all-to-all-done.in_ref = f32[16,264,128]{2,1,0:T(8,128)S(1)} async-done(((f32[16,264,128]{2,1,0:T(8,128)}), f32[16,264,128]{2,1,0:T(8,128)S(1)}, u32[]{:S(2)}, u32[]{:S(2)}) %all-to-all-start) | async-done | bytes 2162720 | tf_op jit(solution)/shard_map/all_to_all | solution.py:532
  40.6 0.0 copy-start
  40.6 1.3 copy-done
  41.9 3.5 %filter_exp.3 = (f32[16,128,128]{2,1,0:T(8,128)}, f32[4,512,128]{2,1,0:T(8,128)}) custom-call(bf16[512,512]{1,0:T(8,128)(2,1)} %get-tuple-element.10.high_ref, bf16[512,512]{1,0:T(8,128)(2,1)} %get-tuple-element.11.low_ref, f32[16,264,128]{2,1,0:T(8,128)} %copy-done), custom_call_target="tpu_custom_call" | custom-call | flops 805306368 | bytes 4194304 | tf_op jit(solution)/shard_map/filter_exp/pallas_call | solution.py:169
  45.5 1.9 %collective-permute-start.1 = (f32[4,512,128]{2,1,0:T(8,128)}, f32[4,512,128]{2,1,0:T(8,128)S(1)}, u32[]{:S(2)}, u32[]{:S(2)}) collective-permute-start(f32[4,512,128]{2,1,0:T(8,128)} %get-tuple-element.13.p1_ref), channel_id=1, source_target_pairs={{1,0},{2,1},{3,2},{4,3},{5,4},{6,5},{7,6},{9,8},{10,9},{11,10},{12... | collective-permute-start | bytes 3145736 | tf_op jit(solution)/shard_map/ppermute | solution.py:554
  47.4 3.6 %filter_exp.2 = (f32[16,128,128]{2,1,0:T(8,128)}, f32[4,512,128]{2,1,0:T(8,128)}) custom-call(bf16[512,512]{1,0:T(8,128)(2,1)} %get-tuple-element.10.high_ref, bf16[512,512]{1,0:T(8,128)(2,1)} %get-tuple-element.11.low_ref, f32[16,264,128]{2,1,0:T(8,128)} %copy-done), custom_call_target="tpu_custom_call" | custom-call | flops 805306368 | bytes 4194304 | tf_op jit(solution)/shard_map/filter_exp/pallas_call | solution.py:169
  50.9 2.4 %collective-permute-start = (f32[4,512,128]{2,1,0:T(8,128)}, f32[4,512,128]{2,1,0:T(8,128)S(1)}, u32[]{:S(2)}, u32[]{:S(2)}) collective-permute-start(f32[4,512,128]{2,1,0:T(8,128)} %get-tuple-element.12.p2_ref), channel_id=1, source_target_pairs={{0,1},{1,2},{2,3},{3,4},{4,5},{5,6},{6,7},{8,9},{9,10},{10,11},{11... | collective-permute-start | bytes 3145736 | tf_op jit(solution)/shard_map/ppermute | solution.py:555
  53.4 0.8 slice.8
  54.2 0.8 slice.9
  55.0 0.7 maximum_convert_fusion.table_ref
  55.7 4.3 %collective-permute-done.1.p3_ref = f32[4,512,128]{2,1,0:T(8,128)S(1)} collective-permute-done((f32[4,512,128]{2,1,0:T(8,128)}, f32[4,512,128]{2,1,0:T(8,128)S(1)}, u32[]{:S(2)}, u32[]{:S(2)}) %collective-permute-start.1) | collective-permute-done | bytes 1048608 | tf_op jit(solution)/shard_map/ppermute | solution.py:554
  60.0 0.0 copy-start.3
  60.0 7.3 %collective-permute-done.p0_ref = f32[4,512,128]{2,1,0:T(8,128)S(1)} collective-permute-done((f32[4,512,128]{2,1,0:T(8,128)}, f32[4,512,128]{2,1,0:T(8,128)S(1)}, u32[]{:S(2)}, u32[]{:S(2)}) %collective-permute-start) | collective-permute-done | bytes 1048608 | tf_op jit(solution)/shard_map/ppermute | solution.py:555
  67.3 0.0 copy-done.3
  67.3 0.0 copy-start.4
  67.3 1.0 copy-done.4
  68.3 10.6 %patch_windows.1 = f32[16,144,384]{2,1,0:T(8,128)} custom-call(s32[16,24]{1,0:T(8,128)} %maximum_convert_fusion.table_ref, f32[4,512,128]{2,1,0:T(8,128)} %copy-done.4, f32[4,512,128]{2,1,0:T(8,128)} %get-tuple-element.13.p1_ref, f32[4,512,128]{2,1,0:T(8,128)} %get-tuple-element.12.p2_ref, f32[4,512,128]{2,1,0:T(8,128)} %copy-done.3), custom_call_target="tpu_custom_call" | custom-call | bytes 16777216 | tf_op jit(solution)/shard_map/patch_windows/pallas_call | solution.py:239
  78.8 49.3 %all_to_all.20.half_ref = f32[16,144,384]{2,1,0:T(8,128)} all-to-all(f32[16,144,384]{2,1,0:T(8,128)} %patch_windows.1), channel_id=1, replica_groups=mesh['wide'=16,'mid'=8] {'wide'}, dimensions={0} | all-to-all | bytes 7077888 | tf_op jit(solution)/shard_map/all_to_all | solution.py:532
  128.1 5.6 %all-to-all-start.3 = ((f32[16,128,128]{2,1,0:T(8,128)}), f32[16,128,128]{2,1,0:T(8,128)S(1)}, u32[]{:S(2)}, u32[]{:S(2)}) async-start(f32[16,128,128]{2,1,0:T(8,128)} %get-tuple-element.16), calls=%async_computation.3 | async-start | bytes 2097152 | tf_op jit(solution)/shard_map/all_to_all | solution.py:532
  133.7 13.8 %all-to-all-done.3.in_ref = f32[16,128,128]{2,1,0:T(8,128)S(1)} async-done(((f32[16,128,128]{2,1,0:T(8,128)}), f32[16,128,128]{2,1,0:T(8,128)S(1)}, u32[]{:S(2)}, u32[]{:S(2)}) %all-to-all-start.3) | async-done | bytes 1048608 | tf_op jit(solution)/shard_map/all_to_all | solution.py:532
  147.5 0.0 copy-start.1
  147.5 5.5 %all-to-all-start.2 = ((f32[16,128,128]{2,1,0:T(8,128)}), f32[16,128,128]{2,1,0:T(8,128)S(1)}, u32[]{:S(2)}, u32[]{:S(2)}) async-start(f32[16,128,128]{2,1,0:T(8,128)} %get-tuple-element.15), calls=%async_computation.2 | async-start | bytes 2097152 | tf_op jit(solution)/shard_map/all_to_all | solution.py:532
  153.0 0.0 copy-done.1
  153.0 3.5 %join_rows.2.refs_0_ = f32[32,32,512]{2,1,0:T(8,128)} custom-call(f32[16,128,128]{2,1,0:T(8,128)} %copy-done.1), custom_call_target="tpu_custom_call" | custom-call | bytes 4194304 | tf_op jit(solution)/shard_map/join_rows/pallas_call | solution.py:121
  156.4 21.2 %solve_patches.1 = f32[8,48,2304]{2,1,0:T(8,128)} custom-call(f32[16,144,384]{2,1,0:T(8,128)} %all_to_all.20.half_ref), custom_call_target="tpu_custom_call" | custom-call | flops 53084160 | bytes 33554432 | tf_op jit(solution)/shard_map/solve_patches/pallas_call | solution.py:499
  177.6 0.0 all-to-all-done.2.in_ref
  177.6 0.0 copy-start.2
  177.6 1.0 copy-done.2
  178.6 3.4 %join_rows.3 = f32[32,32,512]{2,1,0:T(8,128)} custom-call(f32[16,128,128]{2,1,0:T(8,128)} %copy-done.2, f32[32,32,512]{2,1,0:T(8,128)} %join_rows.2.refs_0_), custom_call_target="tpu_custom_call", output_to_operand_aliasing={{}: (1, {})} | custom-call | bytes 4194304 | tf_op jit(solution)/shard_map/join_rows/pallas_call | solution.py:121
  (1 shorter events, 0.0 us)
Async XLA Ops:
  4.3 8.3 %copy-start.5 = (f32[512]{0:T(512)S(1)}, f32[512]{0:T(512)}, u32[]{:S(2)}) copy-start(f32[512]{0:T(512)} %param.6) | copy-start | bytes 6148
  4.3 36.2 %all-to-all-start = ((f32[16,264,128]{2,1,0:T(8,128)}), f32[16,264,128]{2,1,0:T(8,128)S(1)}, u32[]{:S(2)}, u32[]{:S(2)}) async-start(f32[16,264,128]{2,1,0:T(8,128)} %split_rows.1), calls=%async_computation | async-start | bytes 4325376 | tf_op jit(solution)/shard_map/all_to_all | solution.py:532
  40.6 1.3 copy-start
  45.5 14.5 %collective-permute-start.1 = (f32[4,512,128]{2,1,0:T(8,128)}, f32[4,512,128]{2,1,0:T(8,128)S(1)}, u32[]{:S(2)}, u32[]{:S(2)}) collective-permute-start(f32[4,512,128]{2,1,0:T(8,128)} %get-tuple-element.13.p1_ref), channel_id=1, source_target_pairs={{1,0},{2,1},{3,2},{4,3},{5,4},{6,5},{7,6},{9,8},{10,9},{11,10},{12... | collective-permute-start | bytes 3145736 | tf_op jit(solution)/shard_map/ppermute | solution.py:554
  50.9 16.3 %collective-permute-start = (f32[4,512,128]{2,1,0:T(8,128)}, f32[4,512,128]{2,1,0:T(8,128)S(1)}, u32[]{:S(2)}, u32[]{:S(2)}) collective-permute-start(f32[4,512,128]{2,1,0:T(8,128)} %get-tuple-element.12.p2_ref), channel_id=1, source_target_pairs={{0,1},{1,2},{2,3},{3,4},{4,5},{5,6},{6,7},{8,9},{9,10},{10,11},{11... | collective-permute-start | bytes 3145736 | tf_op jit(solution)/shard_map/ppermute | solution.py:555
  60.0 7.3 %copy-start.3 = (f32[4,512,128]{2,1,0:T(8,128)}, f32[4,512,128]{2,1,0:T(8,128)S(1)}, u32[]{:S(2)}) copy-start(f32[4,512,128]{2,1,0:T(8,128)S(1)} %collective-permute-done.1.p3_ref) | copy-start | bytes 3145732
  67.3 1.0 copy-start.4
  128.1 19.4 %all-to-all-start.3 = ((f32[16,128,128]{2,1,0:T(8,128)}), f32[16,128,128]{2,1,0:T(8,128)S(1)}, u32[]{:S(2)}, u32[]{:S(2)}) async-start(f32[16,128,128]{2,1,0:T(8,128)} %get-tuple-element.16), calls=%async_computation.3 | async-start | bytes 2097152 | tf_op jit(solution)/shard_map/all_to_all | solution.py:532
  147.5 5.5 %copy-start.1 = (f32[16,128,128]{2,1,0:T(8,128)}, f32[16,128,128]{2,1,0:T(8,128)S(1)}, u32[]{:S(2)}) copy-start(f32[16,128,128]{2,1,0:T(8,128)S(1)} %all-to-all-done.3.in_ref) | copy-start | bytes 3145732
  147.5 30.1 %all-to-all-start.2 = ((f32[16,128,128]{2,1,0:T(8,128)}), f32[16,128,128]{2,1,0:T(8,128)S(1)}, u32[]{:S(2)}, u32[]{:S(2)}) async-start(f32[16,128,128]{2,1,0:T(8,128)} %get-tuple-element.15), calls=%async_computation.2 | async-start | bytes 2097152 | tf_op jit(solution)/shard_map/all_to_all | solution.py:532
  177.6 1.0 copy-start.2

commit v4 on v3

--- a/solution.py
+++ b/solution.py
@@ -1,3 +1,4 @@
+import functools
 import math
 
 import jax
@@ -22,6 +23,7 @@
 SIDE = 128
 TILES = NZ // SIDE
 ROWS = 2 * TILES * CX
+OWNERS = 4
 TINY = 1e-06
 F32 = jnp.float32
 VMEM_LIMIT = 56 * 1024 * 1024
@@ -108,28 +110,29 @@
     )(block, send, source)
 
 
-def join_kernel(in_ref, *refs):
-    out_ref = refs[-1]
-    for x in range(0, CX, 8):
-        for y in range(0, WIDE, 8):
-            pieces = exchange([in_ref[y + i, x:x + 8, :] for i in range(8)])
-            for i in range(8):
-                out_ref[x + i, y:y + 8, :] = pieces[i]
-
-
-def join_rows(t, parts, *others):
+def join_kernel(low_ref, high_ref, out_ref):
+    for t, in_ref in enumerate((low_ref, high_ref)):
+        for x in range(0, CX, 8):
+            for y in range(0, WIDE, 8):
+                pieces = exchange([in_ref[y + i, x:x + 8, :] for i in range(8)])
+                for i in range(8):
+                    out_ref[x + i, t * WIDE + y:t * WIDE + y + 8, :] = pieces[i]
+
+
+def join_rows(parts):
     return pl.pallas_call(
         join_kernel,
         grid=(TILES,),
-        in_specs=[pl.BlockSpec((WIDE, CX, SIDE), lambda j: (0, j, 0))]
-        + [pl.BlockSpec(memory_space=pl.ANY)] * len(others),
-        out_specs=pl.BlockSpec((CX, WIDE, SIDE), lambda j: (0, t, j)),
+        in_specs=[
+            pl.BlockSpec((WIDE, CX, SIDE), lambda j: (0, j, 0)),
+            pl.BlockSpec((WIDE, CX, SIDE), lambda j: (0, TILES + j, 0)),
+        ],
+        out_specs=pl.BlockSpec((CX, CY, SIDE), lambda j: (0, 0, j)),
         out_shape=full((CX, CY, NZ)),
-        input_output_aliases={1: 0} if others else {},
         compiler_params=params(),
-        cost_estimate=pl.CostEstimate(flops=0, bytes_accessed=4 << 20, transcendentals=0),
+        cost_estimate=pl.CostEstimate(flops=0, bytes_accessed=8 << 20, transcendentals=0),
         name="join_rows",
-    )(parts, *others)
+    )(parts, parts)
 
 
 def pair_kernel(in_ref, high_ref, low_ref):
@@ -149,7 +152,8 @@
     )(matrix)
 
 
-def filter_kernel(high_ref, low_ref, in_ref, parts_ref, plane_ref):
+def filter_kernel(high_ref, low_ref, in_ref, *refs):
+    parts_ref, plane_ref = refs[-2:]
     lines = jnp.concatenate(
         [in_ref[:, 0:CX, :].reshape(NX, SIDE), in_ref[:, CX:, :].reshape(NX, SIDE)], axis=1
     )
@@ -164,40 +168,44 @@
         plane_ref[k] = 0.5 * side
 
 
-def filter_exp(t, pair, lines):
+def filter_exp(t, pair, lines, *others):
     whole = pl.BlockSpec((NX, NX), lambda i: (0, 0))
     return pl.pallas_call(
         filter_kernel,
         grid=(2,),
-        in_specs=[whole, whole, pl.BlockSpec((WIDE, 2 * CX, SIDE), lambda i: (0, 2 * t + i, 0))],
+        in_specs=[whole, whole, pl.BlockSpec((WIDE, 2 * CX, SIDE), lambda i: (0, 2 * t + i, 0))]
+        + [pl.BlockSpec(memory_space=pl.ANY)] * len(others),
         out_specs=[
-            pl.BlockSpec((WIDE, 2 * CX, SIDE), lambda i: (0, i, 0)),
+            pl.BlockSpec((WIDE, 2 * CX, SIDE), lambda i: (0, 2 * t + i, 0)),
             pl.BlockSpec((2, NX, SIDE), lambda i: (i, 0, 0)),
         ],
-        out_shape=[full((WIDE, TILES * CX, SIDE)), full((TILES, NX, SIDE))],
+        out_shape=[full((WIDE, ROWS, SIDE)), full((TILES, NX, SIDE))],
+        input_output_aliases={3: 0} if others else {},
         compiler_params=params(),
         cost_estimate=pl.CostEstimate(
             flops=6 * NX * NX * NZ, bytes_accessed=4 << 20, transcendentals=NX * NZ
         ),
         name="filter_exp",
-    )(*pair, lines)
-
-
-def window_kernel(table_ref, p0_ref, p1_ref, p2_ref, p3_ref, out_ref, held, sems):
-    owner = pl.program_id(0)
-
-    @pl.when(owner == 0)
+    )(*pair, lines, *others)
+
+
+def window_kernel(slots, table_ref, *refs):
+    low_ref, high_ref = refs[:2]
+    out_ref, held, sems = refs[-3:]
+    step = pl.program_id(0)
+
+    @pl.when(step == 0)
     def _():
         copies = [
             pltpu.make_async_copy(
                 src, held.at[t, pl.ds(1, TILES), pl.ds(LAYER, NX), :], sems.at[t]
             )
-            for t, src in enumerate((p0_ref, p1_ref, p2_ref, p3_ref))
+            for t, src in enumerate((low_ref, high_ref))
         ]
         for copy in copies:
             copy.start()
         side = jnp.zeros((NX + 2 * LAYER, SIDE), F32)
-        for t in range(4):
+        for t in range(2):
             held[t, 0] = side
             held[t, TILES + 1] = side
             for j in range(TILES):
@@ -206,53 +214,62 @@
         for copy in copies:
             copy.wait()
 
-    places = []
-    for p in range(PATCH_DEV):
-        source = table_ref[owner, WIDE + p]
-        core = jnp.maximum(table_ref[source, owner], 0)
-        x_at = source * CX + (core >> 6) * CORE
-        t_at = (core >> 5) & 1
-        z_at = (core & 31) * CORE + (SIDE - LAYER)
-        tile = z_at >> 7
-        offset = z_at & (SIDE - 1)
-        turn = ((p * EDGE) % SIDE - offset) & (SIDE - 1)
-        places.append((pl.multiple_of(x_at, CORE), t_at, tile, offset, turn))
     lane = lax.broadcasted_iota(jnp.int32, (EDGE, SIDE), 1)
-    for t in range(TAPS):
-        tiles = [None] * 3
-        for p, (x_at, t_at, tile, offset, turn) in enumerate(places):
-            rows = pl.ds(x_at, EDGE)
-            first = held[t_at + t, tile, rows, :]
-            second = held[t_at + t, tile + 1, rows, :]
-            moved = pltpu.roll(jnp.where(lane >= offset, first, second), turn, 1)
-            at = (p * EDGE) % SIDE
-            q = (p * EDGE) // SIDE
-            tiles[q] = moved if at == 0 else jnp.where(lane >= at, moved, tiles[q])
-            if at + EDGE > SIDE:
-                tiles[q + 1] = moved
-        for q in range(3):
-            out_ref[t * EDGE:(t + 1) * EDGE, q * SIDE:(q + 1) * SIDE] = tiles[q]
-
-
-def windows(table, planes):
-    rows = TAPS * EDGE
+
+    def one_owner(k, _):
+        owner = step * OWNERS + k
+        places = []
+        for p in range(PATCH_DEV):
+            source = table_ref[owner, WIDE + p]
+            core = jnp.maximum(table_ref[source, owner], 0)
+            x_at = source * CX + (core >> 6) * CORE
+            z_at = (core & 31) * CORE + (SIDE - LAYER)
+            offset = z_at & (SIDE - 1)
+            turn = ((p * EDGE) % SIDE - offset) & (SIDE - 1)
+            places.append((pl.multiple_of(x_at, CORE), (core >> 5) & 1, z_at >> 7, offset, turn))
+        for t in range(slots):
+            tiles = [None] * 3
+            for p, (x_at, t_at, tile, offset, turn) in enumerate(places):
+                plane = t if slots == 2 else t_at
+                rows = pl.ds(x_at, EDGE)
+                near = held[plane, tile, rows, :]
+                far = held[plane, tile + 1, rows, :]
+                moved = pltpu.roll(jnp.where(lane >= offset, near, far), turn, 1)
+                at = (p * EDGE) % SIDE
+                q = (p * EDGE) // SIDE
+                tiles[q] = moved if at == 0 else jnp.where(lane >= at, moved, tiles[q])
+                if at + EDGE > SIDE:
+                    tiles[q + 1] = moved
+            for q in range(3):
+                out_ref[k, t * EDGE:(t + 1) * EDGE, q * SIDE:(q + 1) * SIDE] = tiles[q]
+        return 0
+
+    lax.fori_loop(0, OWNERS, one_owner, 0)
+
+
+def windows(table, planes, *others):
+    slots = 1 if others else 2
+    at = 2 if others else 0
     return pl.pallas_call(
-        window_kernel,
+        functools.partial(window_kernel, slots),
         grid_spec=pltpu.PrefetchScalarGridSpec(
             num_scalar_prefetch=1,
-            grid=(WIDE,),
-            in_specs=[pl.BlockSpec(memory_space=pl.ANY)] * 4,
-            out_specs=pl.BlockSpec((None, rows, LANES), lambda d, table: (d, 0, 0)),
+            grid=(WIDE // OWNERS,),
+            in_specs=[pl.BlockSpec(memory_space=pl.ANY)] * (2 + len(others)),
+            out_specs=pl.BlockSpec((OWNERS, slots * EDGE, LANES), lambda d, table: (d, at, 0)),
             scratch_shapes=[
-                pltpu.VMEM((4, TILES + 2, NX + 2 * LAYER, SIDE), F32),
-                pltpu.SemaphoreType.DMA((4,)),
+                pltpu.VMEM((2, TILES + 2, NX + 2 * LAYER, SIDE), F32),
+                pltpu.SemaphoreType.DMA((2,)),
             ],
         ),
-        out_shape=full((WIDE, rows, LANES)),
+        out_shape=full((WIDE, TAPS * EDGE, LANES)),
+        input_output_aliases={3: 0} if others else {},
         compiler_params=params(),
-        cost_estimate=pl.CostEstimate(flops=0, bytes_accessed=16 << 20, transcendentals=0),
+        cost_estimate=pl.CostEstimate(
+            flops=0, bytes_accessed=slots * (6 << 20), transcendentals=0
+        ),
         name="patch_windows",
-    )(table, *planes)
+    )(table, *planes, *others)
 
 
 STRIPS = EDGE // 8
@@ -264,10 +281,12 @@
     return (pl.ds(8 * i, 8), pl.ds(SIDE * q, SIDE))
 
 
-def solve_kernel(half_ref, out_ref, half, first, image, heavy, face_x, face_y, face_z, ready, arrive, leave):
+def solve_kernel(
+    half_ref, later_ref, out_ref, half, first, image, heavy, face_x, face_y, face_z, ready, arrive, leave
+):
     arrivals = [
         pltpu.make_async_copy(
-            half_ref.at[:, pl.ds(t * EDGE, EDGE), :], half.at[pl.ds(1 + t * WIDE, WIDE)], arrive.at[t]
+            half_ref.at[:, pl.ds(t * EDGE, EDGE), :], (heavy, face_x, face_y)[t].at[pl.ds(0, WIDE)], arrive.at[t]
         )
         for t in range(TAPS)
     ]
@@ -351,40 +370,61 @@
 
     nothing = (none, none, none)
 
+    for copy in arrivals:
+        copy.wait()
+    in_order = [
+        jnp.broadcast_to(later_ref[:, SIDE * q:SIDE * (q + 1)], (8, SIDE)) != 0 for q in range(3)
+    ]
+
+    def arrange(w, _):
+        for i, q in PIECES:
+            at = piece(i, q)
+            a, b, c = heavy[w, *at], face_x[w, *at], face_y[w, *at]
+            half[1 + w, *at] = jnp.where(in_order[q], a, c)
+            half[1 + WIDE + w, *at] = jnp.where(in_order[q], b, a)
+            half[1 + 2 * WIDE + w, *at] = jnp.where(in_order[q], c, b)
+        return 0
+
+    lax.fori_loop(0, WIDE, arrange, 0)
+
     def faces_of(y, rr):
         rr = list(rr)
         h = load(half, y + 1)
         h_up = above_x(h)
         h_down = below_x(h)
+        deep_up, deep_down = {}, {}
         for i in range(STRIPS):
             ups, downs = above_z(strip(h, i)), below_z(strip(h, i))
             for q in range(3):
-                here, to = h[i, q], piece(i, q)
-                v = h_up[i, q] - h_down[i, q]
-                z_up = jnp.where(z_high[q], 0.0, ups[q])
-                z_down = jnp.where(z_low[q], 0.0, downs[q])
-                y_up = half[y + 2, *to]
-                y_down = half[y, *to]
-                across = here + h_up[i, q]
-                if i == STRIPS - 1:
-                    across = jnp.where(row_high, 0.0, across)
-                heavy[y, *to] = (
-                    (1.0 + 6.0 * here) + (h_up[i, q] + h_down[i, q])
-                    + ((y_up + y_down) + (z_up + z_down))
-                )
-                face_x[y, *to] = across
-                face_y[y, *to] = here + y_up
-                face_z[y, *to] = jnp.where(z_high[q], 0.0, here + z_up)
-                first[y, *to] = v
-                rr[q] = rr[q] + v * v
+                deep_up[i, q] = jnp.where(z_high[q], 0.0, ups[q])
+                deep_down[i, q] = jnp.where(z_low[q], 0.0, downs[q])
+        up_up, up_down = above_x(deep_up), below_x(deep_up)
+        down_up, down_down = above_x(deep_down), below_x(deep_down)
+        for i, q in PIECES:
+            here, to = h[i, q], piece(i, q)
+            z_up, z_down = deep_up[i, q], deep_down[i, q]
+            v = h_up[i, q] - h_down[i, q]
+            y_up = half[y + 2, *to]
+            y_down = half[y, *to]
+            across = here + h_up[i, q]
+            if i == STRIPS - 1:
+                across = jnp.where(row_high, 0.0, across)
+            deep = here + z_up
+            heavy[y, *to] = (
+                (1.0 + 6.0 * here) + (h_up[i, q] + h_down[i, q])
+                + ((y_up + y_down) + (z_up + z_down))
+            )
+            face_x[y, *to] = across
+            face_y[y, *to] = here + y_up
+            face_z[y, *to] = jnp.where(z_high[q], 0.0, deep)
+            first[y, *to] = v
+            image[y, *to] = deep * (up_up[i, q] - up_down[i, q]) + (here + z_down) * (
+                down_up[i, q] - down_down[i, q]
+            )
+            rr[q] = rr[q] + v * v
         return tuple(rr)
 
-    rr = nothing
-    for t in range(TAPS):
-        arrivals[t].wait()
-        start = 0 if t == 0 else t * WIDE - 1
-        stop = EDGE if t == TAPS - 1 else (t + 1) * WIDE - 1
-        rr = lax.fori_loop(start, stop, faces_of, rr)
+    rr = lax.fori_loop(0, EDGE, faces_of, nothing)
     for at in PIECES:
         face_y[EDGE - 1, *piece(*at)] = none
         ready[0, *piece(*at)] = none
@@ -396,20 +436,15 @@
         v_up = above_x(v)
         across = load(face_x, y)
         from_x = below_x({at: across[at] * v[at] for at in PIECES})
-        for i in range(STRIPS):
-            deep = [face_z[y, *piece(i, q)] for q in range(3)]
-            ups = above_z(strip(v, i))
-            downs = below_z([deep[q] * v[i, q] for q in range(3)])
-            for q in range(3):
-                to = piece(i, q)
-                along = face_y[y, *to]
-                couple = across[i, q] * v_up[i, q] + from_x[i, q]
-                couple = couple + (along * first[y + 1, *to] + ready[0, *to])
-                couple = couple + (deep[q] * ups[q] + downs[q])
-                result = heavy[y, *to] * v[i, q] - couple
-                ready[0, *to] = along * v[i, q]
-                image[y, *to] = result
-                total[q] = total[q] + v[i, q] * result
+        for i, q in PIECES:
+            to = piece(i, q)
+            along = face_y[y, *to]
+            couple = across[i, q] * v_up[i, q] + from_x[i, q]
+            couple = couple + (along * first[y + 1, *to] + ready[0, *to])
+            result = heavy[y, *to] * v[i, q] - (couple + image[y, *to])
+            ready[0, *to] = along * v[i, q]
+            image[y, *to] = result
+            total[q] = total[q] + v[i, q] * result
         return tuple(total)
 
     alpha = divide(rr, patch_total(lax.fori_loop(0, EDGE, image_of, nothing)))
@@ -493,12 +528,12 @@
         copy.wait()
 
 
-def solve(half):
+def solve(half, later):
     cube = pltpu.VMEM((EDGE, EDGE, LANES), F32)
     longer = pltpu.VMEM((EDGE + 1, EDGE, LANES), F32)
     return pl.pallas_call(
         solve_kernel,
-        in_specs=[pl.BlockSpec(memory_space=pl.ANY)],
+        in_specs=[pl.BlockSpec(memory_space=pl.ANY), pl.BlockSpec(memory_space=pltpu.VMEM)],
         out_specs=pl.BlockSpec(memory_space=pl.ANY),
         out_shape=full((PATCH_DEV, EDGE, EDGE * EDGE)),
         scratch_shapes=[
@@ -518,7 +553,7 @@
             flops=60 * EDGE**3 * PATCH_DEV, bytes_accessed=32 << 20, transcendentals=0
         ),
         name="solve_patches",
-    )(half)
+    )(half, later)
 
 
 def wave_tables():
@@ -549,18 +584,19 @@
     forward = [(i, i + 1) for i in range(count - 1)]
     backward = [(i + 1, i) for i in range(count - 1)]
     pair = bf16_pair(matrix)
-    parts_low, low = filter_exp(0, pair, lines)
-    parts_high, high = filter_exp(1, pair, lines)
+    parts, low = filter_exp(0, pair, lines)
     above = lax.ppermute(low, "mid", backward)
+    parts, high = filter_exp(1, pair, lines, parts)
     below = lax.ppermute(high, "mid", forward)
-    back_low = swap(parts_low)
-    outgoing = windows(table, (below, low, high, above))
+    back = swap(parts)
+    outgoing = windows(table, (low, high))
+    outgoing = windows(table, (below, above), outgoing)
+    outgoing, back = lax.optimization_barrier((outgoing, back))
     incoming = swap(outgoing)
-    coefficient = join_rows(0, back_low)
-    incoming, parts_high = lax.optimization_barrier((incoming, parts_high))
-    back_high = swap(parts_high)
-    solved = solve(incoming)
-    coefficient = join_rows(1, back_high, coefficient)
+    coefficient = join_rows(back)
+    cores = table[recv_source.reshape(-1), lax.axis_index("wide")]
+    later = jnp.repeat((cores >> 5) & 1, EDGE).reshape(1, LANES)
+    solved = solve(incoming, later)
     return coefficient, solved.reshape(1, 1, PATCH_DEV, EDGE, EDGE * EDGE)
 
 

time: 183 us -> 163 us (0.89)
  the two profiles are of different devices: /device:TPU:10 before, /device:TPU:117 now
where the time goes in v4:
time: 163 us
  waiting for transfers between devices  69.5 us (43%)
  Pallas kernels  49.4 us (30%)
  starting transfers between devices  28.4 us (17%)
  matrix products  7.14 us (4%)
  local copies, waits for them, and re-layouts  6.72 us (4%)
    all_to_all x3, waiting for transfers between devices, on_device(): swap = lambda v: lax.all_to_all(v, 'wide', split_axis=0, concat_axis=0)  63.5 us
    pallas_call x1, Pallas kernels, solve(): pl.pallas_call(solve_kernel, in_specs=[pl.BlockSpec(memory_space=pl.ANY),...  21 us
    all_to_all x3, starting transfers between devices, on_device(): swap = lambda v: lax.all_to_all(v, 'wide', split_axis=0, concat_axis=0)  20.1 us
    pallas_call x2, Pallas kernels, windows(): pl.pallas_call(functools.partial(window_kernel, slots), grid_spec=pltpu.P...  11.5 us
    pallas_call x2, Pallas kernels, filter_exp(): pl.pallas_call(filter_kernel, grid=(2,), in_specs=[whole, whole, pl.Block...  7.14 us
    dot_general x1, matrix products, on_device(): lax.dot_general(waves, waves * weights, (((0,), (0,)), ((), ())), precisi...  7.14 us
    ppermute x1, starting transfers between devices, on_device(): below = lax.ppermute(high, 'mid', forward)  6.37 us
    ppermute x1, waiting for transfers between devices, on_device(): above = lax.ppermute(low, 'mid', backward)  4.38 us
  transfers between devices with their start and end apart: 5, of which 4 were waited for; matrix products, arithmetic and copies ran while one was open for 7% of the time, Pallas kernels for 11%

profile of v4, /device:TPU:117, one launch (start us, length us, event | category | flops | bytes accessed | tf_op | source)
XLA Modules:
  0.0 162.6 jit_solution(12404130345388293956)
XLA Ops:
  0.6 3.7 %split_rows.1 = f32[16,264,128]{2,1,0:T(8,128)} custom-call(f32[32,32,512]{2,1,0:T(8,128)} %in_ref.1, s32[1,16]{1,0:T(1,128)} %bitcast.18, s32[1,8]{1,0:T(1,128)} %bitcast.19), custom_call_target="tpu_custom_call" | custom-call | bytes 8388608 | tf_op jit(solution)/shard_map/split_rows/pallas_call | solution.py:93
  4.3 0.0 copy-start.6
  4.3 6.4 %all-to-all-start = ((f32[16,264,128]{2,1,0:T(8,128)}), f32[16,264,128]{2,1,0:T(8,128)S(1)}, u32[]{:S(2)}, u32[]{:S(2)}) async-start(f32[16,264,128]{2,1,0:T(8,128)} %split_rows.1), calls=%async_computation | async-start | bytes 4325376 | tf_op jit(solution)/shard_map/all_to_all | solution.py:567
  10.7 0.0 copy-done.6
  10.7 7.1 %fusion.in_ref = f32[512,512]{1,0:T(8,128)} fusion(f32[1024,512]{1,0:T(8,128)} %constant.22.clone, f32[1024]{0:T(1024)S(1)} %maximum_multiply_fusion), kind=kOutput, calls=%fused_computation.1 | convolution fusion | flops 3221749760 | bytes 3149824 | tf_op jit(solution)/shard_map/dot_general | solution.py:576
  17.9 2.3 %bf16_pair.1 = (bf16[512,512]{1,0:T(8,128)(2,1)}, bf16[512,512]{1,0:T(8,128)(2,1)}) custom-call(f32[512,512]{1,0:T(8,128)} %fusion.in_ref), custom_call_target="tpu_custom_call" | custom-call | bytes 2097152 | tf_op jit(solution)/shard_map/bf16_pair/pallas_call | solution.py:146
  20.1 16.2 %all-to-all-done.in_ref = f32[16,264,128]{2,1,0:T(8,128)S(1)} async-done(((f32[16,264,128]{2,1,0:T(8,128)}), f32[16,264,128]{2,1,0:T(8,128)S(1)}, u32[]{:S(2)}, u32[]{:S(2)}) %all-to-all-start) | async-done | bytes 2162720 | tf_op jit(solution)/shard_map/all_to_all | solution.py:567
  36.3 0.0 copy-start.1
  36.3 1.3 copy-done.1
  37.7 3.5 %filter_exp.2 = (f32[16,256,128]{2,1,0:T(8,128)}, f32[4,512,128]{2,1,0:T(8,128)}) custom-call(bf16[512,512]{1,0:T(8,128)(2,1)} %get-tuple-element.10.high_ref, bf16[512,512]{1,0:T(8,128)(2,1)} %get-tuple-element.11.low_ref, f32[16,264,128]{2,1,0:T(8,128)} %copy-done.1), custom_call_target="tpu_custom_call" | custom-call | flops 805306368 | bytes 4194304 | tf_op jit(solution)/shard_map/filter_exp/pallas_call | solution.py:173
  41.2 3.6 %filter_exp.3 = (f32[16,256,128]{2,1,0:T(8,128)}, f32[4,512,128]{2,1,0:T(8,128)}) custom-call(bf16[512,512]{1,0:T(8,128)(2,1)} %get-tuple-element.10.high_ref, bf16[512,512]{1,0:T(8,128)(2,1)} %get-tuple-element.11.low_ref, f32[16,264,128]{2,1,0:T(8,128)} %copy-done.1, f32[16,256,128]{2,1,0:T(8,128)} %get-tuple-element.12.refs_0_), custom_call_target="tpu_custom_call", output_to_operand_aliasing={{0}: (3, {})} | custom-call | flops 805306368 | bytes 4194304 | tf_op jit(solution)/shard_map/filter_exp/pallas_call | solution.py:173
  44.8 0.0 copy-start.3
  44.8 7.0 %all-to-all-start.1 = ((f32[16,256,128]{2,1,0:T(8,128)}), f32[16,256,128]{2,1,0:T(8,128)S(1)}, u32[]{:S(2)}, u32[]{:S(2)}) async-start(f32[16,256,128]{2,1,0:T(8,128)} %get-tuple-element.15), calls=%async_computation.1 | async-start | bytes 4194304 | tf_op jit(solution)/shard_map/all_to_all | solution.py:567
  51.9 6.4 %collective-permute-start = (f32[4,512,128]{2,1,0:T(8,128)}, f32[4,512,128]{2,1,0:T(8,128)S(1)}, u32[]{:S(2)}, u32[]{:S(2)}) collective-permute-start(f32[4,512,128]{2,1,0:T(8,128)} %get-tuple-element.13.refs_1_), channel_id=1, source_target_pairs={{0,1},{1,2},{2,3},{3,4},{4,5},{5,6},{6,7},{8,9},{9,10},{10,11},{11... | collective-permute-start | bytes 3145736 | tf_op jit(solution)/shard_map/ppermute | solution.py:590
  58.2 0.0 copy-done.3
  58.2 1.9 %collective-permute-start.1 = (f32[4,512,128]{2,1,0:T(8,128)S(1)}, f32[4,512,128]{2,1,0:T(8,128)S(1)}, u32[]{:S(2)}, u32[]{:S(2)}) collective-permute-start(f32[4,512,128]{2,1,0:T(8,128)S(1)} %copy-done.3), channel_id=1, source_target_pairs={{1,0},{2,1},{3,2},{4,3},{5,4},{6,5},{7,6},{9,8},{10,9},{11,10},{12... | collective-permute-start | bytes 3145736 | tf_op jit(solution)/shard_map/ppermute | solution.py:588
  60.2 0.8 slice.10
  61.0 0.8 slice.11
  61.9 0.7 maximum_convert_fusion.table_ref
  62.5 6.1 %patch_windows.2.refs_2_ = f32[16,144,384]{2,1,0:T(8,128)} custom-call(s32[16,24]{1,0:T(8,128)} %maximum_convert_fusion.table_ref, f32[4,512,128]{2,1,0:T(8,128)} %get-tuple-element.14.refs_0_, f32[4,512,128]{2,1,0:T(8,128)} %get-tuple-element.13.refs_1_), custom_call_target="tpu_custom_call" | custom-call | bytes 12582912 | tf_op jit(solution)/shard_map/patch_windows/pallas_call | solution.py:253
  68.7 1.6 collective-permute-done.refs_0_
  70.3 0.0 copy-start.4
  70.3 4.4 %collective-permute-done.1.refs_1_ = f32[4,512,128]{2,1,0:T(8,128)S(1)} collective-permute-done((f32[4,512,128]{2,1,0:T(8,128)S(1)}, f32[4,512,128]{2,1,0:T(8,128)S(1)}, u32[]{:S(2)}, u32[]{:S(2)}) %collective-permute-start.1) | collective-permute-done | bytes 1048608 | tf_op jit(solution)/shard_map/ppermute | solution.py:588
  74.7 0.0 copy-done.4
  74.7 0.0 copy-start.5
  74.7 1.0 copy-done.5
  75.7 5.4 %patch_windows.3 = f32[16,144,384]{2,1,0:T(8,128)} custom-call(s32[16,24]{1,0:T(8,128)} %maximum_convert_fusion.table_ref, f32[4,512,128]{2,1,0:T(8,128)} %copy-done.4, f32[4,512,128]{2,1,0:T(8,128)} %copy-done.5, f32[16,144,384]{2,1,0:T(8,128)} %patch_windows.2.refs_2_), custom_call_target="tpu_custom_call", output_to_operand_aliasing={{}: (3, {})} | custom-call | bytes 6291456 | tf_op jit(solution)/shard_map/patch_windows/pallas_call | solution.py:253
  81.0 0.0 copy-start.7
  81.0 0.0 copy-start
  81.0 0.0 all-to-all-done.1.low_ref.high_ref
  81.1 0.0 copy-start.2
  81.1 1.3 copy-done.2
  82.4 6.7 %all-to-all-start.2 = ((f32[16,144,384]{2,1,0:T(8,128)}), f32[16,144,384]{2,1,0:T(8,128)}, u32[]{:S(2)}, u32[]{:S(2)}) async-start(f32[16,144,384]{2,1,0:T(8,128)} %patch_windows.3), calls=%async_computation.2 | async-start | bytes 7077888 | tf_op jit(solution)/shard_map/all_to_all | solution.py:567
  89.0 0.0 copy-done.7
  89.1 0.0 copy-done
  89.1 0.6 gather_fusion
  89.7 0.1 broadcast_in_dim.2
  89.8 0.6 reshape_reshape.3.later_ref
  90.4 3.9 %join_rows.1 = f32[32,32,512]{2,1,0:T(8,128)} custom-call(f32[16,256,128]{2,1,0:T(8,128)} %copy-done.2, f32[16,256,128]{2,1,0:T(8,128)} %copy-done.2), custom_call_target="tpu_custom_call" | custom-call | bytes 8388608 | tf_op jit(solution)/shard_map/join_rows/pallas_call | solution.py:123
  94.3 47.3 %all-to-all-done.2.half_ref = f32[16,144,384]{2,1,0:T(8,128)} async-done(((f32[16,144,384]{2,1,0:T(8,128)}), f32[16,144,384]{2,1,0:T(8,128)}, u32[]{:S(2)}, u32[]{:S(2)}) %all-to-all-start.2) | async-done | bytes 3538976 | tf_op jit(solution)/shard_map/all_to_all | solution.py:567
  141.6 21.0 %solve_patches.1 = f32[8,48,2304]{2,1,0:T(8,128)} custom-call(f32[16,144,384]{2,1,0:T(8,128)} %all-to-all-done.2.half_ref, s32[1,384]{1,0:T(1,128)} %reshape_reshape.3.later_ref), custom_call_target="tpu_custom_call" | custom-call | flops 53084160 | bytes 33554432 | tf_op jit(solution)/shard_map/solve_patches/pallas_call | solution.py:534
  (3 shorter events, 0.0 us)
Async XLA Ops:
  4.3 6.4 %copy-start.6 = (f32[512]{0:T(512)S(1)}, f32[512]{0:T(512)}, u32[]{:S(2)}) copy-start(f32[512]{0:T(512)} %param.6) | copy-start | bytes 6148
  4.3 32.0 %all-to-all-start = ((f32[16,264,128]{2,1,0:T(8,128)}), f32[16,264,128]{2,1,0:T(8,128)S(1)}, u32[]{:S(2)}, u32[]{:S(2)}) async-start(f32[16,264,128]{2,1,0:T(8,128)} %split_rows.1), calls=%async_computation | async-start | bytes 4325376 | tf_op jit(solution)/shard_map/all_to_all | solution.py:567
  36.3 1.3 copy-start.1
  44.8 13.4 %copy-start.3 = (f32[4,512,128]{2,1,0:T(8,128)S(1)}, f32[4,512,128]{2,1,0:T(8,128)}, u32[]{:S(2)}) copy-start(f32[4,512,128]{2,1,0:T(8,128)} %get-tuple-element.14.refs_0_) | copy-start | bytes 3145732
  44.8 36.2 %all-to-all-start.1 = ((f32[16,256,128]{2,1,0:T(8,128)}), f32[16,256,128]{2,1,0:T(8,128)S(1)}, u32[]{:S(2)}, u32[]{:S(2)}) async-start(f32[16,256,128]{2,1,0:T(8,128)} %get-tuple-element.15), calls=%async_computation.1 | async-start | bytes 4194304 | tf_op jit(solution)/shard_map/all_to_all | solution.py:567
  51.9 18.4 %collective-permute-start = (f32[4,512,128]{2,1,0:T(8,128)}, f32[4,512,128]{2,1,0:T(8,128)S(1)}, u32[]{:S(2)}, u32[]{:S(2)}) collective-permute-start(f32[4,512,128]{2,1,0:T(8,128)} %get-tuple-element.13.refs_1_), channel_id=1, source_target_pairs={{0,1},{1,2},{2,3},{3,4},{4,5},{5,6},{6,7},{8,9},{9,10},{10,11},{11... | collective-permute-start | bytes 3145736 | tf_op jit(solution)/shard_map/ppermute | solution.py:590
  58.2 16.4 %collective-permute-start.1 = (f32[4,512,128]{2,1,0:T(8,128)S(1)}, f32[4,512,128]{2,1,0:T(8,128)S(1)}, u32[]{:S(2)}, u32[]{:S(2)}) collective-permute-start(f32[4,512,128]{2,1,0:T(8,128)S(1)} %copy-done.3), channel_id=1, source_target_pairs={{1,0},{2,1},{3,2},{4,3},{5,4},{6,5},{7,6},{9,8},{10,9},{11,10},{12... | collective-permute-start | bytes 3145736 | tf_op jit(solution)/shard_map/ppermute | solution.py:588
  70.3 4.4 %copy-start.4 = (f32[4,512,128]{2,1,0:T(8,128)}, f32[4,512,128]{2,1,0:T(8,128)S(1)}, u32[]{:S(2)}) copy-start(f32[4,512,128]{2,1,0:T(8,128)S(1)} %collective-permute-done.refs_0_) | copy-start | bytes 3145732
  74.7 1.0 copy-start.5
  81.0 8.0 %copy-start.7 = (s32[1,1,8]{2,1,0:T(1,128)S(1)}, s32[1,1,8]{2,1,0:T(1,128)}, u32[]{:S(2)}) copy-start(s32[1,1,8]{2,1,0:T(1,128)} %param.8) | copy-start | bytes 100
  81.0 8.0 %copy-start = (s32[16,24]{1,0:T(8,128)S(1)}, s32[16,24]{1,0:T(8,128)}, u32[]{:S(2)}) copy-start(s32[16,24]{1,0:T(8,128)} %maximum_convert_fusion.table_ref) | copy-start | bytes 4612
  81.1 1.3 copy-start.2
  82.4 59.3 %all-to-all-start.2 = ((f32[16,144,384]{2,1,0:T(8,128)}), f32[16,144,384]{2,1,0:T(8,128)}, u32[]{:S(2)}, u32[]{:S(2)}) async-start(f32[16,144,384]{2,1,0:T(8,128)} %patch_windows.3), calls=%async_computation.2 | async-start | bytes 7077888 | tf_op jit(solution)/shard_map/all_to_all | solution.py:567

commit v5 on v4

--- a/solution.py
+++ b/solution.py
@@ -24,13 +24,13 @@
 TILES = NZ // SIDE
 ROWS = 2 * TILES * CX
 OWNERS = 4
+UNROLL = 2
 TINY = 1e-06
 F32 = jnp.float32
-VMEM_LIMIT = 56 * 1024 * 1024
-
-
-def params():
-    return pltpu.CompilerParams(vmem_limit_bytes=VMEM_LIMIT)
+
+
+def params(mebibytes):
+    return pltpu.CompilerParams(vmem_limit_bytes=mebibytes * 1024 * 1024)
 
 
 def full(shape):
@@ -104,7 +104,7 @@
             pltpu.VMEM((WIDE, ROWS + 8, SIDE), F32),
             pltpu.SemaphoreType.DMA((3, TILES)),
         ],
-        compiler_params=params(),
+        compiler_params=params(56),
         cost_estimate=pl.CostEstimate(flops=0, bytes_accessed=8 << 20, transcendentals=0),
         name="split_rows",
     )(block, send, source)
@@ -129,7 +129,7 @@
         ],
         out_specs=pl.BlockSpec((CX, CY, SIDE), lambda j: (0, 0, j)),
         out_shape=full((CX, CY, NZ)),
-        compiler_params=params(),
+        compiler_params=params(12),
         cost_estimate=pl.CostEstimate(flops=0, bytes_accessed=8 << 20, transcendentals=0),
         name="join_rows",
     )(parts, parts)
@@ -146,14 +146,13 @@
     return pl.pallas_call(
         pair_kernel,
         out_shape=[jax.ShapeDtypeStruct((NX, NX), jnp.bfloat16)] * 2,
-        compiler_params=params(),
+        compiler_params=params(12),
         cost_estimate=pl.CostEstimate(flops=0, bytes_accessed=2 << 20, transcendentals=0),
         name="bf16_pair",
     )(matrix)
 
 
-def filter_kernel(high_ref, low_ref, in_ref, *refs):
-    parts_ref, plane_ref = refs[-2:]
+def filter_kernel(high_ref, low_ref, in_ref, parts_ref, first_ref, second_ref):
     lines = jnp.concatenate(
         [in_ref[:, 0:CX, :].reshape(NX, SIDE), in_ref[:, CX:, :].reshape(NX, SIDE)], axis=1
     )
@@ -162,31 +161,37 @@
     dot = lambda a, b: jnp.dot(a, b, preferred_element_type=F32)
     small = dot(high_ref[...], low) + dot(low_ref[...], high)
     value = jnp.exp(dot(high_ref[...], high) + small)
+    sides = [value[:, :SIDE], value[:, SIDE:]]
     for k in range(2):
-        side = value[:, k * SIDE:(k + 1) * SIDE]
-        parts_ref[:, k * CX:(k + 1) * CX, :] = side.reshape(WIDE, CX, SIDE)
-        plane_ref[k] = 0.5 * side
-
-
-def filter_exp(t, pair, lines, *others):
+        parts_ref[:, k * CX:(k + 1) * CX, :] = sides[k].reshape(WIDE, CX, SIDE)
+
+    def plane(ref):
+        for k in range(2):
+            ref[k] = 0.5 * sides[k]
+
+    pl.when(pl.program_id(0) < 2)(lambda: plane(first_ref))
+    pl.when(pl.program_id(0) >= 2)(lambda: plane(second_ref))
+
+
+def filter_exp(pair, lines):
     whole = pl.BlockSpec((NX, NX), lambda i: (0, 0))
+    block = pl.BlockSpec((WIDE, 2 * CX, SIDE), lambda i: (0, i, 0))
     return pl.pallas_call(
         filter_kernel,
-        grid=(2,),
-        in_specs=[whole, whole, pl.BlockSpec((WIDE, 2 * CX, SIDE), lambda i: (0, 2 * t + i, 0))]
-        + [pl.BlockSpec(memory_space=pl.ANY)] * len(others),
+        grid=(4,),
+        in_specs=[whole, whole, block],
         out_specs=[
-            pl.BlockSpec((WIDE, 2 * CX, SIDE), lambda i: (0, 2 * t + i, 0)),
-            pl.BlockSpec((2, NX, SIDE), lambda i: (i, 0, 0)),
+            block,
+            pl.BlockSpec((2, NX, SIDE), lambda i: (jnp.minimum(i, 1), 0, 0)),
+            pl.BlockSpec((2, NX, SIDE), lambda i: (jnp.maximum(i - 2, 0), 0, 0)),
         ],
-        out_shape=[full((WIDE, ROWS, SIDE)), full((TILES, NX, SIDE))],
-        input_output_aliases={3: 0} if others else {},
-        compiler_params=params(),
+        out_shape=[full((WIDE, ROWS, SIDE)), full((TILES, NX, SIDE)), full((TILES, NX, SIDE))],
+        compiler_params=params(20),
         cost_estimate=pl.CostEstimate(
-            flops=6 * NX * NX * NZ, bytes_accessed=4 << 20, transcendentals=NX * NZ
+            flops=12 * NX * NX * NZ, bytes_accessed=8 << 20, transcendentals=2 * NX * NZ
         ),
         name="filter_exp",
-    )(*pair, lines, *others)
+    )(*pair, lines)
 
 
 def window_kernel(slots, table_ref, *refs):
@@ -244,7 +249,7 @@
                 out_ref[k, t * EDGE:(t + 1) * EDGE, q * SIDE:(q + 1) * SIDE] = tiles[q]
         return 0
 
-    lax.fori_loop(0, OWNERS, one_owner, 0)
+    lax.fori_loop(0, OWNERS, one_owner, 0, unroll=UNROLL)
 
 
 def windows(table, planes, *others):
@@ -264,7 +269,7 @@
         ),
         out_shape=full((WIDE, TAPS * EDGE, LANES)),
         input_output_aliases={3: 0} if others else {},
-        compiler_params=params(),
+        compiler_params=params(16),
         cost_estimate=pl.CostEstimate(
             flops=0, bytes_accessed=slots * (6 << 20), transcendentals=0
         ),
@@ -273,6 +278,7 @@
 
 
 STRIPS = EDGE // 8
+SLABS = 3
 GROUPS = EDGE // 8
 PIECES = [(i, q) for i in range(STRIPS) for q in range(3)]
 
@@ -415,7 +421,7 @@
                 + ((y_up + y_down) + (z_up + z_down))
             )
             face_x[y, *to] = across
-            face_y[y, *to] = here + y_up
+            face_y[y + 1, *to] = here + y_up
             face_z[y, *to] = jnp.where(z_high[q], 0.0, deep)
             first[y, *to] = v
             image[y, *to] = deep * (up_up[i, q] - up_down[i, q]) + (here + z_down) * (
@@ -424,10 +430,10 @@
             rr[q] = rr[q] + v * v
         return tuple(rr)
 
-    rr = lax.fori_loop(0, EDGE, faces_of, nothing)
+    rr = lax.fori_loop(0, EDGE, faces_of, nothing, unroll=3)
     for at in PIECES:
-        face_y[EDGE - 1, *piece(*at)] = none
-        ready[0, *piece(*at)] = none
+        face_y[0, *piece(*at)] = none
+        face_y[EDGE, *piece(*at)] = none
     rr = patch_total(rr)
 
     def image_of(y, total):
@@ -438,16 +444,15 @@
         from_x = below_x({at: across[at] * v[at] for at in PIECES})
         for i, q in PIECES:
             to = piece(i, q)
-            along = face_y[y, *to]
             couple = across[i, q] * v_up[i, q] + from_x[i, q]
-            couple = couple + (along * first[y + 1, *to] + ready[0, *to])
+            couple = couple + face_y[y + 1, *to] * first[y + 1, *to]
+            couple = couple + face_y[y, *to] * first[jnp.maximum(y - 1, 0), *to]
             result = heavy[y, *to] * v[i, q] - (couple + image[y, *to])
-            ready[0, *to] = along * v[i, q]
             image[y, *to] = result
             total[q] = total[q] + v[i, q] * result
         return tuple(total)
 
-    alpha = divide(rr, patch_total(lax.fori_loop(0, EDGE, image_of, nothing)))
+    alpha = divide(rr, patch_total(lax.fori_loop(0, EDGE, image_of, nothing, unroll=3)))
 
     def residual_of(y, total):
         total = list(total)
@@ -456,7 +461,7 @@
             total[q] = total[q] + left * left
         return tuple(total)
 
-    new = patch_total(lax.fori_loop(0, EDGE, residual_of, nothing))
+    new = patch_total(lax.fori_loop(0, EDGE, residual_of, nothing, unroll=4))
     beta = divide(new, rr)
 
     def direction(y, i, q):
@@ -466,56 +471,74 @@
     for at in PIECES:
         ready[0, *piece(*at)] = direction(0, *at)
 
-    def energy_of(y, total):
+    def energy_of(step, total):
         total = list(total)
         v = load(ready, 0)
-        v_up = above_x(v)
-        for i in range(STRIPS):
-            ups = above_z(strip(v, i))
-            for q in range(3):
-                to = piece(i, q)
-                y_up = direction(y + 1, i, q)
-                ready[0, *to] = y_up
-                couple = face_x[y, *to] * v_up[i, q]
-                couple = couple + face_y[y, *to] * y_up
-                couple = couple + face_z[y, *to] * ups[q]
-                total[q] = total[q] + v[i, q] * (heavy[y, *to] * v[i, q] - 2.0 * couple)
+        for k in range(SLABS):
+            y = step * SLABS + k
+            v_up = above_x(v)
+            v_next = {at: direction(y + 1, *at) for at in PIECES}
+            for i in range(STRIPS):
+                ups = above_z(strip(v, i))
+                for q in range(3):
+                    to = piece(i, q)
+                    couple = face_x[y, *to] * v_up[i, q]
+                    couple = couple + face_y[y + 1, *to] * v_next[i, q]
+                    couple = couple + face_z[y, *to] * ups[q]
+                    total[q] = total[q] + v[i, q] * (heavy[y, *to] * v[i, q] - 2.0 * couple)
+            v = v_next
+        for at in PIECES:
+            ready[0, *piece(*at)] = v[at]
         return tuple(total)
 
-    alpha_next = divide(new, patch_total(lax.fori_loop(0, EDGE, energy_of, nothing)))
+    energy = lax.fori_loop(0, EDGE // SLABS, energy_of, nothing)
+    alpha_next = divide(new, patch_total(energy))
     on_first = [alpha[q] + alpha_next[q] * (1.0 + beta[q]) for q in range(3)]
     on_image = [-(alpha_next[q] * alpha[q]) for q in range(3)]
 
     ends = [lane < end for end in (48, 96, 16, 64, 112, 32, 80)]
+
+    def gather(c):
+        return (
+            jnp.where(ends[0], c[0][0], jnp.where(ends[1], c[1][0], c[2][0])),
+            jnp.where(
+                ends[2],
+                c[2][1],
+                jnp.where(ends[3], c[3][1], jnp.where(ends[4], c[4][1], c[5][1])),
+            ),
+            jnp.where(ends[5], c[5][2], jnp.where(ends[6], c[6][2], c[7][2])),
+        )
+
     departures = []
     for group in range(GROUPS):
 
         def correct(i, _):
-            rows = pl.ds(8*i,8)
-            chunks = []
+            rows = pl.ds(pl.multiple_of(8 * i, 8), 8)
+            lines = []
             for j in range(8):
-                line = []
-                for q in range(3):
-                    at = (8 * group + j, rows, pl.ds(SIDE * q, SIDE))
-                    line.append(on_first[q] * first[*at] + on_image[q] * image[*at])
-                a, b, c = line
-                cut = [a, a, jnp.where(ends[1], b, a), b, b, jnp.where(ends[4], c, b), c, c]
-                chunks.append(cut)
+                y = 8 * group + j
+                lines.append([
+                    on_first[q] * first[y, rows, pl.ds(SIDE * q, SIDE)]
+                    + on_image[q] * image[y, rows, pl.ds(SIDE * q, SIDE)]
+                    for q in range(3)
+                ])
+            turned = []
+            for k in range(8):
+                a, b, c = gather([lines[(p + k) % 8] for p in range(8)])
+                far, near = divmod(EDGE * k, SIDE)
+                r = [pltpu.roll(v, near, 1) if near else v for v in (a, b, c)]
+                r = [r[(q - far) % 3] for q in range(3)]
+                before = [r[2], r[0], r[1]]
+                if near:
+                    r = [jnp.where(lane < near, before[q], r[q]) for q in range(3)]
+                turned.append(r)
             for p in range(PATCH_DEV):
-                c = []
-                for j in range(8):
-                    turn = (EDGE * (j - p)) % SIDE
-                    c.append(pltpu.roll(chunks[j][p], turn, 1) if turn else chunks[j][p])
-                tiles = (
-                    jnp.where(ends[0], c[0], jnp.where(ends[1], c[1], c[2])),
-                    jnp.where(ends[2], c[2], jnp.where(ends[3], c[3], jnp.where(ends[4], c[4], c[5]))),
-                    jnp.where(ends[5], c[5], jnp.where(ends[6], c[6], c[7])),
-                )
+                tiles = gather([turned[(j - p) % 8] for j in range(8)])
                 for q in range(3):
                     heavy[8 * group + p, rows, pl.ds(SIDE * q, SIDE)] = tiles[q]
             return 0
 
-        [correct(i,0) for i in range(STRIPS)]
+        lax.fori_loop(0, STRIPS, correct, 0, unroll=True)
         departures.append(
             pltpu.make_async_copy(
                 heavy.at[pl.ds(8 * group, PATCH_DEV)],
@@ -542,13 +565,13 @@
             longer,
             cube,
             cube,
-            cube,
+            longer,
             cube,
             pltpu.VMEM((1, EDGE, LANES), F32),
             pltpu.SemaphoreType.DMA((TAPS,)),
             pltpu.SemaphoreType.DMA((GROUPS,)),
         ],
-        compiler_params=params(),
+        compiler_params=params(40),
         cost_estimate=pl.CostEstimate(
             flops=60 * EDGE**3 * PATCH_DEV, bytes_accessed=32 << 20, transcendentals=0
         ),
@@ -584,9 +607,8 @@
     forward = [(i, i + 1) for i in range(count - 1)]
     backward = [(i + 1, i) for i in range(count - 1)]
     pair = bf16_pair(matrix)
-    parts, low = filter_exp(0, pair, lines)
+    parts, low, high = filter_exp(pair, lines)
     above = lax.ppermute(low, "mid", backward)
-    parts, high = filter_exp(1, pair, lines, parts)
     below = lax.ppermute(high, "mid", forward)
     back = swap(parts)
     outgoing = windows(table, (low, high))

time: 163 us -> 151 us (0.926)
  the two profiles are of different devices: /device:TPU:117 before, /device:TPU:0 now
where the time goes in v5:
time: 151 us; the launch traced here: 150 us
  waiting for transfers between devices  81 us (54%)
  Pallas kernels  33.4 us (22%)
  starting transfers between devices  18.9 us (13%)
  local copies, waits for them, and re-layouts  9.68 us (6%)
  matrix products  6.16 us (4%)
    all_to_all x3, waiting for transfers between devices, on_device(): swap = lambda v: lax.all_to_all(v, 'wide', split_axis=0, concat_axis=0)  81 us
    all_to_all x3, starting transfers between devices, on_device(): swap = lambda v: lax.all_to_all(v, 'wide', split_axis=0, concat_axis=0)  16.2 us
    pallas_call x1, Pallas kernels, solve(): pl.pallas_call(solve_kernel, in_specs=[pl.BlockSpec(memory_space=pl.ANY),...  15.5 us
    pallas_call x2, Pallas kernels, windows(): pl.pallas_call(functools.partial(window_kernel, slots), grid_spec=pltpu.P...  7.75 us
    unnamed x18, local copies, waits for them, and re-layouts  7.19 us
    dot_general x1, matrix products, on_device(): lax.dot_general(waves, waves * weights, (((0,), (0,)), ((), ())), precisi...  6.16 us
    pallas_call x1, Pallas kernels, filter_exp(): pl.pallas_call(filter_kernel, grid=(4,), in_specs=[whole, whole, block],...  4.15 us
    pallas_call x1, Pallas kernels, split_rows(): pl.pallas_call(split_kernel, grid=(TILES,), in_specs=[pl.BlockSpec((CX, C...  3.69 us
  transfers between devices with their start and end apart: 5, of which 3 were waited for; matrix products, arithmetic and copies ran while one was open for 6% of the time, Pallas kernels for 7%

profile of v5, /device:TPU:0, one launch (start us, length us, event | category | flops | bytes accessed | tf_op | source)
XLA Modules:
  0.0 150.0 jit_solution(3123226395206866842)
XLA Ops:
  0.6 3.7 %split_rows.1 = f32[16,264,128]{2,1,0:T(8,128)} custom-call(f32[32,32,512]{2,1,0:T(8,128)} %in_ref.1, s32[1,16]{1,0:T(1,128)} %bitcast.18, s32[1,8]{1,0:T(1,128)} %bitcast.19), custom_call_target="tpu_custom_call" | custom-call | bytes 8388608 | tf_op jit(solution)/shard_map/split_rows/pallas_call | solution.py:93
  4.3 0.0 copy-start.7
  4.3 8.0 %all-to-all-start = ((f32[16,264,128]{2,1,0:T(8,128)}), f32[16,264,128]{2,1,0:T(8,128)}, u32[]{:S(2)}, u32[]{:S(2)}) async-start(f32[16,264,128]{2,1,0:T(8,128)} %split_rows.1), calls=%async_computation | async-start | bytes 4325376 | tf_op jit(solution)/shard_map/all_to_all | solution.py:590
  12.4 0.0 copy-done.7
  12.4 6.2 %fusion.in_ref = f32[512,512]{1,0:T(8,128)S(1)} fusion(f32[1024,512]{1,0:T(8,128)} %constant.22.clone, f32[1024]{0:T(1024)S(1)} %maximum_multiply_fusion), kind=kOutput, calls=%fused_computation.1 | convolution fusion | flops 3221749760 | bytes 3149824 | tf_op jit(solution)/shard_map/dot_general | solution.py:599
  18.6 0.1 bf16_pair.1
  18.7 0.0 copy-start.3
  18.7 0.8 copy-done.3
  19.5 0.0 copy-start.5
  19.5 0.8 copy-done.5
  20.3 23.3 %all-to-all-done.in_ref = f32[16,264,128]{2,1,0:T(8,128)} async-done(((f32[16,264,128]{2,1,0:T(8,128)}), f32[16,264,128]{2,1,0:T(8,128)}, u32[]{:S(2)}, u32[]{:S(2)}) %all-to-all-start) | async-done | bytes 2162720 | tf_op jit(solution)/shard_map/all_to_all | solution.py:590
  43.6 0.0 copy-start.4
  43.6 1.0 copy-done.4
  44.7 0.0 copy-start.6
  44.7 1.0 copy-done.6
  45.7 4.2 %filter_exp.1 = (f32[16,256,128]{2,1,0:T(8,128)S(1)}, f32[4,512,128]{2,1,0:T(8,128)S(1)}, f32[4,512,128]{2,1,0:T(8,128)S(1)}) custom-call(bf16[512,512]{1,0:T(8,128)(2,1)S(1)} %copy-done.4, bf16[512,512]{1,0:T(8,128)(2,1)S(1)} %copy-done.6, f32[16,264,128]{2,1,0:T(8,128)} %all-to-all-done.in_ref), custom_call_target="tpu_custom_call" | custom-call | flops 1610612736 | bytes 8388608 | tf_op jit(solution)/shard_map/filter_exp/pallas_call | solution.py:179
  49.9 0.0 copy-start
  49.9 1.3 copy-done
  51.2 0.0 copy-start.1
  51.2 1.0 copy-done.1
  52.2 3.7 %all-to-all-start.1 = ((f32[16,256,128]{2,1,0:T(8,128)}), f32[16,256,128]{2,1,0:T(8,128)S(1)}, u32[]{:S(2)}, u32[]{:S(2)}) async-start(f32[16,256,128]{2,1,0:T(8,128)} %copy-done), calls=%async_computation.1 | async-start | bytes 4194304 | tf_op jit(solution)/shard_map/all_to_all | solution.py:590
  55.9 1.4 collective-permute-start
  57.3 1.3 collective-permute-start.1
  58.6 0.8 slice.10
  59.4 0.8 slice.11
  60.3 0.1 maximum_convert_fusion.table_ref
  60.3 0.0 copy-start.2
  60.3 1.2 copy-done.2
  61.6 4.3 %patch_windows.2.refs_2_ = f32[16,144,384]{2,1,0:T(8,128)} custom-call(s32[16,24]{1,0:T(8,128)S(1)} %maximum_convert_fusion.table_ref, f32[4,512,128]{2,1,0:T(8,128)S(1)} %get-tuple-element.12.refs_0_, f32[4,512,128]{2,1,0:T(8,128)S(1)} %copy-done.2), custom_call_target="tpu_custom_call" | custom-call | bytes 12582912 | tf_op jit(solution)/shard_map/patch_windows/pallas_call | solution.py:258
  65.8 0.0 collective-permute-done.refs_0_
  65.8 0.0 collective-permute-done.1.refs_1_
  65.8 3.5 %patch_windows.3 = f32[16,144,384]{2,1,0:T(8,128)} custom-call(s32[16,24]{1,0:T(8,128)S(1)} %maximum_convert_fusion.table_ref, f32[4,512,128]{2,1,0:T(8,128)S(1)} %collective-permute-done.refs_0_, f32[4,512,128]{2,1,0:T(8,128)S(1)} %collective-permute-done.1.refs_1_, f32[16,144,384]{2,1,0:T(8,128)} %patch_windows.2.refs_2_), custom_call_target="tpu_custom_call", output_to_operand_aliasing={{}: (3, {})} | custom-call | bytes 6291456 | tf_op jit(solution)/shard_map/patch_windows/pallas_call | solution.py:258
  69.4 0.0 copy-start.8
  69.4 14.2 %all-to-all-done.1.low_ref.high_ref = f32[16,256,128]{2,1,0:T(8,128)S(1)} async-done(((f32[16,256,128]{2,1,0:T(8,128)}), f32[16,256,128]{2,1,0:T(8,128)S(1)}, u32[]{:S(2)}, u32[]{:S(2)}) %all-to-all-start.1) | async-done | bytes 2097184 | tf_op jit(solution)/shard_map/all_to_all | solution.py:590
  83.6 4.5 %all-to-all-start.2 = ((f32[16,144,384]{2,1,0:T(8,128)}), f32[16,144,384]{2,1,0:T(8,128)}, u32[]{:S(2)}, u32[]{:S(2)}) async-start(f32[16,144,384]{2,1,0:T(8,128)} %patch_windows.3), calls=%async_computation.2 | async-start | bytes 7077888 | tf_op jit(solution)/shard_map/all_to_all | solution.py:590
  88.1 0.0 copy-done.8
  88.1 0.6 gather_fusion
  88.8 0.1 broadcast_in_dim.2
  88.8 0.1 reshape_reshape.3.later_ref
  88.9 2.1 %join_rows.1 = f32[32,32,512]{2,1,0:T(8,128)} custom-call(f32[16,256,128]{2,1,0:T(8,128)S(1)} %all-to-all-done.1.low_ref.high_ref, f32[16,256,128]{2,1,0:T(8,128)S(1)} %all-to-all-done.1.low_ref.high_ref), custom_call_target="tpu_custom_call" | custom-call | bytes 8388608 | tf_op jit(solution)/shard_map/join_rows/pallas_call | solution.py:123
  91.0 43.4 %all-to-all-done.2.half_ref = f32[16,144,384]{2,1,0:T(8,128)} async-done(((f32[16,144,384]{2,1,0:T(8,128)}), f32[16,144,384]{2,1,0:T(8,128)}, u32[]{:S(2)}, u32[]{:S(2)}) %all-to-all-start.2) | async-done | bytes 3538976 | tf_op jit(solution)/shard_map/all_to_all | solution.py:590
  134.5 15.5 %solve_patches.1 = f32[8,48,2304]{2,1,0:T(8,128)} custom-call(f32[16,144,384]{2,1,0:T(8,128)} %all-to-all-done.2.half_ref, s32[1,384]{1,0:T(1,128)S(1)} %reshape_reshape.3.later_ref), custom_call_target="tpu_custom_call" | custom-call | flops 53084160 | bytes 33554432 | tf_op jit(solution)/shard_map/solve_patches/pallas_call | solution.py:557
  (3 shorter events, 0.0 us)
Async XLA Ops:
  4.3 8.0 %copy-start.7 = (f32[512]{0:T(512)S(1)}, f32[512]{0:T(512)}, u32[]{:S(2)}) copy-start(f32[512]{0:T(512)} %param.6) | copy-start | bytes 6148
  4.3 39.3 %all-to-all-start = ((f32[16,264,128]{2,1,0:T(8,128)}), f32[16,264,128]{2,1,0:T(8,128)}, u32[]{:S(2)}, u32[]{:S(2)}) async-start(f32[16,264,128]{2,1,0:T(8,128)} %split_rows.1), calls=%async_computation | async-start | bytes 4325376 | tf_op jit(solution)/shard_map/all_to_all | solution.py:590
  18.7 0.8 copy-start.3
  19.5 0.8 copy-start.5
  43.6 1.0 copy-start.4
  44.7 1.0 copy-start.6
  49.9 1.3 copy-start
  51.2 1.0 copy-start.1
  52.2 31.4 %all-to-all-start.1 = ((f32[16,256,128]{2,1,0:T(8,128)}), f32[16,256,128]{2,1,0:T(8,128)S(1)}, u32[]{:S(2)}, u32[]{:S(2)}) async-start(f32[16,256,128]{2,1,0:T(8,128)} %copy-done), calls=%async_computation.1 | async-start | bytes 4194304 | tf_op jit(solution)/shard_map/all_to_all | solution.py:590
  55.9 9.9 %collective-permute-start = (f32[4,512,128]{2,1,0:T(8,128)}, f32[4,512,128]{2,1,0:T(8,128)S(1)}, u32[]{:S(2)}, u32[]{:S(2)}) collective-permute-start(f32[4,512,128]{2,1,0:T(8,128)} %copy-done.1), channel_id=1, source_target_pairs={{0,1},{1,2},{2,3},{3,4},{4,5},{5,6},{6,7},{8,9},{9,10},{10,11},{11... | collective-permute-start | bytes 3145736 | tf_op jit(solution)/shard_map/ppermute | solution.py:612
  57.3 8.6 %collective-permute-start.1 = (f32[4,512,128]{2,1,0:T(8,128)S(1)}, f32[4,512,128]{2,1,0:T(8,128)S(1)}, u32[]{:S(2)}, u32[]{:S(2)}) collective-permute-start(f32[4,512,128]{2,1,0:T(8,128)S(1)} %get-tuple-element.12.refs_0_), channel_id=1, source_target_pairs={{1,0},{2,1},{3,2},{4,3},{5,4},{6,5},{7,6},{9,8},{10,9},{11,10},{12... | collective-permute-start | bytes 3145736 | tf_op jit(solution)/shard_map/ppermute | solution.py:611
  60.3 1.2 copy-start.2
  69.4 18.7 %copy-start.8 = (s32[1,1,8]{2,1,0:T(1,128)S(1)}, s32[1,1,8]{2,1,0:T(1,128)}, u32[]{:S(2)}) copy-start(s32[1,1,8]{2,1,0:T(1,128)} %param.8) | copy-start | bytes 100
  83.6 50.9 %all-to-all-start.2 = ((f32[16,144,384]{2,1,0:T(8,128)}), f32[16,144,384]{2,1,0:T(8,128)}, u32[]{:S(2)}, u32[]{:S(2)}) async-start(f32[16,144,384]{2,1,0:T(8,128)} %patch_windows.3), calls=%async_computation.2 | async-start | bytes 7077888 | tf_op jit(solution)/shard_map/all_to_all | solution.py:590

commit v6 on v5

--- a/solution.py
+++ b/solution.py
@@ -146,13 +146,15 @@
     return pl.pallas_call(
         pair_kernel,
         out_shape=[jax.ShapeDtypeStruct((NX, NX), jnp.bfloat16)] * 2,
-        compiler_params=params(12),
+        compiler_params=params(56),
         cost_estimate=pl.CostEstimate(flops=0, bytes_accessed=2 << 20, transcendentals=0),
         name="bf16_pair",
     )(matrix)
 
 
-def filter_kernel(high_ref, low_ref, in_ref, parts_ref, first_ref, second_ref):
+def filter_kernel(high_ref, low_ref, in_ref, extra_ref, parts_ref, first_ref, second_ref, table_ref):
+    for k in range(2):
+        table_ref[k] = extra_ref[:, k, :].astype(jnp.int32)
     lines = jnp.concatenate(
         [in_ref[:, 0:CX, :].reshape(NX, SIDE), in_ref[:, CX:, :].reshape(NX, SIDE)], axis=1
     )
@@ -179,19 +181,25 @@
     return pl.pallas_call(
         filter_kernel,
         grid=(4,),
-        in_specs=[whole, whole, block],
+        in_specs=[whole, whole, block, pl.BlockSpec((WIDE, 8, SIDE), lambda i: (0, ROWS // 8, 0))],
         out_specs=[
             block,
             pl.BlockSpec((2, NX, SIDE), lambda i: (jnp.minimum(i, 1), 0, 0)),
             pl.BlockSpec((2, NX, SIDE), lambda i: (jnp.maximum(i - 2, 0), 0, 0)),
+            pl.BlockSpec((2, WIDE, SIDE), lambda i: (0, 0, 0)),
         ],
-        out_shape=[full((WIDE, ROWS, SIDE)), full((TILES, NX, SIDE)), full((TILES, NX, SIDE))],
-        compiler_params=params(20),
+        out_shape=[
+            full((WIDE, ROWS, SIDE)),
+            full((TILES, NX, SIDE)),
+            full((TILES, NX, SIDE)),
+            jax.ShapeDtypeStruct((2, WIDE, SIDE), jnp.int32),
+        ],
+        compiler_params=params(56),
         cost_estimate=pl.CostEstimate(
             flops=12 * NX * NX * NZ, bytes_accessed=8 << 20, transcendentals=2 * NX * NZ
         ),
         name="filter_exp",
-    )(*pair, lines)
+    )(*pair, lines, lines)
 
 
 def window_kernel(slots, table_ref, *refs):
@@ -225,8 +233,8 @@
         owner = step * OWNERS + k
         places = []
         for p in range(PATCH_DEV):
-            source = table_ref[owner, WIDE + p]
-            core = jnp.maximum(table_ref[source, owner], 0)
+            source = table_ref[1, owner, p]
+            core = jnp.maximum(table_ref[0, source, owner], 0)
             x_at = source * CX + (core >> 6) * CORE
             z_at = (core & 31) * CORE + (SIDE - LAYER)
             offset = z_at & (SIDE - 1)
@@ -269,7 +277,7 @@
         ),
         out_shape=full((WIDE, TAPS * EDGE, LANES)),
         input_output_aliases={3: 0} if others else {},
-        compiler_params=params(16),
+        compiler_params=params(16 if others else 56),
         cost_estimate=pl.CostEstimate(
             flops=0, bytes_accessed=slots * (6 << 20), transcendentals=0
         ),
@@ -291,13 +299,19 @@
     half_ref, later_ref, out_ref, half, first, image, heavy, face_x, face_y, face_z, ready, arrive, leave
 ):
     arrivals = [
-        pltpu.make_async_copy(
-            half_ref.at[:, pl.ds(t * EDGE, EDGE), :], (heavy, face_x, face_y)[t].at[pl.ds(0, WIDE)], arrive.at[t]
-        )
-        for t in range(TAPS)
+        [
+            pltpu.make_async_copy(
+                half_ref.at[pl.ds(4 * g, 4), pl.ds(t * EDGE, EDGE), :],
+                (heavy, face_x, face_y)[t].at[pl.ds(4 * g, 4)],
+                arrive.at[g, t],
+            )
+            for t in range(TAPS)
+        ]
+        for g in range(WIDE // 4)
     ]
-    for copy in arrivals:
-        copy.start()
+    for group in arrivals:
+        for copy in group:
+            copy.start()
     none = jnp.zeros((8, SIDE), F32)
     for at in PIECES:
         half[0, *piece(*at)] = none
@@ -376,8 +390,6 @@
 
     nothing = (none, none, none)
 
-    for copy in arrivals:
-        copy.wait()
     in_order = [
         jnp.broadcast_to(later_ref[:, SIDE * q:SIDE * (q + 1)], (8, SIDE)) != 0 for q in range(3)
     ]
@@ -391,7 +403,10 @@
             half[1 + 2 * WIDE + w, *at] = jnp.where(in_order[q], c, b)
         return 0
 
-    lax.fori_loop(0, WIDE, arrange, 0)
+    for g, group in enumerate(arrivals):
+        for copy in group:
+            copy.wait()
+        lax.fori_loop(4 * g, 4 * g + 4, arrange, 0, unroll=2)
 
     def faces_of(y, rr):
         rr = list(rr)
@@ -568,7 +583,7 @@
             longer,
             cube,
             pltpu.VMEM((1, EDGE, LANES), F32),
-            pltpu.SemaphoreType.DMA((TAPS,)),
+            pltpu.SemaphoreType.DMA((WIDE // 4, TAPS)),
             pltpu.SemaphoreType.DMA((GROUPS,)),
         ],
         compiler_params=params(40),
@@ -591,9 +606,6 @@
     lines = swap(
         split_rows(noise, send_core.reshape(1, WIDE), recv_source.reshape(1, PATCH_DEV))
     )
-    table = jnp.concatenate(
-        [lines[:, ROWS, :WIDE], lines[:, ROWS + 1, :PATCH_DEV]], axis=1
-    ).astype(jnp.int32)
     waves = jnp.asarray(wave_tables())
     weights = jnp.concatenate([spectrum, spectrum])[:, None] / NX
     matrix = lax.dot_general(
@@ -607,7 +619,7 @@
     forward = [(i, i + 1) for i in range(count - 1)]
     backward = [(i + 1, i) for i in range(count - 1)]
     pair = bf16_pair(matrix)
-    parts, low, high = filter_exp(pair, lines)
+    parts, low, high, table = filter_exp(pair, lines)
     above = lax.ppermute(low, "mid", backward)
     below = lax.ppermute(high, "mid", forward)
     back = swap(parts)
@@ -616,7 +628,7 @@
     outgoing, back = lax.optimization_barrier((outgoing, back))
     incoming = swap(outgoing)
     coefficient = join_rows(back)
-    cores = table[recv_source.reshape(-1), lax.axis_index("wide")]
+    cores = table[0, recv_source.reshape(-1), lax.axis_index("wide")]
     later = jnp.repeat((cores >> 5) & 1, EDGE).reshape(1, LANES)
     solved = solve(incoming, later)
     return coefficient, solved.reshape(1, 1, PATCH_DEV, EDGE, EDGE * EDGE)

time: 151 us -> 154 us (1.020)
  the two profiles are of different devices: /device:TPU:0 before, /device:TPU:117 now
where the time goes in v6:
time: 154 us; the launch traced here: 153 us
  waiting for transfers between devices  76.2 us (49%)
  Pallas kernels  38.1 us (25%)
  starting transfers between devices  28.6 us (19%)
  matrix products  4.92 us (3%)
  local copies, waits for them, and re-layouts  4.61 us (3%)
    all_to_all x3, waiting for transfers between devices, on_device(): swap = lambda v: lax.all_to_all(v, 'wide', split_axis=0, concat_axis=0)  67.6 us
    all_to_all x3, starting transfers between devices, on_device(): swap = lambda v: lax.all_to_all(v, 'wide', split_axis=0, concat_axis=0)  20.3 us
    pallas_call x1, Pallas kernels, solve(): pl.pallas_call(solve_kernel, in_specs=[pl.BlockSpec(memory_space=pl.ANY),...  15.4 us
    pallas_call x2, Pallas kernels, windows(): pl.pallas_call(functools.partial(window_kernel, slots), grid_spec=pltpu.P...  8.65 us
    ppermute x1, starting transfers between devices, on_device(): below = lax.ppermute(high, 'mid', forward)  6.37 us
    pallas_call x1, Pallas kernels, filter_exp(): pl.pallas_call(filter_kernel, grid=(4,), in_specs=[whole, whole, block, p...  5.94 us
    dot_general x1, matrix products, on_device(): lax.dot_general(waves, waves * weights, (((0,), (0,)), ((), ())), precisi...  4.92 us
    ppermute x1, waiting for transfers between devices, on_device(): above = lax.ppermute(low, 'mid', backward)  4.38 us
  transfers between devices with their start and end apart: 5, of which 4 were waited for; matrix products, arithmetic and copies ran while one was open for 4% of the time, Pallas kernels for 9%

profile of v6, /device:TPU:117, one launch (start us, length us, event | category | flops | bytes accessed | tf_op | source)
XLA Modules:
  0.0 153.2 jit_solution(15887950968329087229)
XLA Ops:
  0.6 3.7 %split_rows.1 = f32[16,264,128]{2,1,0:T(8,128)} custom-call(f32[32,32,512]{2,1,0:T(8,128)} %in_ref.1, s32[1,16]{1,0:T(1,128)} %bitcast.9, s32[1,8]{1,0:T(1,128)} %bitcast.10), custom_call_target="tpu_custom_call" | custom-call | bytes 8388608 | tf_op jit(solution)/shard_map/split_rows/pallas_call | solution.py:93
  4.3 0.0 copy-start.5
  4.3 0.0 copy-start.3
  4.4 6.5 %all-to-all-start = ((f32[16,264,128]{2,1,0:T(8,128)}), f32[16,264,128]{2,1,0:T(8,128)}, u32[]{:S(2)}, u32[]{:S(2)}) async-start(f32[16,264,128]{2,1,0:T(8,128)} %split_rows.1), calls=%async_computation | async-start | bytes 4325376 | tf_op jit(solution)/shard_map/all_to_all | solution.py:605
  10.9 0.0 copy-done.5
  10.9 0.0 copy-done.3
  10.9 4.9 %fusion.in_ref = f32[512,512]{1,0:T(8,128)} fusion(f32[1024,512]{1,0:T(8,128)S(1)} %copy-done.3, f32[1024]{0:T(1024)S(1)} %maximum_multiply_fusion), kind=kOutput, calls=%fused_computation.1 | convolution fusion | flops 3221749760 | bytes 3149824 | tf_op jit(solution)/shard_map/dot_general | solution.py:611
  15.8 2.3 %bf16_pair.1 = (bf16[512,512]{1,0:T(8,128)(2,1)}, bf16[512,512]{1,0:T(8,128)(2,1)}) custom-call(f32[512,512]{1,0:T(8,128)} %fusion.in_ref), custom_call_target="tpu_custom_call" | custom-call | bytes 2097152 | tf_op jit(solution)/shard_map/bf16_pair/pallas_call | solution.py:146
  18.1 18.5 %all-to-all-done.in_ref.extra_ref = f32[16,264,128]{2,1,0:T(8,128)} async-done(((f32[16,264,128]{2,1,0:T(8,128)}), f32[16,264,128]{2,1,0:T(8,128)}, u32[]{:S(2)}, u32[]{:S(2)}) %all-to-all-start) | async-done | bytes 2162720 | tf_op jit(solution)/shard_map/all_to_all | solution.py:605
  36.6 5.9 %filter_exp.1 = (f32[16,256,128]{2,1,0:T(8,128)}, f32[4,512,128]{2,1,0:T(8,128)}, f32[4,512,128]{2,1,0:T(8,128)}, s32[2,16,128]{2,1,0:T(8,128)}) custom-call(bf16[512,512]{1,0:T(8,128)(2,1)} %get-tuple-element.10.high_ref, bf16[512,512]{1,0:T(8,128)(2,1)} %get-tuple-element.11.low_ref, f32[16,264,128]{2,1,0:T(8,128)} %all-to-all-done.in_ref.extra_ref, ...), custom_call_target="tpu_custom_call" | custom-call | flops 1610612736 | bytes 8388608 | tf_op jit(solution)/shard_map/filter_exp/pallas_call | solution.py:181
  42.5 0.0 copy-start.4
  42.5 7.0 %all-to-all-start.1 = ((f32[16,256,128]{2,1,0:T(8,128)}), f32[16,256,128]{2,1,0:T(8,128)S(1)}, u32[]{:S(2)}, u32[]{:S(2)}) async-start(f32[16,256,128]{2,1,0:T(8,128)} %get-tuple-element.15), calls=%async_computation.1 | async-start | bytes 4194304 | tf_op jit(solution)/shard_map/all_to_all | solution.py:605
  49.6 6.4 %collective-permute-start = (f32[4,512,128]{2,1,0:T(8,128)}, f32[4,512,128]{2,1,0:T(8,128)S(1)}, u32[]{:S(2)}, u32[]{:S(2)}) collective-permute-start(f32[4,512,128]{2,1,0:T(8,128)} %get-tuple-element.13.refs_1_), channel_id=1, source_target_pairs={{0,1},{1,2},{2,3},{3,4},{4,5},{5,6},{6,7},{8,9},{9,10},{10,11},{11... | collective-permute-start | bytes 3145736 | tf_op jit(solution)/shard_map/ppermute | solution.py:624
  56.0 0.0 copy-done.4
  56.0 1.9 %collective-permute-start.1 = (f32[4,512,128]{2,1,0:T(8,128)S(1)}, f32[4,512,128]{2,1,0:T(8,128)S(1)}, u32[]{:S(2)}, u32[]{:S(2)}) collective-permute-start(f32[4,512,128]{2,1,0:T(8,128)S(1)} %copy-done.4), channel_id=1, source_target_pairs={{1,0},{2,1},{3,2},{4,3},{5,4},{6,5},{7,6},{9,8},{10,9},{11,10},{12... | collective-permute-start | bytes 3145736 | tf_op jit(solution)/shard_map/ppermute | solution.py:623
  57.9 0.0 copy-start.2
  57.9 6.0 %patch_windows.2.refs_2_ = f32[16,144,384]{2,1,0:T(8,128)} custom-call(s32[2,16,128]{2,1,0:T(8,128)} %get-tuple-element.12.table_ref, f32[4,512,128]{2,1,0:T(8,128)} %get-tuple-element.14.refs_0_, f32[4,512,128]{2,1,0:T(8,128)} %get-tuple-element.13.refs_1_), custom_call_target="tpu_custom_call" | custom-call | bytes 12582912 | tf_op jit(solution)/shard_map/patch_windows/pallas_call | solution.py:266
  63.9 4.1 %collective-permute-done.refs_0_ = f32[4,512,128]{2,1,0:T(8,128)S(1)} collective-permute-done((f32[4,512,128]{2,1,0:T(8,128)}, f32[4,512,128]{2,1,0:T(8,128)S(1)}, u32[]{:S(2)}, u32[]{:S(2)}) %collective-permute-start) | collective-permute-done | bytes 1048608 | tf_op jit(solution)/shard_map/ppermute | solution.py:624
  68.0 4.4 %collective-permute-done.1.refs_1_ = f32[4,512,128]{2,1,0:T(8,128)S(1)} collective-permute-done((f32[4,512,128]{2,1,0:T(8,128)S(1)}, f32[4,512,128]{2,1,0:T(8,128)S(1)}, u32[]{:S(2)}, u32[]{:S(2)}) %collective-permute-start.1) | collective-permute-done | bytes 1048608 | tf_op jit(solution)/shard_map/ppermute | solution.py:623
  72.4 0.0 copy-done.2
  72.4 0.0 copy-start
  72.4 2.0 %copy-done = f32[16,144,384]{2,1,0:T(8,128)S(1)} copy-done((f32[16,144,384]{2,1,0:T(8,128)S(1)}, f32[16,144,384]{2,1,0:T(8,128)}, u32[]{:S(2)}) %copy-start) | copy-done | bytes 3538968
  74.4 2.7 %patch_windows.3 = f32[16,144,384]{2,1,0:T(8,128)S(1)} custom-call(s32[2,16,128]{2,1,0:T(8,128)S(1)} %copy-done.2, f32[4,512,128]{2,1,0:T(8,128)S(1)} %collective-permute-done.refs_0_, f32[4,512,128]{2,1,0:T(8,128)S(1)} %collective-permute-done.1.refs_1_, f32[16,144,384]{2,1,0:T(8,128)S(1)} %copy-done), custom_call_target="tpu_custom_call", output_to_operand_aliasing={{}: (3, {})} | custom-call | bytes 6291456 | tf_op jit(solution)/shard_map/patch_windows/pallas_call | solution.py:266
  77.1 0.0 copy-start.1
  77.1 1.8 %copy-done.1 = f32[16,144,384]{2,1,0:T(8,128)} copy-done((f32[16,144,384]{2,1,0:T(8,128)}, f32[16,144,384]{2,1,0:T(8,128)S(1)}, u32[]{:S(2)}) %copy-start.1) | copy-done | bytes 3538968
  78.9 0.0 copy-start.6
  78.9 0.0 all-to-all-done.1.low_ref.high_ref
  78.9 6.8 %all-to-all-start.2 = ((f32[16,144,384]{2,1,0:T(8,128)}), f32[16,144,384]{2,1,0:T(8,128)}, u32[]{:S(2)}, u32[]{:S(2)}) async-start(f32[16,144,384]{2,1,0:T(8,128)} %copy-done.1), calls=%async_computation.2 | async-start | bytes 7077888 | tf_op jit(solution)/shard_map/all_to_all | solution.py:605
  85.7 0.0 copy-done.6
  85.7 0.6 gather_fusion
  86.3 0.1 broadcast_in_dim.9
  86.4 0.1 reshape_reshape.3.later_ref
  86.5 2.1 %join_rows.1 = f32[32,32,512]{2,1,0:T(8,128)} custom-call(f32[16,256,128]{2,1,0:T(8,128)S(1)} %all-to-all-done.1.low_ref.high_ref, f32[16,256,128]{2,1,0:T(8,128)S(1)} %all-to-all-done.1.low_ref.high_ref), custom_call_target="tpu_custom_call" | custom-call | bytes 8388608 | tf_op jit(solution)/shard_map/join_rows/pallas_call | solution.py:123
  88.6 49.1 %all-to-all-done.2.half_ref = f32[16,144,384]{2,1,0:T(8,128)} async-done(((f32[16,144,384]{2,1,0:T(8,128)}), f32[16,144,384]{2,1,0:T(8,128)}, u32[]{:S(2)}, u32[]{:S(2)}) %all-to-all-start.2) | async-done | bytes 3538976 | tf_op jit(solution)/shard_map/all_to_all | solution.py:605
  137.8 15.4 %solve_patches.1 = f32[8,48,2304]{2,1,0:T(8,128)} custom-call(f32[16,144,384]{2,1,0:T(8,128)} %all-to-all-done.2.half_ref, s32[1,384]{1,0:T(1,128)S(1)} %reshape_reshape.3.later_ref), custom_call_target="tpu_custom_call" | custom-call | flops 53084160 | bytes 33554432 | tf_op jit(solution)/shard_map/solve_patches/pallas_call | solution.py:572
  (3 shorter events, 0.0 us)
Async XLA Ops:
  4.3 6.5 %copy-start.5 = (f32[512]{0:T(512)S(1)}, f32[512]{0:T(512)}, u32[]{:S(2)}) copy-start(f32[512]{0:T(512)} %param.6) | copy-start | bytes 6148
  4.3 6.6 %copy-start.3 = (f32[1024,512]{1,0:T(8,128)S(1)}, f32[1024,512]{1,0:T(8,128)}, u32[]{:S(2)}) copy-start(f32[1024,512]{1,0:T(8,128)} %constant.23.clone) | copy-start | bytes 6291460
  4.4 32.2 %all-to-all-start = ((f32[16,264,128]{2,1,0:T(8,128)}), f32[16,264,128]{2,1,0:T(8,128)}, u32[]{:S(2)}, u32[]{:S(2)}) async-start(f32[16,264,128]{2,1,0:T(8,128)} %split_rows.1), calls=%async_computation | async-start | bytes 4325376 | tf_op jit(solution)/shard_map/all_to_all | solution.py:605
  42.5 13.4 %copy-start.4 = (f32[4,512,128]{2,1,0:T(8,128)S(1)}, f32[4,512,128]{2,1,0:T(8,128)}, u32[]{:S(2)}) copy-start(f32[4,512,128]{2,1,0:T(8,128)} %get-tuple-element.14.refs_0_) | copy-start | bytes 3145732
  42.5 36.3 %all-to-all-start.1 = ((f32[16,256,128]{2,1,0:T(8,128)}), f32[16,256,128]{2,1,0:T(8,128)S(1)}, u32[]{:S(2)}, u32[]{:S(2)}) async-start(f32[16,256,128]{2,1,0:T(8,128)} %get-tuple-element.15), calls=%async_computation.1 | async-start | bytes 4194304 | tf_op jit(solution)/shard_map/all_to_all | solution.py:605
  49.6 18.4 %collective-permute-start = (f32[4,512,128]{2,1,0:T(8,128)}, f32[4,512,128]{2,1,0:T(8,128)S(1)}, u32[]{:S(2)}, u32[]{:S(2)}) collective-permute-start(f32[4,512,128]{2,1,0:T(8,128)} %get-tuple-element.13.refs_1_), channel_id=1, source_target_pairs={{0,1},{1,2},{2,3},{3,4},{4,5},{5,6},{6,7},{8,9},{9,10},{10,11},{11... | collective-permute-start | bytes 3145736 | tf_op jit(solution)/shard_map/ppermute | solution.py:624
  56.0 16.4 %collective-permute-start.1 = (f32[4,512,128]{2,1,0:T(8,128)S(1)}, f32[4,512,128]{2,1,0:T(8,128)S(1)}, u32[]{:S(2)}, u32[]{:S(2)}) collective-permute-start(f32[4,512,128]{2,1,0:T(8,128)S(1)} %copy-done.4), channel_id=1, source_target_pairs={{1,0},{2,1},{3,2},{4,3},{5,4},{6,5},{7,6},{9,8},{10,9},{11,10},{12... | collective-permute-start | bytes 3145736 | tf_op jit(solution)/shard_map/ppermute | solution.py:623
  57.9 14.5 %copy-start.2 = (s32[2,16,128]{2,1,0:T(8,128)S(1)}, s32[2,16,128]{2,1,0:T(8,128)}, u32[]{:S(2)}) copy-start(s32[2,16,128]{2,1,0:T(8,128)} %get-tuple-element.12.table_ref) | copy-start | bytes 49156
  72.4 2.0 %copy-start = (f32[16,144,384]{2,1,0:T(8,128)S(1)}, f32[16,144,384]{2,1,0:T(8,128)}, u32[]{:S(2)}) copy-start(f32[16,144,384]{2,1,0:T(8,128)} %patch_windows.2.refs_2_) | copy-start | bytes 10616836
  77.1 1.8 %copy-start.1 = (f32[16,144,384]{2,1,0:T(8,128)}, f32[16,144,384]{2,1,0:T(8,128)S(1)}, u32[]{:S(2)}) copy-start(f32[16,144,384]{2,1,0:T(8,128)S(1)} %patch_windows.3) | copy-start | bytes 10616836
  78.9 6.8 %copy-start.6 = (s32[1,1,8]{2,1,0:T(1,128)S(1)}, s32[1,1,8]{2,1,0:T(1,128)}, u32[]{:S(2)}) copy-start(s32[1,1,8]{2,1,0:T(1,128)} %param.8) | copy-start | bytes 100
  78.9 58.9 %all-to-all-start.2 = ((f32[16,144,384]{2,1,0:T(8,128)}), f32[16,144,384]{2,1,0:T(8,128)}, u32[]{:S(2)}, u32[]{:S(2)}) async-start(f32[16,144,384]{2,1,0:T(8,128)} %copy-done.1), calls=%async_computation.2 | async-start | bytes 7077888 | tf_op jit(solution)/shard_map/all_to_all | solution.py:605

commit v7 on v6

--- a/solution.py
+++ b/solution.py
@@ -146,7 +146,7 @@
     return pl.pallas_call(
         pair_kernel,
         out_shape=[jax.ShapeDtypeStruct((NX, NX), jnp.bfloat16)] * 2,
-        compiler_params=params(56),
+        compiler_params=params(60),
         cost_estimate=pl.CostEstimate(flops=0, bytes_accessed=2 << 20, transcendentals=0),
         name="bf16_pair",
     )(matrix)
@@ -194,7 +194,7 @@
             full((TILES, NX, SIDE)),
             jax.ShapeDtypeStruct((2, WIDE, SIDE), jnp.int32),
         ],
-        compiler_params=params(56),
+        compiler_params=params(60),
         cost_estimate=pl.CostEstimate(
             flops=12 * NX * NX * NZ, bytes_accessed=8 << 20, transcendentals=2 * NX * NZ
         ),
@@ -277,7 +277,7 @@
         ),
         out_shape=full((WIDE, TAPS * EDGE, LANES)),
         input_output_aliases={3: 0} if others else {},
-        compiler_params=params(16 if others else 56),
+        compiler_params=params(58 if others else 60),
         cost_estimate=pl.CostEstimate(
             flops=0, bytes_accessed=slots * (6 << 20), transcendentals=0
         ),

time: 154 us -> 155 us (level)
  the two profiles are of different devices: /device:TPU:117 before, /device:TPU:116 now
where the time goes in v7:
time: 155 us
  waiting for transfers between devices  79.7 us (51%)
  Pallas kernels  40.3 us (26%)
  starting transfers between devices  28 us (18%)
  matrix products  4.93 us (3%)
    all_to_all x3, waiting for transfers between devices, on_device(): swap = lambda v: lax.all_to_all(v, 'wide', split_axis=0, concat_axis=0)  72.9 us
    all_to_all x3, starting transfers between devices, on_device(): swap = lambda v: lax.all_to_all(v, 'wide', split_axis=0, concat_axis=0)  22.5 us
    pallas_call x1, Pallas kernels, solve(): pl.pallas_call(solve_kernel, in_specs=[pl.BlockSpec(memory_space=pl.ANY),...  15.4 us
    pallas_call x2, Pallas kernels, windows(): pl.pallas_call(functools.partial(window_kernel, slots), grid_spec=pltpu.P...  10.9 us
    pallas_call x1, Pallas kernels, filter_exp(): pl.pallas_call(filter_kernel, grid=(4,), in_specs=[whole, whole, block, p...  5.95 us
    dot_general x1, matrix products, on_device(): lax.dot_general(waves, waves * weights, (((0,), (0,)), ((), ())), precisi...  4.93 us
    ppermute x1, waiting for transfers between devices, on_device(): below = lax.ppermute(high, 'mid', forward)  4.92 us
    pallas_call x1, Pallas kernels, split_rows(): pl.pallas_call(split_kernel, grid=(TILES,), in_specs=[pl.BlockSpec((CX, C...  3.69 us
  transfers between devices with their start and end apart: 5, of which 5 were waited for; matrix products, arithmetic and copies ran while one was open for 4% of the time, Pallas kernels for 10%

profile of v7, /device:TPU:116, one launch (start us, length us, event | category | flops | bytes accessed | tf_op | source)
XLA Modules:
  0.0 154.5 jit_solution(11593548050555209230)
XLA Ops:
  0.6 3.7 %split_rows.1 = f32[16,264,128]{2,1,0:T(8,128)} custom-call(f32[32,32,512]{2,1,0:T(8,128)} %in_ref.1, s32[1,16]{1,0:T(1,128)} %bitcast.9, s32[1,8]{1,0:T(1,128)} %bitcast.10), custom_call_target="tpu_custom_call" | custom-call | bytes 8388608 | tf_op jit(solution)/shard_map/split_rows/pallas_call | solution.py:93
  4.3 0.0 copy-start.3
  4.3 0.0 copy-start.1
  4.4 7.1 %all-to-all-start = ((f32[16,264,128]{2,1,0:T(8,128)}), f32[16,264,128]{2,1,0:T(8,128)}, u32[]{:S(2)}, u32[]{:S(2)}) async-start(f32[16,264,128]{2,1,0:T(8,128)} %split_rows.1), calls=%async_computation | async-start | bytes 4325376 | tf_op jit(solution)/shard_map/all_to_all | solution.py:605
  11.4 0.0 copy-done.3
  11.4 0.0 copy-done.1
  11.5 4.9 %fusion.in_ref = f32[512,512]{1,0:T(8,128)} fusion(f32[1024,512]{1,0:T(8,128)S(1)} %copy-done.1, f32[1024]{0:T(1024)S(1)} %maximum_multiply_fusion), kind=kOutput, calls=%fused_computation.1 | convolution fusion | flops 3221749760 | bytes 3149824 | tf_op jit(solution)/shard_map/dot_general | solution.py:611
  16.4 2.3 %bf16_pair.1 = (bf16[512,512]{1,0:T(8,128)(2,1)}, bf16[512,512]{1,0:T(8,128)(2,1)}) custom-call(f32[512,512]{1,0:T(8,128)} %fusion.in_ref), custom_call_target="tpu_custom_call" | custom-call | bytes 2097152 | tf_op jit(solution)/shard_map/bf16_pair/pallas_call | solution.py:146
  18.6 20.2 %all-to-all-done.in_ref.extra_ref = f32[16,264,128]{2,1,0:T(8,128)} async-done(((f32[16,264,128]{2,1,0:T(8,128)}), f32[16,264,128]{2,1,0:T(8,128)}, u32[]{:S(2)}, u32[]{:S(2)}) %all-to-all-start) | async-done | bytes 2162720 | tf_op jit(solution)/shard_map/all_to_all | solution.py:605
  38.9 5.9 %filter_exp.1 = (f32[16,256,128]{2,1,0:T(8,128)}, f32[4,512,128]{2,1,0:T(8,128)}, f32[4,512,128]{2,1,0:T(8,128)}, s32[2,16,128]{2,1,0:T(8,128)}) custom-call(bf16[512,512]{1,0:T(8,128)(2,1)} %get-tuple-element.10.high_ref, bf16[512,512]{1,0:T(8,128)(2,1)} %get-tuple-element.11.low_ref, f32[16,264,128]{2,1,0:T(8,128)} %all-to-all-done.in_ref.extra_ref, ...), custom_call_target="tpu_custom_call" | custom-call | flops 1610612736 | bytes 8388608 | tf_op jit(solution)/shard_map/filter_exp/pallas_call | solution.py:181
  44.8 7.6 %all-to-all-start.1 = ((f32[16,256,128]{2,1,0:T(8,128)}), f32[16,256,128]{2,1,0:T(8,128)S(1)}, u32[]{:S(2)}, u32[]{:S(2)}) async-start(f32[16,256,128]{2,1,0:T(8,128)} %get-tuple-element.15), calls=%async_computation.1 | async-start | bytes 4194304 | tf_op jit(solution)/shard_map/all_to_all | solution.py:605
  52.4 1.9 %collective-permute-start = (f32[4,512,128]{2,1,0:T(8,128)}, f32[4,512,128]{2,1,0:T(8,128)S(1)}, u32[]{:S(2)}, u32[]{:S(2)}) collective-permute-start(f32[4,512,128]{2,1,0:T(8,128)} %get-tuple-element.13.refs_1_), channel_id=1, source_target_pairs={{0,1},{1,2},{2,3},{3,4},{4,5},{5,6},{6,7},{8,9},{9,10},{10,11},{11... | collective-permute-start | bytes 3145736 | tf_op jit(solution)/shard_map/ppermute | solution.py:624
  54.3 3.6 %collective-permute-start.1 = (f32[4,512,128]{2,1,0:T(8,128)}, f32[4,512,128]{2,1,0:T(8,128)}, u32[]{:S(2)}, u32[]{:S(2)}) collective-permute-start(f32[4,512,128]{2,1,0:T(8,128)} %get-tuple-element.14.refs_0_), channel_id=1, source_target_pairs={{1,0},{2,1},{3,2},{4,3},{5,4},{6,5},{7,6},{9,8},{10,9},{11,10},{12... | collective-permute-start | bytes 3145736 | tf_op jit(solution)/shard_map/ppermute | solution.py:623
  57.9 5.8 %patch_windows.2.refs_2_ = f32[16,144,384]{2,1,0:T(8,128)} custom-call(s32[2,16,128]{2,1,0:T(8,128)} %get-tuple-element.12.table_ref, f32[4,512,128]{2,1,0:T(8,128)} %get-tuple-element.14.refs_0_, f32[4,512,128]{2,1,0:T(8,128)} %get-tuple-element.13.refs_1_), custom_call_target="tpu_custom_call" | custom-call | bytes 12582912 | tf_op jit(solution)/shard_map/patch_windows/pallas_call | solution.py:266
  63.8 4.9 %collective-permute-done.refs_0_ = f32[4,512,128]{2,1,0:T(8,128)S(1)} collective-permute-done((f32[4,512,128]{2,1,0:T(8,128)}, f32[4,512,128]{2,1,0:T(8,128)S(1)}, u32[]{:S(2)}, u32[]{:S(2)}) %collective-permute-start) | collective-permute-done | bytes 1048608 | tf_op jit(solution)/shard_map/ppermute | solution.py:624
  68.7 0.0 copy-start.2
  68.7 1.9 %collective-permute-done.1.refs_1_ = f32[4,512,128]{2,1,0:T(8,128)} collective-permute-done((f32[4,512,128]{2,1,0:T(8,128)}, f32[4,512,128]{2,1,0:T(8,128)}, u32[]{:S(2)}, u32[]{:S(2)}) %collective-permute-start.1) | collective-permute-done | bytes 1048608 | tf_op jit(solution)/shard_map/ppermute | solution.py:623
  70.5 0.0 copy-done.2
  70.5 5.0 %patch_windows.3 = f32[16,144,384]{2,1,0:T(8,128)} custom-call(s32[2,16,128]{2,1,0:T(8,128)} %get-tuple-element.12.table_ref, f32[4,512,128]{2,1,0:T(8,128)} %copy-done.2, f32[4,512,128]{2,1,0:T(8,128)} %collective-permute-done.1.refs_1_, f32[16,144,384]{2,1,0:T(8,128)} %patch_windows.2.refs_2_), custom_call_target="tpu_custom_call", output_to_operand_aliasing={{}: (3, {})} | custom-call | bytes 6291456 | tf_op jit(solution)/shard_map/patch_windows/pallas_call | solution.py:266
  75.6 0.0 copy-start.4
  75.6 0.0 copy-start
  75.6 1.0 all-to-all-done.1.low_ref.high_ref
  76.6 7.8 %all-to-all-start.2 = ((f32[16,144,384]{2,1,0:T(8,128)}), f32[16,144,384]{2,1,0:T(8,128)}, u32[]{:S(2)}, u32[]{:S(2)}) async-start(f32[16,144,384]{2,1,0:T(8,128)} %patch_windows.3), calls=%async_computation.2 | async-start | bytes 7077888 | tf_op jit(solution)/shard_map/all_to_all | solution.py:605
  84.5 0.0 copy-done.4
  84.5 0.0 copy-done
  84.5 0.6 gather_fusion
  85.2 0.1 broadcast_in_dim.9
  85.2 0.1 reshape_reshape.3.later_ref
  85.3 2.1 %join_rows.1 = f32[32,32,512]{2,1,0:T(8,128)} custom-call(f32[16,256,128]{2,1,0:T(8,128)S(1)} %all-to-all-done.1.low_ref.high_ref, f32[16,256,128]{2,1,0:T(8,128)S(1)} %all-to-all-done.1.low_ref.high_ref), custom_call_target="tpu_custom_call" | custom-call | bytes 8388608 | tf_op jit(solution)/shard_map/join_rows/pallas_call | solution.py:123
  87.4 51.7 %all-to-all-done.2.half_ref = f32[16,144,384]{2,1,0:T(8,128)} async-done(((f32[16,144,384]{2,1,0:T(8,128)}), f32[16,144,384]{2,1,0:T(8,128)}, u32[]{:S(2)}, u32[]{:S(2)}) %all-to-all-start.2) | async-done | bytes 3538976 | tf_op jit(solution)/shard_map/all_to_all | solution.py:605
  139.1 15.4 %solve_patches.1 = f32[8,48,2304]{2,1,0:T(8,128)} custom-call(f32[16,144,384]{2,1,0:T(8,128)} %all-to-all-done.2.half_ref, s32[1,384]{1,0:T(1,128)S(1)} %reshape_reshape.3.later_ref), custom_call_target="tpu_custom_call" | custom-call | flops 53084160 | bytes 33554432 | tf_op jit(solution)/shard_map/solve_patches/pallas_call | solution.py:572
  (3 shorter events, 0.0 us)
Async XLA Ops:
  4.3 7.1 %copy-start.3 = (f32[512]{0:T(512)S(1)}, f32[512]{0:T(512)}, u32[]{:S(2)}) copy-start(f32[512]{0:T(512)} %param.6) | copy-start | bytes 6148
  4.3 7.1 %copy-start.1 = (f32[1024,512]{1,0:T(8,128)S(1)}, f32[1024,512]{1,0:T(8,128)}, u32[]{:S(2)}) copy-start(f32[1024,512]{1,0:T(8,128)} %constant.23.clone) | copy-start | bytes 6291460
  4.4 34.5 %all-to-all-start = ((f32[16,264,128]{2,1,0:T(8,128)}), f32[16,264,128]{2,1,0:T(8,128)}, u32[]{:S(2)}, u32[]{:S(2)}) async-start(f32[16,264,128]{2,1,0:T(8,128)} %split_rows.1), calls=%async_computation | async-start | bytes 4325376 | tf_op jit(solution)/shard_map/all_to_all | solution.py:605
  44.8 31.8 %all-to-all-start.1 = ((f32[16,256,128]{2,1,0:T(8,128)}), f32[16,256,128]{2,1,0:T(8,128)S(1)}, u32[]{:S(2)}, u32[]{:S(2)}) async-start(f32[16,256,128]{2,1,0:T(8,128)} %get-tuple-element.15), calls=%async_computation.1 | async-start | bytes 4194304 | tf_op jit(solution)/shard_map/all_to_all | solution.py:605
  52.4 16.3 %collective-permute-start = (f32[4,512,128]{2,1,0:T(8,128)}, f32[4,512,128]{2,1,0:T(8,128)S(1)}, u32[]{:S(2)}, u32[]{:S(2)}) collective-permute-start(f32[4,512,128]{2,1,0:T(8,128)} %get-tuple-element.13.refs_1_), channel_id=1, source_target_pairs={{0,1},{1,2},{2,3},{3,4},{4,5},{5,6},{6,7},{8,9},{9,10},{10,11},{11... | collective-permute-start | bytes 3145736 | tf_op jit(solution)/shard_map/ppermute | solution.py:624
  54.3 16.3 %collective-permute-start.1 = (f32[4,512,128]{2,1,0:T(8,128)}, f32[4,512,128]{2,1,0:T(8,128)}, u32[]{:S(2)}, u32[]{:S(2)}) collective-permute-start(f32[4,512,128]{2,1,0:T(8,128)} %get-tuple-element.14.refs_0_), channel_id=1, source_target_pairs={{1,0},{2,1},{3,2},{4,3},{5,4},{6,5},{7,6},{9,8},{10,9},{11,10},{12... | collective-permute-start | bytes 3145736 | tf_op jit(solution)/shard_map/ppermute | solution.py:623
  68.7 1.9 %copy-start.2 = (f32[4,512,128]{2,1,0:T(8,128)}, f32[4,512,128]{2,1,0:T(8,128)S(1)}, u32[]{:S(2)}) copy-start(f32[4,512,128]{2,1,0:T(8,128)S(1)} %collective-permute-done.refs_0_) | copy-start | bytes 3145732
  75.6 8.9 %copy-start.4 = (s32[1,1,8]{2,1,0:T(1,128)S(1)}, s32[1,1,8]{2,1,0:T(1,128)}, u32[]{:S(2)}) copy-start(s32[1,1,8]{2,1,0:T(1,128)} %param.8) | copy-start | bytes 100
  75.6 8.9 %copy-start = (s32[2,16,128]{2,1,0:T(8,128)S(1)}, s32[2,16,128]{2,1,0:T(8,128)}, u32[]{:S(2)}) copy-start(s32[2,16,128]{2,1,0:T(8,128)} %get-tuple-element.12.table_ref) | copy-start | bytes 49156
  76.6 62.5 %all-to-all-start.2 = ((f32[16,144,384]{2,1,0:T(8,128)}), f32[16,144,384]{2,1,0:T(8,128)}, u32[]{:S(2)}, u32[]{:S(2)}) async-start(f32[16,144,384]{2,1,0:T(8,128)} %patch_windows.3), calls=%async_computation.2 | async-start | bytes 7077888 | tf_op jit(solution)/shard_map/all_to_all | solution.py:605

commit v8 on v7

--- a/solution.py
+++ b/solution.py
@@ -152,7 +152,7 @@
     )(matrix)
 
 
-def filter_kernel(high_ref, low_ref, in_ref, extra_ref, parts_ref, first_ref, second_ref, table_ref):
+def filter_kernel(odd_ref, high_ref, low_ref, in_ref, extra_ref, parts_ref, first_ref, second_ref, table_ref):
     for k in range(2):
         table_ref[k] = extra_ref[:, k, :].astype(jnp.int32)
     lines = jnp.concatenate(
@@ -175,19 +175,29 @@
     pl.when(pl.program_id(0) >= 2)(lambda: plane(second_ref))
 
 
-def filter_exp(pair, lines):
-    whole = pl.BlockSpec((NX, NX), lambda i: (0, 0))
-    block = pl.BlockSpec((WIDE, 2 * CX, SIDE), lambda i: (0, i, 0))
+def filter_exp(odd, pair, lines):
+    whole = pl.BlockSpec((NX, NX), lambda i, odd: (0, 0))
+    block = pl.BlockSpec(
+        (WIDE, 2 * CX, SIDE), lambda i, odd: (0, 2 * ((i >> 1) ^ odd[0]) + (i & 1), 0)
+    )
     return pl.pallas_call(
         filter_kernel,
-        grid=(4,),
-        in_specs=[whole, whole, block, pl.BlockSpec((WIDE, 8, SIDE), lambda i: (0, ROWS // 8, 0))],
-        out_specs=[
-            block,
-            pl.BlockSpec((2, NX, SIDE), lambda i: (jnp.minimum(i, 1), 0, 0)),
-            pl.BlockSpec((2, NX, SIDE), lambda i: (jnp.maximum(i - 2, 0), 0, 0)),
-            pl.BlockSpec((2, WIDE, SIDE), lambda i: (0, 0, 0)),
-        ],
+        grid_spec=pltpu.PrefetchScalarGridSpec(
+            num_scalar_prefetch=1,
+            grid=(4,),
+            in_specs=[
+                whole,
+                whole,
+                block,
+                pl.BlockSpec((WIDE, 8, SIDE), lambda i, odd: (0, ROWS // 8, 0)),
+            ],
+            out_specs=[
+                block,
+                pl.BlockSpec((2, NX, SIDE), lambda i, odd: (jnp.minimum(i, 1), 0, 0)),
+                pl.BlockSpec((2, NX, SIDE), lambda i, odd: (jnp.maximum(i - 2, 0), 0, 0)),
+                pl.BlockSpec((2, WIDE, SIDE), lambda i, odd: (0, 0, 0)),
+            ],
+        ),
         out_shape=[
             full((WIDE, ROWS, SIDE)),
             full((TILES, NX, SIDE)),
@@ -199,10 +209,10 @@
             flops=12 * NX * NX * NZ, bytes_accessed=8 << 20, transcendentals=2 * NX * NZ
         ),
         name="filter_exp",
-    )(*pair, lines, lines)
-
-
-def window_kernel(slots, table_ref, *refs):
+    )(odd, *pair, lines, lines)
+
+
+def window_kernel(slots, table_ref, odd_ref, *refs):
     low_ref, high_ref = refs[:2]
     out_ref, held, sems = refs[-3:]
     step = pl.program_id(0)
@@ -243,7 +253,7 @@
         for t in range(slots):
             tiles = [None] * 3
             for p, (x_at, t_at, tile, offset, turn) in enumerate(places):
-                plane = t if slots == 2 else t_at
+                plane = (t if slots == 2 else t_at) ^ odd_ref[0]
                 rows = pl.ds(x_at, EDGE)
                 near = held[plane, tile, rows, :]
                 far = held[plane, tile + 1, rows, :]
@@ -260,29 +270,29 @@
     lax.fori_loop(0, OWNERS, one_owner, 0, unroll=UNROLL)
 
 
-def windows(table, planes, *others):
+def windows(table, odd, planes, *others):
     slots = 1 if others else 2
     at = 2 if others else 0
     return pl.pallas_call(
         functools.partial(window_kernel, slots),
         grid_spec=pltpu.PrefetchScalarGridSpec(
-            num_scalar_prefetch=1,
+            num_scalar_prefetch=2,
             grid=(WIDE // OWNERS,),
             in_specs=[pl.BlockSpec(memory_space=pl.ANY)] * (2 + len(others)),
-            out_specs=pl.BlockSpec((OWNERS, slots * EDGE, LANES), lambda d, table: (d, at, 0)),
+            out_specs=pl.BlockSpec((OWNERS, slots * EDGE, LANES), lambda d, table, odd: (d, at, 0)),
             scratch_shapes=[
                 pltpu.VMEM((2, TILES + 2, NX + 2 * LAYER, SIDE), F32),
                 pltpu.SemaphoreType.DMA((2,)),
             ],
         ),
         out_shape=full((WIDE, TAPS * EDGE, LANES)),
-        input_output_aliases={3: 0} if others else {},
+        input_output_aliases={4: 0} if others else {},
         compiler_params=params(58 if others else 60),
         cost_estimate=pl.CostEstimate(
             flops=0, bytes_accessed=slots * (6 << 20), transcendentals=0
         ),
         name="patch_windows",
-    )(table, *planes, *others)
+    )(table, odd, *planes, *others)
 
 
 STRIPS = EDGE // 8
@@ -616,15 +626,17 @@
         preferred_element_type=F32,
     )
     count = lax.axis_size("mid")
-    forward = [(i, i + 1) for i in range(count - 1)]
-    backward = [(i + 1, i) for i in range(count - 1)]
+    pairs = lambda start: [
+        edge for i in range(start, count - 1, 2) for edge in ((i, i + 1), (i + 1, i))
+    ]
+    odd = (lax.axis_index("mid") & 1).reshape(1)
     pair = bf16_pair(matrix)
-    parts, low, high, table = filter_exp(pair, lines)
-    above = lax.ppermute(low, "mid", backward)
-    below = lax.ppermute(high, "mid", forward)
+    parts, crossing, staying, table = filter_exp(odd, pair, lines)
+    crossed = lax.ppermute(crossing, "mid", pairs(1))
+    stayed = lax.ppermute(staying, "mid", pairs(0))
     back = swap(parts)
-    outgoing = windows(table, (low, high))
-    outgoing = windows(table, (below, above), outgoing)
+    outgoing = windows(table, odd, (crossing, staying))
+    outgoing = windows(table, odd, (crossed, stayed), outgoing)
     outgoing, back = lax.optimization_barrier((outgoing, back))
     incoming = swap(outgoing)
     coefficient = join_rows(back)

time: 155 us -> 147 us (0.948)
  the two profiles are of different devices: /device:TPU:116 before, /device:TPU:0 now
where the time goes in v8:
time: 147 us; the launch traced here: 146 us
  waiting for transfers between devices  77.8 us (53%)
  Pallas kernels  40.4 us (27%)
  starting transfers between devices  20.1 us (14%)
  matrix products  4.92 us (3%)
  local copies, waits for them, and re-layouts  1.8 us (1%)
    all_to_all x3, waiting for transfers between devices, on_device(): swap = lambda v: lax.all_to_all(v, 'wide', split_axis=0, concat_axis=0)  77.8 us
    all_to_all x3, starting transfers between devices, on_device(): swap = lambda v: lax.all_to_all(v, 'wide', split_axis=0, concat_axis=0)  16.4 us
    pallas_call x1, Pallas kernels, solve(): pl.pallas_call(solve_kernel, in_specs=[pl.BlockSpec(memory_space=pl.ANY),...  15.4 us
    pallas_call x2, Pallas kernels, windows(): pl.pallas_call(functools.partial(window_kernel, slots), grid_spec=pltpu.P...  11 us
    pallas_call x1, Pallas kernels, filter_exp(): pl.pallas_call(filter_kernel, grid_spec=pltpu.PrefetchScalarGridSpec(num_...  5.94 us
    dot_general x1, matrix products, on_device(): lax.dot_general(waves, waves * weights, (((0,), (0,)), ((), ())), precisi...  4.92 us
    pallas_call x1, Pallas kernels, split_rows(): pl.pallas_call(split_kernel, grid=(TILES,), in_specs=[pl.BlockSpec((CX, C...  3.69 us
    ppermute x1, starting transfers between devices, on_device(): stayed = lax.ppermute(staying, 'mid', pairs(0))  2.95 us
  transfers between devices with their start and end apart: 5, of which 3 were waited for; matrix products, arithmetic and copies ran while one was open for 4% of the time, Pallas kernels for 11%

profile of v8, /device:TPU:0, one launch (start us, length us, event | category | flops | bytes accessed | tf_op | source)
XLA Modules:
  0.0 145.8 jit_solution(10519605881505226108)
XLA Ops:
  0.6 3.7 %split_rows.1 = f32[16,264,128]{2,1,0:T(8,128)} custom-call(f32[32,32,512]{2,1,0:T(8,128)} %in_ref.1, s32[1,16]{1,0:T(1,128)} %bitcast.10, s32[1,8]{1,0:T(1,128)} %bitcast.11), custom_call_target="tpu_custom_call" | custom-call | bytes 8388608 | tf_op jit(solution)/shard_map/split_rows/pallas_call | solution.py:93
  4.3 0.0 copy-start.3
  4.3 0.0 copy-start.1
  4.4 8.1 %all-to-all-start = ((f32[16,264,128]{2,1,0:T(8,128)}), f32[16,264,128]{2,1,0:T(8,128)}, u32[]{:S(2)}, u32[]{:S(2)}) async-start(f32[16,264,128]{2,1,0:T(8,128)} %split_rows.1), calls=%async_computation | async-start | bytes 4325376 | tf_op jit(solution)/shard_map/all_to_all | solution.py:615
  12.5 0.0 copy-done.3
  12.5 0.0 copy-done.1
  12.5 4.9 %fusion.in_ref = f32[512,512]{1,0:T(8,128)} fusion(f32[1024,512]{1,0:T(8,128)S(1)} %copy-done.1, f32[1024]{0:T(1024)S(1)} %maximum_multiply_fusion), kind=kOutput, calls=%fused_computation.1 | convolution fusion | flops 3221749760 | bytes 3149824 | tf_op jit(solution)/shard_map/dot_general | solution.py:621
  17.5 2.3 %bf16_pair.1 = (bf16[512,512]{1,0:T(8,128)(2,1)}, bf16[512,512]{1,0:T(8,128)(2,1)}) custom-call(f32[512,512]{1,0:T(8,128)} %fusion.in_ref), custom_call_target="tpu_custom_call" | custom-call | bytes 2097152 | tf_op jit(solution)/shard_map/bf16_pair/pallas_call | solution.py:146
  19.7 24.0 %all-to-all-done.in_ref.extra_ref = f32[16,264,128]{2,1,0:T(8,128)} async-done(((f32[16,264,128]{2,1,0:T(8,128)}), f32[16,264,128]{2,1,0:T(8,128)}, u32[]{:S(2)}, u32[]{:S(2)}) %all-to-all-start) | async-done | bytes 2162720 | tf_op jit(solution)/shard_map/all_to_all | solution.py:615
  43.8 5.9 %filter_exp.1 = (f32[16,256,128]{2,1,0:T(8,128)}, f32[4,512,128]{2,1,0:T(8,128)}, f32[4,512,128]{2,1,0:T(8,128)}, s32[2,16,128]{2,1,0:T(8,128)}) custom-call(s32[1]{0:T(128)} %bitcast.odd_ref, bf16[512,512]{1,0:T(8,128)(2,1)} %get-tuple-element.10.high_ref, bf16[512,512]{1,0:T(8,128)(2,1)} %get-tuple-element.11.low_ref, ...), custom_call_target="tpu_custom_call" | custom-call | flops 1610612736 | bytes 8388608 | tf_op jit(solution)/shard_map/filter_exp/pallas_call | solution.py:183
  49.7 3.7 %all-to-all-start.1 = ((f32[16,256,128]{2,1,0:T(8,128)}), f32[16,256,128]{2,1,0:T(8,128)S(1)}, u32[]{:S(2)}, u32[]{:S(2)}) async-start(f32[16,256,128]{2,1,0:T(8,128)} %get-tuple-element.15), calls=%async_computation.1 | async-start | bytes 4194304 | tf_op jit(solution)/shard_map/all_to_all | solution.py:615
  53.4 0.7 collective-permute-start
  54.2 3.0 %collective-permute-start.1 = (f32[4,512,128]{2,1,0:T(8,128)}, f32[4,512,128]{2,1,0:T(8,128)}, u32[]{:S(2)}, u32[]{:S(2)}) collective-permute-start(f32[4,512,128]{2,1,0:T(8,128)} %get-tuple-element.14.refs_1_), channel_id=1, source_target_pairs={{0,1},{1,0},{2,3},{3,2},{4,5},{5,4},{6,7},{7,6},{8,9},{9,8},{10,11... | collective-permute-start | bytes 3145736 | tf_op jit(solution)/shard_map/ppermute | solution.py:636
  57.1 5.9 %patch_windows.2.refs_2_ = f32[16,144,384]{2,1,0:T(8,128)} custom-call(s32[2,16,128]{2,1,0:T(8,128)} %get-tuple-element.12.table_ref, s32[1]{0:T(128)} %bitcast.odd_ref, f32[4,512,128]{2,1,0:T(8,128)} %get-tuple-element.13.refs_0_, f32[4,512,128]{2,1,0:T(8,128)} %get-tuple-element.14.refs_1_), custom_call_target="tpu_custom_call" | custom-call | bytes 12582912 | tf_op jit(solution)/shard_map/patch_windows/pallas_call | solution.py:276
  63.0 0.0 collective-permute-done.refs_0_
  63.0 0.0 copy-start.2
  63.0 0.0 collective-permute-done.1.refs_1_
  63.0 1.0 copy-done.2
  64.0 5.1 %patch_windows.3 = f32[16,144,384]{2,1,0:T(8,128)} custom-call(s32[2,16,128]{2,1,0:T(8,128)} %get-tuple-element.12.table_ref, s32[1]{0:T(128)} %bitcast.odd_ref, f32[4,512,128]{2,1,0:T(8,128)} %copy-done.2, f32[4,512,128]{2,1,0:T(8,128)} %collective-permute-done.1.refs_1_, f32[16,144,384]{2,1,0:T(8,128)} %patch_windows.2.refs_2_), custom_call_target="tpu_custom_call", output_to_operand_aliasing={{}: (4, {})} | custom-call | bytes 6291456 | tf_op jit(solution)/shard_map/patch_windows/pallas_call | solution.py:276
  69.1 0.0 copy-start.4
  69.1 0.0 copy-start
  69.1 12.0 %all-to-all-done.1.low_ref.high_ref = f32[16,256,128]{2,1,0:T(8,128)S(1)} async-done(((f32[16,256,128]{2,1,0:T(8,128)}), f32[16,256,128]{2,1,0:T(8,128)S(1)}, u32[]{:S(2)}, u32[]{:S(2)}) %all-to-all-start.1) | async-done | bytes 2097184 | tf_op jit(solution)/shard_map/all_to_all | solution.py:615
  81.1 4.5 %all-to-all-start.2 = ((f32[16,144,384]{2,1,0:T(8,128)}), f32[16,144,384]{2,1,0:T(8,128)}, u32[]{:S(2)}, u32[]{:S(2)}) async-start(f32[16,144,384]{2,1,0:T(8,128)} %patch_windows.3), calls=%async_computation.2 | async-start | bytes 7077888 | tf_op jit(solution)/shard_map/all_to_all | solution.py:615
  85.6 0.0 copy-done.4
  85.6 0.0 copy-done
  85.7 0.6 gather_fusion
  86.3 0.1 broadcast_in_dim.9
  86.4 0.1 reshape_reshape.3.later_ref
  86.5 2.1 %join_rows.1 = f32[32,32,512]{2,1,0:T(8,128)} custom-call(f32[16,256,128]{2,1,0:T(8,128)S(1)} %all-to-all-done.1.low_ref.high_ref, f32[16,256,128]{2,1,0:T(8,128)S(1)} %all-to-all-done.1.low_ref.high_ref), custom_call_target="tpu_custom_call" | custom-call | bytes 8388608 | tf_op jit(solution)/shard_map/join_rows/pallas_call | solution.py:123
  88.6 41.8 %all-to-all-done.2.half_ref = f32[16,144,384]{2,1,0:T(8,128)} async-done(((f32[16,144,384]{2,1,0:T(8,128)}), f32[16,144,384]{2,1,0:T(8,128)}, u32[]{:S(2)}, u32[]{:S(2)}) %all-to-all-start.2) | async-done | bytes 3538976 | tf_op jit(solution)/shard_map/all_to_all | solution.py:615
  130.4 15.4 %solve_patches.1 = f32[8,48,2304]{2,1,0:T(8,128)} custom-call(f32[16,144,384]{2,1,0:T(8,128)} %all-to-all-done.2.half_ref, s32[1,384]{1,0:T(1,128)S(1)} %reshape_reshape.3.later_ref), custom_call_target="tpu_custom_call" | custom-call | flops 53084160 | bytes 33554432 | tf_op jit(solution)/shard_map/solve_patches/pallas_call | solution.py:582
  (3 shorter events, 0.0 us)
Async XLA Ops:
  4.3 8.2 %copy-start.3 = (f32[512]{0:T(512)S(1)}, f32[512]{0:T(512)}, u32[]{:S(2)}) copy-start(f32[512]{0:T(512)} %param.6) | copy-start | bytes 6148
  4.3 8.2 %copy-start.1 = (f32[1024,512]{1,0:T(8,128)S(1)}, f32[1024,512]{1,0:T(8,128)}, u32[]{:S(2)}) copy-start(f32[1024,512]{1,0:T(8,128)} %constant.27.clone) | copy-start | bytes 6291460
  4.4 39.4 %all-to-all-start = ((f32[16,264,128]{2,1,0:T(8,128)}), f32[16,264,128]{2,1,0:T(8,128)}, u32[]{:S(2)}, u32[]{:S(2)}) async-start(f32[16,264,128]{2,1,0:T(8,128)} %split_rows.1), calls=%async_computation | async-start | bytes 4325376 | tf_op jit(solution)/shard_map/all_to_all | solution.py:615
  49.7 31.4 %all-to-all-start.1 = ((f32[16,256,128]{2,1,0:T(8,128)}), f32[16,256,128]{2,1,0:T(8,128)S(1)}, u32[]{:S(2)}, u32[]{:S(2)}) async-start(f32[16,256,128]{2,1,0:T(8,128)} %get-tuple-element.15), calls=%async_computation.1 | async-start | bytes 4194304 | tf_op jit(solution)/shard_map/all_to_all | solution.py:615
  53.4 9.5 %collective-permute-start = (f32[4,512,128]{2,1,0:T(8,128)}, f32[4,512,128]{2,1,0:T(8,128)S(1)}, u32[]{:S(2)}, u32[]{:S(2)}) collective-permute-start(f32[4,512,128]{2,1,0:T(8,128)} %get-tuple-element.13.refs_0_), channel_id=1, source_target_pairs={{1,2},{2,1},{3,4},{4,3},{5,6},{6,5},{9,10},{10,9},{11,12},{12,11},... | collective-permute-start | bytes 3145736 | tf_op jit(solution)/shard_map/ppermute | solution.py:635
  54.2 8.8 %collective-permute-start.1 = (f32[4,512,128]{2,1,0:T(8,128)}, f32[4,512,128]{2,1,0:T(8,128)}, u32[]{:S(2)}, u32[]{:S(2)}) collective-permute-start(f32[4,512,128]{2,1,0:T(8,128)} %get-tuple-element.14.refs_1_), channel_id=1, source_target_pairs={{0,1},{1,0},{2,3},{3,2},{4,5},{5,4},{6,7},{7,6},{8,9},{9,8},{10,11... | collective-permute-start | bytes 3145736 | tf_op jit(solution)/shard_map/ppermute | solution.py:636
  63.0 1.0 copy-start.2
  69.1 16.5 %copy-start.4 = (s32[1,1,8]{2,1,0:T(1,128)S(1)}, s32[1,1,8]{2,1,0:T(1,128)}, u32[]{:S(2)}) copy-start(s32[1,1,8]{2,1,0:T(1,128)} %param.8) | copy-start | bytes 100
  69.1 16.5 %copy-start = (s32[2,16,128]{2,1,0:T(8,128)S(1)}, s32[2,16,128]{2,1,0:T(8,128)}, u32[]{:S(2)}) copy-start(s32[2,16,128]{2,1,0:T(8,128)} %get-tuple-element.12.table_ref) | copy-start | bytes 49156
  81.1 49.3 %all-to-all-start.2 = ((f32[16,144,384]{2,1,0:T(8,128)}), f32[16,144,384]{2,1,0:T(8,128)}, u32[]{:S(2)}, u32[]{:S(2)}) async-start(f32[16,144,384]{2,1,0:T(8,128)} %patch_windows.3), calls=%async_computation.2 | async-start | bytes 7077888 | tf_op jit(solution)/shard_map/all_to_all | solution.py:615

commit v9 on v8

--- a/solution.py
+++ b/solution.py
@@ -53,58 +53,58 @@
     return pieces
 
 
-def split_kernel(in_ref, send_ref, source_ref, out_ref, held, sems):
-    j = pl.program_id(0)
-
-    def leave(t, tile):
-        rows = pl.ds(pl.multiple_of((t * TILES + tile) * CX, CX), CX)
-        return pltpu.make_async_copy(held.at[:, rows, :], out_ref.at[:, rows, :], sems.at[t, tile])
-
-    def leave_tables():
-        rows = pl.ds(ROWS, 8)
-        return pltpu.make_async_copy(held.at[:, rows, :], out_ref.at[:, rows, :], sems.at[2, 0])
-
-    @pl.when(j == 0)
-    def _():
-        for w in range(WIDE):
-            held[w, ROWS:ROWS + 1, 0:WIDE] = send_ref[...].astype(F32)
-            held[w, ROWS + 1:ROWS + 2, 0:PATCH_DEV] = source_ref[...].astype(F32)
-        leave_tables().start()
-
-    for t in range(2):
-        first = pl.multiple_of((t * TILES + j) * CX, CX)
-        for x in range(0, CX, 8):
-            for y in range(0, WIDE, 8):
-                at = t * WIDE + y
-                pieces = exchange([in_ref[x + i, at:at + 8, :] for i in range(8)])
-                for i in range(8):
-                    held[y + i, pl.ds(first + x, 8), :] = pieces[i]
-        leave(t, j).start()
-
-    @pl.when(j == TILES - 1)
-    def _():
-        leave_tables().wait()
+def split_kernel(in_ref, send_ref, source_ref, out_ref, taken, held, arrive, leave):
+    arrivals = [
+        pltpu.make_async_copy(
+            in_ref.at[:, :, pl.ds(j * SIDE, SIDE)], taken.at[j], arrive.at[j]
+        )
+        for j in range(TILES)
+    ]
+    for copy in arrivals:
+        copy.start()
+
+    def depart(first, count, sem):
+        rows = pl.ds(first, count)
+        copy = pltpu.make_async_copy(held.at[:, rows, :], out_ref.at[:, rows, :], sem)
+        copy.start()
+        return copy
+
+    for w in range(WIDE):
+        held[w, ROWS:ROWS + 1, 0:WIDE] = send_ref[...].astype(F32)
+        held[w, ROWS + 1:ROWS + 2, 0:PATCH_DEV] = source_ref[...].astype(F32)
+    departures = [depart(ROWS, 8, leave.at[2, 0])]
+    for j in range(TILES):
+        arrivals[j].wait()
         for t in range(2):
-            for tile in range(TILES):
-                leave(t, tile).wait()
+            first = (t * TILES + j) * CX
+            for x in range(0, CX, 8):
+                for y in range(0, WIDE, 8):
+                    at = t * WIDE + y
+                    pieces = exchange([taken[j, x + i, at:at + 8, :] for i in range(8)])
+                    for i in range(8):
+                        held[y + i, first + x:first + x + 8, :] = pieces[i]
+            departures.append(depart(first, CX, leave.at[t, j]))
+    for copy in departures:
+        copy.wait()
 
 
 def split_rows(block, send, source):
     return pl.pallas_call(
         split_kernel,
-        grid=(TILES,),
         in_specs=[
-            pl.BlockSpec((CX, CY, SIDE), lambda j: (0, 0, j)),
-            pl.BlockSpec((1, WIDE), lambda j: (0, 0)),
-            pl.BlockSpec((1, PATCH_DEV), lambda j: (0, 0)),
+            pl.BlockSpec(memory_space=pl.ANY),
+            pl.BlockSpec(memory_space=pltpu.VMEM),
+            pl.BlockSpec(memory_space=pltpu.VMEM),
         ],
         out_specs=pl.BlockSpec(memory_space=pl.ANY),
         out_shape=full((WIDE, ROWS + 8, SIDE)),
         scratch_shapes=[
+            pltpu.VMEM((TILES, CX, CY, SIDE), F32),
             pltpu.VMEM((WIDE, ROWS + 8, SIDE), F32),
+            pltpu.SemaphoreType.DMA((TILES,)),
             pltpu.SemaphoreType.DMA((3, TILES)),
         ],
-        compiler_params=params(56),
+        compiler_params=params(60),
         cost_estimate=pl.CostEstimate(flops=0, bytes_accessed=8 << 20, transcendentals=0),
         name="split_rows",
     )(block, send, source)
@@ -221,9 +221,10 @@
     def _():
         copies = [
             pltpu.make_async_copy(
-                src, held.at[t, pl.ds(1, TILES), pl.ds(LAYER, NX), :], sems.at[t]
+                src.at[j], held.at[t, 1 + j, pl.ds(LAYER, NX), :], sems.at[t, j]
             )
             for t, src in enumerate((low_ref, high_ref))
+            for j in range(TILES)
         ]
         for copy in copies:
             copy.start()
@@ -282,7 +283,7 @@
             out_specs=pl.BlockSpec((OWNERS, slots * EDGE, LANES), lambda d, table, odd: (d, at, 0)),
             scratch_shapes=[
                 pltpu.VMEM((2, TILES + 2, NX + 2 * LAYER, SIDE), F32),
-                pltpu.SemaphoreType.DMA((2,)),
+                pltpu.SemaphoreType.DMA((2, TILES)),
             ],
         ),
         out_shape=full((WIDE, TAPS * EDGE, LANES)),
@@ -296,7 +297,7 @@
 
 
 STRIPS = EDGE // 8
-SLABS = 3
+SLABS = 4
 GROUPS = EDGE // 8
 PIECES = [(i, q) for i in range(STRIPS) for q in range(3)]
 
@@ -412,11 +413,6 @@
             half[1 + WIDE + w, *at] = jnp.where(in_order[q], b, a)
             half[1 + 2 * WIDE + w, *at] = jnp.where(in_order[q], c, b)
         return 0
-
-    for g, group in enumerate(arrivals):
-        for copy in group:
-            copy.wait()
-        lax.fori_loop(4 * g, 4 * g + 4, arrange, 0, unroll=2)
 
     def faces_of(y, rr):
         rr = list(rr)
@@ -455,7 +451,22 @@
             rr[q] = rr[q] + v * v
         return tuple(rr)
 
-    rr = lax.fori_loop(0, EDGE, faces_of, nothing, unroll=3)
+    def span(start, count, rr):
+        def body(t, rr):
+            for k in range(count):
+                rr = faces_of(t * WIDE + start + k, rr)
+            return rr
+
+        return lax.fori_loop(0, TAPS, body, rr)
+
+    rr = nothing
+    for g, group in enumerate(arrivals):
+        for copy in group:
+            copy.wait()
+        lax.fori_loop(4 * g, 4 * g + 4, arrange, 0, unroll=2)
+        rr = span(4 * g - 1, 4, rr) if g else span(1, 2, rr)
+    for y in (0, 15, 16, 31, 32, 47):
+        rr = faces_of(y, rr)
     for at in PIECES:
         face_y[0, *piece(*at)] = none
         face_y[EDGE, *piece(*at)] = none
@@ -477,7 +488,7 @@
             total[q] = total[q] + v[i, q] * result
         return tuple(total)
 
-    alpha = divide(rr, patch_total(lax.fori_loop(0, EDGE, image_of, nothing, unroll=3)))
+    alpha = divide(rr, patch_total(lax.fori_loop(0, EDGE, image_of, nothing, unroll=4)))
 
     def residual_of(y, total):
         total = list(total)
@@ -486,7 +497,7 @@
             total[q] = total[q] + left * left
         return tuple(total)
 
-    new = patch_total(lax.fori_loop(0, EDGE, residual_of, nothing, unroll=4))
+    new = patch_total(lax.fori_loop(0, EDGE, residual_of, nothing, unroll=8))
     beta = divide(new, rr)
 
     def direction(y, i, q):

time: 147 us -> 145 us (0.986)
  Pallas kernels: 40.4 us -> 38.8 us
where the time goes in v9:
time: 145 us; the launch traced here: 144 us
  waiting for transfers between devices  77.8 us (54%)
  Pallas kernels  38.8 us (27%)
  starting transfers between devices  20.1 us (14%)
  matrix products  4.92 us (3%)
  local copies, waits for them, and re-layouts  1.8 us (1%)
    all_to_all x3, waiting for transfers between devices, on_device(): swap = lambda v: lax.all_to_all(v, 'wide', split_axis=0, concat_axis=0)  77.8 us
    all_to_all x3, starting transfers between devices, on_device(): swap = lambda v: lax.all_to_all(v, 'wide', split_axis=0, concat_axis=0)  16.4 us
    pallas_call x1, Pallas kernels, solve(): pl.pallas_call(solve_kernel, in_specs=[pl.BlockSpec(memory_space=pl.ANY),...  14.3 us
    pallas_call x2, Pallas kernels, windows(): pl.pallas_call(functools.partial(window_kernel, slots), grid_spec=pltpu.P...  11 us
    pallas_call x1, Pallas kernels, filter_exp(): pl.pallas_call(filter_kernel, grid_spec=pltpu.PrefetchScalarGridSpec(num_...  5.94 us
    dot_general x1, matrix products, on_device(): lax.dot_general(waves, waves * weights, (((0,), (0,)), ((), ())), precisi...  4.92 us
    pallas_call x1, Pallas kernels, split_rows(): pl.pallas_call(split_kernel, in_specs=[pl.BlockSpec(memory_space=pl.ANY),...  3.24 us
    ppermute x1, starting transfers between devices, on_device(): stayed = lax.ppermute(staying, 'mid', pairs(0))  2.95 us
  transfers between devices with their start and end apart: 5, of which 3 were waited for; matrix products, arithmetic and copies ran while one was open for 4% of the time, Pallas kernels for 11%

profile of v9, /device:TPU:0, one launch (start us, length us, event | category | flops | bytes accessed | tf_op | source)
XLA Modules:
  0.0 144.3 jit_solution(12432877520693372050)
XLA Ops:
  0.6 3.2 %split_rows.1 = f32[16,264,128]{2,1,0:T(8,128)} custom-call(f32[32,32,512]{2,1,0:T(8,128)} %in_ref.1, s32[1,16]{1,0:T(1,128)} %bitcast.10, s32[1,8]{1,0:T(1,128)} %bitcast.11), custom_call_target="tpu_custom_call" | custom-call | bytes 8388608 | tf_op jit(solution)/shard_map/split_rows/pallas_call | solution.py:92
  3.9 0.0 copy-start.3
  3.9 0.0 copy-start.1
  3.9 8.1 %all-to-all-start = ((f32[16,264,128]{2,1,0:T(8,128)}), f32[16,264,128]{2,1,0:T(8,128)}, u32[]{:S(2)}, u32[]{:S(2)}) async-start(f32[16,264,128]{2,1,0:T(8,128)} %split_rows.1), calls=%async_computation | async-start | bytes 4325376 | tf_op jit(solution)/shard_map/all_to_all | solution.py:626
  12.1 0.0 copy-done.3
  12.1 0.0 copy-done.1
  12.1 4.9 %fusion.in_ref = f32[512,512]{1,0:T(8,128)} fusion(f32[1024,512]{1,0:T(8,128)S(1)} %copy-done.1, f32[1024]{0:T(1024)S(1)} %maximum_multiply_fusion), kind=kOutput, calls=%fused_computation.1 | convolution fusion | flops 3221749760 | bytes 3149824 | tf_op jit(solution)/shard_map/dot_general | solution.py:632
  17.0 2.3 %bf16_pair.1 = (bf16[512,512]{1,0:T(8,128)(2,1)}, bf16[512,512]{1,0:T(8,128)(2,1)}) custom-call(f32[512,512]{1,0:T(8,128)} %fusion.in_ref), custom_call_target="tpu_custom_call" | custom-call | bytes 2097152 | tf_op jit(solution)/shard_map/bf16_pair/pallas_call | solution.py:146
  19.3 24.0 %all-to-all-done.in_ref.extra_ref = f32[16,264,128]{2,1,0:T(8,128)} async-done(((f32[16,264,128]{2,1,0:T(8,128)}), f32[16,264,128]{2,1,0:T(8,128)}, u32[]{:S(2)}, u32[]{:S(2)}) %all-to-all-start) | async-done | bytes 2162720 | tf_op jit(solution)/shard_map/all_to_all | solution.py:626
  43.3 5.9 %filter_exp.1 = (f32[16,256,128]{2,1,0:T(8,128)}, f32[4,512,128]{2,1,0:T(8,128)}, f32[4,512,128]{2,1,0:T(8,128)}, s32[2,16,128]{2,1,0:T(8,128)}) custom-call(s32[1]{0:T(128)} %bitcast.odd_ref, bf16[512,512]{1,0:T(8,128)(2,1)} %get-tuple-element.10.high_ref, bf16[512,512]{1,0:T(8,128)(2,1)} %get-tuple-element.11.low_ref, ...), custom_call_target="tpu_custom_call" | custom-call | flops 1610612736 | bytes 8388608 | tf_op jit(solution)/shard_map/filter_exp/pallas_call | solution.py:183
  49.3 3.7 %all-to-all-start.1 = ((f32[16,256,128]{2,1,0:T(8,128)}), f32[16,256,128]{2,1,0:T(8,128)S(1)}, u32[]{:S(2)}, u32[]{:S(2)}) async-start(f32[16,256,128]{2,1,0:T(8,128)} %get-tuple-element.15), calls=%async_computation.1 | async-start | bytes 4194304 | tf_op jit(solution)/shard_map/all_to_all | solution.py:626
  53.0 0.7 collective-permute-start
  53.7 3.0 %collective-permute-start.1 = (f32[4,512,128]{2,1,0:T(8,128)}, f32[4,512,128]{2,1,0:T(8,128)}, u32[]{:S(2)}, u32[]{:S(2)}) collective-permute-start(f32[4,512,128]{2,1,0:T(8,128)} %get-tuple-element.14.refs_1_), channel_id=1, source_target_pairs={{0,1},{1,0},{2,3},{3,2},{4,5},{5,4},{6,7},{7,6},{8,9},{9,8},{10,11... | collective-permute-start | bytes 3145736 | tf_op jit(solution)/shard_map/ppermute | solution.py:647
  56.7 5.9 %patch_windows.2.refs_2_ = f32[16,144,384]{2,1,0:T(8,128)} custom-call(s32[2,16,128]{2,1,0:T(8,128)} %get-tuple-element.12.table_ref, s32[1]{0:T(128)} %bitcast.odd_ref, f32[4,512,128]{2,1,0:T(8,128)} %get-tuple-element.13.refs_0_, f32[4,512,128]{2,1,0:T(8,128)} %get-tuple-element.14.refs_1_), custom_call_target="tpu_custom_call" | custom-call | bytes 12582912 | tf_op jit(solution)/shard_map/patch_windows/pallas_call | solution.py:277
  62.6 0.0 collective-permute-done.refs_0_
  62.6 0.0 copy-start.2
  62.6 0.0 collective-permute-done.1.refs_1_
  62.6 1.0 copy-done.2
  63.6 5.1 %patch_windows.3 = f32[16,144,384]{2,1,0:T(8,128)} custom-call(s32[2,16,128]{2,1,0:T(8,128)} %get-tuple-element.12.table_ref, s32[1]{0:T(128)} %bitcast.odd_ref, f32[4,512,128]{2,1,0:T(8,128)} %copy-done.2, f32[4,512,128]{2,1,0:T(8,128)} %collective-permute-done.1.refs_1_, f32[16,144,384]{2,1,0:T(8,128)} %patch_windows.2.refs_2_), custom_call_target="tpu_custom_call", output_to_operand_aliasing={{}: (4, {})} | custom-call | bytes 6291456 | tf_op jit(solution)/shard_map/patch_windows/pallas_call | solution.py:277
  68.7 0.0 copy-start.4
  68.7 0.0 copy-start
  68.7 11.9 %all-to-all-done.1.low_ref.high_ref = f32[16,256,128]{2,1,0:T(8,128)S(1)} async-done(((f32[16,256,128]{2,1,0:T(8,128)}), f32[16,256,128]{2,1,0:T(8,128)S(1)}, u32[]{:S(2)}, u32[]{:S(2)}) %all-to-all-start.1) | async-done | bytes 2097184 | tf_op jit(solution)/shard_map/all_to_all | solution.py:626
  80.6 4.5 %all-to-all-start.2 = ((f32[16,144,384]{2,1,0:T(8,128)}), f32[16,144,384]{2,1,0:T(8,128)}, u32[]{:S(2)}, u32[]{:S(2)}) async-start(f32[16,144,384]{2,1,0:T(8,128)} %patch_windows.3), calls=%async_computation.2 | async-start | bytes 7077888 | tf_op jit(solution)/shard_map/all_to_all | solution.py:626
  85.2 0.0 copy-done.4
  85.2 0.0 copy-done
  85.2 0.6 gather_fusion
  85.9 0.1 broadcast_in_dim.9
  85.9 0.1 reshape_reshape.3.later_ref
  86.0 2.1 %join_rows.1 = f32[32,32,512]{2,1,0:T(8,128)} custom-call(f32[16,256,128]{2,1,0:T(8,128)S(1)} %all-to-all-done.1.low_ref.high_ref, f32[16,256,128]{2,1,0:T(8,128)S(1)} %all-to-all-done.1.low_ref.high_ref), custom_call_target="tpu_custom_call" | custom-call | bytes 8388608 | tf_op jit(solution)/shard_map/join_rows/pallas_call | solution.py:123
  88.1 41.9 %all-to-all-done.2.half_ref = f32[16,144,384]{2,1,0:T(8,128)} async-done(((f32[16,144,384]{2,1,0:T(8,128)}), f32[16,144,384]{2,1,0:T(8,128)}, u32[]{:S(2)}, u32[]{:S(2)}) %all-to-all-start.2) | async-done | bytes 3538976 | tf_op jit(solution)/shard_map/all_to_all | solution.py:626
  130.0 14.3 %solve_patches.1 = f32[8,48,2304]{2,1,0:T(8,128)} custom-call(f32[16,144,384]{2,1,0:T(8,128)} %all-to-all-done.2.half_ref, s32[1,384]{1,0:T(1,128)S(1)} %reshape_reshape.3.later_ref), custom_call_target="tpu_custom_call" | custom-call | flops 53084160 | bytes 33554432 | tf_op jit(solution)/shard_map/solve_patches/pallas_call | solution.py:593
  (3 shorter events, 0.0 us)
Async XLA Ops:
  3.9 8.2 %copy-start.3 = (f32[512]{0:T(512)S(1)}, f32[512]{0:T(512)}, u32[]{:S(2)}) copy-start(f32[512]{0:T(512)} %param.6) | copy-start | bytes 6148
  3.9 8.2 %copy-start.1 = (f32[1024,512]{1,0:T(8,128)S(1)}, f32[1024,512]{1,0:T(8,128)}, u32[]{:S(2)}) copy-start(f32[1024,512]{1,0:T(8,128)} %constant.27.clone) | copy-start | bytes 6291460
  3.9 39.4 %all-to-all-start = ((f32[16,264,128]{2,1,0:T(8,128)}), f32[16,264,128]{2,1,0:T(8,128)}, u32[]{:S(2)}, u32[]{:S(2)}) async-start(f32[16,264,128]{2,1,0:T(8,128)} %split_rows.1), calls=%async_computation | async-start | bytes 4325376 | tf_op jit(solution)/shard_map/all_to_all | solution.py:626
  49.3 31.4 %all-to-all-start.1 = ((f32[16,256,128]{2,1,0:T(8,128)}), f32[16,256,128]{2,1,0:T(8,128)S(1)}, u32[]{:S(2)}, u32[]{:S(2)}) async-start(f32[16,256,128]{2,1,0:T(8,128)} %get-tuple-element.15), calls=%async_computation.1 | async-start | bytes 4194304 | tf_op jit(solution)/shard_map/all_to_all | solution.py:626
  53.0 9.6 %collective-permute-start = (f32[4,512,128]{2,1,0:T(8,128)}, f32[4,512,128]{2,1,0:T(8,128)S(1)}, u32[]{:S(2)}, u32[]{:S(2)}) collective-permute-start(f32[4,512,128]{2,1,0:T(8,128)} %get-tuple-element.13.refs_0_), channel_id=1, source_target_pairs={{1,2},{2,1},{3,4},{4,3},{5,6},{6,5},{9,10},{10,9},{11,12},{12,11},... | collective-permute-start | bytes 3145736 | tf_op jit(solution)/shard_map/ppermute | solution.py:646
  53.7 8.9 %collective-permute-start.1 = (f32[4,512,128]{2,1,0:T(8,128)}, f32[4,512,128]{2,1,0:T(8,128)}, u32[]{:S(2)}, u32[]{:S(2)}) collective-permute-start(f32[4,512,128]{2,1,0:T(8,128)} %get-tuple-element.14.refs_1_), channel_id=1, source_target_pairs={{0,1},{1,0},{2,3},{3,2},{4,5},{5,4},{6,7},{7,6},{8,9},{9,8},{10,11... | collective-permute-start | bytes 3145736 | tf_op jit(solution)/shard_map/ppermute | solution.py:647
  62.6 1.0 copy-start.2
  68.7 16.5 %copy-start.4 = (s32[1,1,8]{2,1,0:T(1,128)S(1)}, s32[1,1,8]{2,1,0:T(1,128)}, u32[]{:S(2)}) copy-start(s32[1,1,8]{2,1,0:T(1,128)} %param.8) | copy-start | bytes 100
  68.7 16.5 %copy-start = (s32[2,16,128]{2,1,0:T(8,128)S(1)}, s32[2,16,128]{2,1,0:T(8,128)}, u32[]{:S(2)}) copy-start(s32[2,16,128]{2,1,0:T(8,128)} %get-tuple-element.12.table_ref) | copy-start | bytes 49156
  80.6 49.3 %all-to-all-start.2 = ((f32[16,144,384]{2,1,0:T(8,128)}), f32[16,144,384]{2,1,0:T(8,128)}, u32[]{:S(2)}, u32[]{:S(2)}) async-start(f32[16,144,384]{2,1,0:T(8,128)} %patch_windows.3), calls=%async_computation.2 | async-start | bytes 7077888 | tf_op jit(solution)/shard_map/all_to_all | solution.py:626

commit v10 on v9

--- a/solution.py
+++ b/solution.py
@@ -156,35 +156,35 @@
     for k in range(2):
         table_ref[k] = extra_ref[:, k, :].astype(jnp.int32)
     lines = jnp.concatenate(
-        [in_ref[:, 0:CX, :].reshape(NX, SIDE), in_ref[:, CX:, :].reshape(NX, SIDE)], axis=1
+        [in_ref[:, k * CX:(k + 1) * CX, :].reshape(NX, SIDE) for k in range(TILES)], axis=1
     )
     high = lines.astype(jnp.bfloat16)
     low = (lines - high.astype(F32)).astype(jnp.bfloat16)
     dot = lambda a, b: jnp.dot(a, b, preferred_element_type=F32)
     small = dot(high_ref[...], low) + dot(low_ref[...], high)
     value = jnp.exp(dot(high_ref[...], high) + small)
-    sides = [value[:, :SIDE], value[:, SIDE:]]
-    for k in range(2):
+    sides = [value[:, k * SIDE:(k + 1) * SIDE] for k in range(TILES)]
+    for k in range(TILES):
         parts_ref[:, k * CX:(k + 1) * CX, :] = sides[k].reshape(WIDE, CX, SIDE)
 
     def plane(ref):
-        for k in range(2):
+        for k in range(TILES):
             ref[k] = 0.5 * sides[k]
 
-    pl.when(pl.program_id(0) < 2)(lambda: plane(first_ref))
-    pl.when(pl.program_id(0) >= 2)(lambda: plane(second_ref))
+    pl.when(pl.program_id(0) == 0)(lambda: plane(first_ref))
+    pl.when(pl.program_id(0) == 1)(lambda: plane(second_ref))
 
 
 def filter_exp(odd, pair, lines):
     whole = pl.BlockSpec((NX, NX), lambda i, odd: (0, 0))
     block = pl.BlockSpec(
-        (WIDE, 2 * CX, SIDE), lambda i, odd: (0, 2 * ((i >> 1) ^ odd[0]) + (i & 1), 0)
+        (WIDE, TILES * CX, SIDE), lambda i, odd: (0, i ^ odd[0], 0)
     )
     return pl.pallas_call(
         filter_kernel,
         grid_spec=pltpu.PrefetchScalarGridSpec(
             num_scalar_prefetch=1,
-            grid=(4,),
+            grid=(2,),
             in_specs=[
                 whole,
                 whole,
@@ -193,8 +193,8 @@
             ],
             out_specs=[
                 block,
-                pl.BlockSpec((2, NX, SIDE), lambda i, odd: (jnp.minimum(i, 1), 0, 0)),
-                pl.BlockSpec((2, NX, SIDE), lambda i, odd: (jnp.maximum(i - 2, 0), 0, 0)),
+                pl.BlockSpec((TILES, NX, SIDE), lambda i, odd: (0, 0, 0)),
+                pl.BlockSpec((TILES, NX, SIDE), lambda i, odd: (0, 0, 0)),
                 pl.BlockSpec((2, WIDE, SIDE), lambda i, odd: (0, 0, 0)),
             ],
         ),

time: 145 us -> 145 us (level)
  no operation moved by 1% of the time
where the time goes in v10:
time: 145 us; the launch traced here: 144 us
  waiting for transfers between devices  77.7 us (54%)
  Pallas kernels  38.3 us (26%)
  starting transfers between devices  20.2 us (14%)
  matrix products  4.92 us (3%)
  local copies, waits for them, and re-layouts  1.8 us (1%)
    all_to_all x3, waiting for transfers between devices, on_device(): swap = lambda v: lax.all_to_all(v, 'wide', split_axis=0, concat_axis=0)  77.6 us
    all_to_all x3, starting transfers between devices, on_device(): swap = lambda v: lax.all_to_all(v, 'wide', split_axis=0, concat_axis=0)  16.6 us
    pallas_call x1, Pallas kernels, solve(): pl.pallas_call(solve_kernel, in_specs=[pl.BlockSpec(memory_space=pl.ANY),...  14.3 us
    pallas_call x2, Pallas kernels, windows(): pl.pallas_call(functools.partial(window_kernel, slots), grid_spec=pltpu.P...  11 us
    pallas_call x1, Pallas kernels, filter_exp(): pl.pallas_call(filter_kernel, grid_spec=pltpu.PrefetchScalarGridSpec(num_...  5.44 us
    dot_general x1, matrix products, on_device(): lax.dot_general(waves, waves * weights, (((0,), (0,)), ((), ())), precisi...  4.92 us
    pallas_call x1, Pallas kernels, split_rows(): pl.pallas_call(split_kernel, in_specs=[pl.BlockSpec(memory_space=pl.ANY),...  3.24 us
    ppermute x1, starting transfers between devices, on_device(): stayed = lax.ppermute(staying, 'mid', pairs(0))  2.95 us
  transfers between devices with their start and end apart: 5, of which 3 were waited for; matrix products, arithmetic and copies ran while one was open for 4% of the time, Pallas kernels for 11%

profile of v10, /device:TPU:0, one launch (start us, length us, event | category | flops | bytes accessed | tf_op | source)
XLA Modules:
  0.0 143.9 jit_solution(3839278827492695141)
XLA Ops:
  0.6 3.2 %split_rows.1 = f32[16,264,128]{2,1,0:T(8,128)} custom-call(f32[32,32,512]{2,1,0:T(8,128)} %in_ref.1, s32[1,16]{1,0:T(1,128)} %bitcast.10, s32[1,8]{1,0:T(1,128)} %bitcast.11), custom_call_target="tpu_custom_call" | custom-call | bytes 8388608 | tf_op jit(solution)/shard_map/split_rows/pallas_call | solution.py:92
  3.9 0.0 copy-start.3
  3.9 0.0 copy-start.1
  3.9 8.1 %all-to-all-start = ((f32[16,264,128]{2,1,0:T(8,128)}), f32[16,264,128]{2,1,0:T(8,128)}, u32[]{:S(2)}, u32[]{:S(2)}) async-start(f32[16,264,128]{2,1,0:T(8,128)} %split_rows.1), calls=%async_computation | async-start | bytes 4325376 | tf_op jit(solution)/shard_map/all_to_all | solution.py:626
  12.1 0.0 copy-done.3
  12.1 0.0 copy-done.1
  12.1 4.9 %fusion.in_ref = f32[512,512]{1,0:T(8,128)} fusion(f32[1024,512]{1,0:T(8,128)S(1)} %copy-done.1, f32[1024]{0:T(1024)S(1)} %maximum_multiply_fusion), kind=kOutput, calls=%fused_computation.1 | convolution fusion | flops 3221749760 | bytes 3149824 | tf_op jit(solution)/shard_map/dot_general | solution.py:632
  17.0 2.3 %bf16_pair.1 = (bf16[512,512]{1,0:T(8,128)(2,1)}, bf16[512,512]{1,0:T(8,128)(2,1)}) custom-call(f32[512,512]{1,0:T(8,128)} %fusion.in_ref), custom_call_target="tpu_custom_call" | custom-call | bytes 2097152 | tf_op jit(solution)/shard_map/bf16_pair/pallas_call | solution.py:146
  19.3 24.0 %all-to-all-done.in_ref.extra_ref = f32[16,264,128]{2,1,0:T(8,128)} async-done(((f32[16,264,128]{2,1,0:T(8,128)}), f32[16,264,128]{2,1,0:T(8,128)}, u32[]{:S(2)}, u32[]{:S(2)}) %all-to-all-start) | async-done | bytes 2162720 | tf_op jit(solution)/shard_map/all_to_all | solution.py:626
  43.3 5.4 %filter_exp.1 = (f32[16,256,128]{2,1,0:T(8,128)}, f32[4,512,128]{2,1,0:T(8,128)}, f32[4,512,128]{2,1,0:T(8,128)}, s32[2,16,128]{2,1,0:T(8,128)}) custom-call(s32[1]{0:T(128)} %bitcast.odd_ref, bf16[512,512]{1,0:T(8,128)(2,1)} %get-tuple-element.10.high_ref, bf16[512,512]{1,0:T(8,128)(2,1)} %get-tuple-element.11.low_ref, ...), custom_call_target="tpu_custom_call" | custom-call | flops 1610612736 | bytes 8388608 | tf_op jit(solution)/shard_map/filter_exp/pallas_call | solution.py:183
  48.7 3.7 %all-to-all-start.1 = ((f32[16,256,128]{2,1,0:T(8,128)}), f32[16,256,128]{2,1,0:T(8,128)S(1)}, u32[]{:S(2)}, u32[]{:S(2)}) async-start(f32[16,256,128]{2,1,0:T(8,128)} %get-tuple-element.15), calls=%async_computation.1 | async-start | bytes 4194304 | tf_op jit(solution)/shard_map/all_to_all | solution.py:626
  52.5 0.7 collective-permute-start
  53.2 3.0 %collective-permute-start.1 = (f32[4,512,128]{2,1,0:T(8,128)}, f32[4,512,128]{2,1,0:T(8,128)}, u32[]{:S(2)}, u32[]{:S(2)}) collective-permute-start(f32[4,512,128]{2,1,0:T(8,128)} %get-tuple-element.14.refs_1_), channel_id=1, source_target_pairs={{0,1},{1,0},{2,3},{3,2},{4,5},{5,4},{6,7},{7,6},{8,9},{9,8},{10,11... | collective-permute-start | bytes 3145736 | tf_op jit(solution)/shard_map/ppermute | solution.py:647
  56.2 5.9 %patch_windows.2.refs_2_ = f32[16,144,384]{2,1,0:T(8,128)} custom-call(s32[2,16,128]{2,1,0:T(8,128)} %get-tuple-element.12.table_ref, s32[1]{0:T(128)} %bitcast.odd_ref, f32[4,512,128]{2,1,0:T(8,128)} %get-tuple-element.13.refs_0_, f32[4,512,128]{2,1,0:T(8,128)} %get-tuple-element.14.refs_1_), custom_call_target="tpu_custom_call" | custom-call | bytes 12582912 | tf_op jit(solution)/shard_map/patch_windows/pallas_call | solution.py:277
  62.0 0.0 collective-permute-done.refs_0_
  62.0 0.0 copy-start.2
  62.1 0.0 collective-permute-done.1.refs_1_
  62.1 1.0 copy-done.2
  63.0 5.1 %patch_windows.3 = f32[16,144,384]{2,1,0:T(8,128)} custom-call(s32[2,16,128]{2,1,0:T(8,128)} %get-tuple-element.12.table_ref, s32[1]{0:T(128)} %bitcast.odd_ref, f32[4,512,128]{2,1,0:T(8,128)} %copy-done.2, f32[4,512,128]{2,1,0:T(8,128)} %collective-permute-done.1.refs_1_, f32[16,144,384]{2,1,0:T(8,128)} %patch_windows.2.refs_2_), custom_call_target="tpu_custom_call", output_to_operand_aliasing={{}: (4, {})} | custom-call | bytes 6291456 | tf_op jit(solution)/shard_map/patch_windows/pallas_call | solution.py:277
  68.2 0.0 copy-start.4
  68.2 0.0 copy-start
  68.2 11.9 %all-to-all-done.1.low_ref.high_ref = f32[16,256,128]{2,1,0:T(8,128)S(1)} async-done(((f32[16,256,128]{2,1,0:T(8,128)}), f32[16,256,128]{2,1,0:T(8,128)S(1)}, u32[]{:S(2)}, u32[]{:S(2)}) %all-to-all-start.1) | async-done | bytes 2097184 | tf_op jit(solution)/shard_map/all_to_all | solution.py:626
  80.1 4.7 %all-to-all-start.2 = ((f32[16,144,384]{2,1,0:T(8,128)}), f32[16,144,384]{2,1,0:T(8,128)}, u32[]{:S(2)}, u32[]{:S(2)}) async-start(f32[16,144,384]{2,1,0:T(8,128)} %patch_windows.3), calls=%async_computation.2 | async-start | bytes 7077888 | tf_op jit(solution)/shard_map/all_to_all | solution.py:626
  84.8 0.0 copy-done.4
  84.9 0.0 copy-done
  84.9 0.6 gather_fusion
  85.5 0.1 broadcast_in_dim.9
  85.6 0.1 reshape_reshape.3.later_ref
  85.7 2.1 %join_rows.1 = f32[32,32,512]{2,1,0:T(8,128)} custom-call(f32[16,256,128]{2,1,0:T(8,128)S(1)} %all-to-all-done.1.low_ref.high_ref, f32[16,256,128]{2,1,0:T(8,128)S(1)} %all-to-all-done.1.low_ref.high_ref), custom_call_target="tpu_custom_call" | custom-call | bytes 8388608 | tf_op jit(solution)/shard_map/join_rows/pallas_call | solution.py:123
  87.8 41.7 %all-to-all-done.2.half_ref = f32[16,144,384]{2,1,0:T(8,128)} async-done(((f32[16,144,384]{2,1,0:T(8,128)}), f32[16,144,384]{2,1,0:T(8,128)}, u32[]{:S(2)}, u32[]{:S(2)}) %all-to-all-start.2) | async-done | bytes 3538976 | tf_op jit(solution)/shard_map/all_to_all | solution.py:626
  129.5 14.3 %solve_patches.1 = f32[8,48,2304]{2,1,0:T(8,128)} custom-call(f32[16,144,384]{2,1,0:T(8,128)} %all-to-all-done.2.half_ref, s32[1,384]{1,0:T(1,128)S(1)} %reshape_reshape.3.later_ref), custom_call_target="tpu_custom_call" | custom-call | flops 53084160 | bytes 33554432 | tf_op jit(solution)/shard_map/solve_patches/pallas_call | solution.py:593
  (3 shorter events, 0.0 us)
Async XLA Ops:
  3.9 8.2 %copy-start.3 = (f32[512]{0:T(512)S(1)}, f32[512]{0:T(512)}, u32[]{:S(2)}) copy-start(f32[512]{0:T(512)} %param.6) | copy-start | bytes 6148
  3.9 8.2 %copy-start.1 = (f32[1024,512]{1,0:T(8,128)S(1)}, f32[1024,512]{1,0:T(8,128)}, u32[]{:S(2)}) copy-start(f32[1024,512]{1,0:T(8,128)} %constant.27.clone) | copy-start | bytes 6291460
  3.9 39.4 %all-to-all-start = ((f32[16,264,128]{2,1,0:T(8,128)}), f32[16,264,128]{2,1,0:T(8,128)}, u32[]{:S(2)}, u32[]{:S(2)}) async-start(f32[16,264,128]{2,1,0:T(8,128)} %split_rows.1), calls=%async_computation | async-start | bytes 4325376 | tf_op jit(solution)/shard_map/all_to_all | solution.py:626
  48.7 31.4 %all-to-all-start.1 = ((f32[16,256,128]{2,1,0:T(8,128)}), f32[16,256,128]{2,1,0:T(8,128)S(1)}, u32[]{:S(2)}, u32[]{:S(2)}) async-start(f32[16,256,128]{2,1,0:T(8,128)} %get-tuple-element.15), calls=%async_computation.1 | async-start | bytes 4194304 | tf_op jit(solution)/shard_map/all_to_all | solution.py:626
  52.5 9.6 %collective-permute-start = (f32[4,512,128]{2,1,0:T(8,128)}, f32[4,512,128]{2,1,0:T(8,128)S(1)}, u32[]{:S(2)}, u32[]{:S(2)}) collective-permute-start(f32[4,512,128]{2,1,0:T(8,128)} %get-tuple-element.13.refs_0_), channel_id=1, source_target_pairs={{1,2},{2,1},{3,4},{4,3},{5,6},{6,5},{9,10},{10,9},{11,12},{12,11},... | collective-permute-start | bytes 3145736 | tf_op jit(solution)/shard_map/ppermute | solution.py:646
  53.2 8.8 %collective-permute-start.1 = (f32[4,512,128]{2,1,0:T(8,128)}, f32[4,512,128]{2,1,0:T(8,128)}, u32[]{:S(2)}, u32[]{:S(2)}) collective-permute-start(f32[4,512,128]{2,1,0:T(8,128)} %get-tuple-element.14.refs_1_), channel_id=1, source_target_pairs={{0,1},{1,0},{2,3},{3,2},{4,5},{5,4},{6,7},{7,6},{8,9},{9,8},{10,11... | collective-permute-start | bytes 3145736 | tf_op jit(solution)/shard_map/ppermute | solution.py:647
  62.0 1.0 copy-start.2
  68.2 16.7 %copy-start.4 = (s32[1,1,8]{2,1,0:T(1,128)S(1)}, s32[1,1,8]{2,1,0:T(1,128)}, u32[]{:S(2)}) copy-start(s32[1,1,8]{2,1,0:T(1,128)} %param.8) | copy-start | bytes 100
  68.2 16.7 %copy-start = (s32[2,16,128]{2,1,0:T(8,128)S(1)}, s32[2,16,128]{2,1,0:T(8,128)}, u32[]{:S(2)}) copy-start(s32[2,16,128]{2,1,0:T(8,128)} %get-tuple-element.12.table_ref) | copy-start | bytes 49156
  80.1 49.3 %all-to-all-start.2 = ((f32[16,144,384]{2,1,0:T(8,128)}), f32[16,144,384]{2,1,0:T(8,128)}, u32[]{:S(2)}, u32[]{:S(2)}) async-start(f32[16,144,384]{2,1,0:T(8,128)} %patch_windows.3), calls=%async_computation.2 | async-start | bytes 7077888 | tf_op jit(solution)/shard_map/all_to_all | solution.py:626

commit v11 on v10

--- a/solution.py
+++ b/solution.py
@@ -23,7 +23,7 @@
 SIDE = 128
 TILES = NZ // SIDE
 ROWS = 2 * TILES * CX
-OWNERS = 4
+OWNERS = 8
 UNROLL = 2
 TINY = 1e-06
 F32 = jnp.float32

time: 145 us -> 144 us (level)
  no operation moved by 1% of the time
where the time goes in v11:
time: 144 us
  waiting for transfers between devices  77.5 us (54%)
  Pallas kernels  38.1 us (26%)
  starting transfers between devices  20.2 us (14%)
  matrix products  4.92 us (3%)
  local copies, waits for them, and re-layouts  1.8 us (1%)
    all_to_all x3, waiting for transfers between devices, on_device(): swap = lambda v: lax.all_to_all(v, 'wide', split_axis=0, concat_axis=0)  77.5 us
    all_to_all x3, starting transfers between devices, on_device(): swap = lambda v: lax.all_to_all(v, 'wide', split_axis=0, concat_axis=0)  16.6 us
    pallas_call x1, Pallas kernels, solve(): pl.pallas_call(solve_kernel, in_specs=[pl.BlockSpec(memory_space=pl.ANY),...  14.3 us
    pallas_call x2, Pallas kernels, windows(): pl.pallas_call(functools.partial(window_kernel, slots), grid_spec=pltpu.P...  10.7 us
    pallas_call x1, Pallas kernels, filter_exp(): pl.pallas_call(filter_kernel, grid_spec=pltpu.PrefetchScalarGridSpec(num_...  5.44 us
    dot_general x1, matrix products, on_device(): lax.dot_general(waves, waves * weights, (((0,), (0,)), ((), ())), precisi...  4.92 us
    pallas_call x1, Pallas kernels, split_rows(): pl.pallas_call(split_kernel, in_specs=[pl.BlockSpec(memory_space=pl.ANY),...  3.24 us
    ppermute x1, starting transfers between devices, on_device(): stayed = lax.ppermute(staying, 'mid', pairs(0))  2.95 us
  transfers between devices with their start and end apart: 5, of which 3 were waited for; matrix products, arithmetic and copies ran while one was open for 4% of the time, Pallas kernels for 11%

profile of v11, /device:TPU:0, one launch (start us, length us, event | category | flops | bytes accessed | tf_op | source)
XLA Modules:
  0.0 143.5 jit_solution(13505006754812707996)
XLA Ops:
  0.6 3.2 %split_rows.1 = f32[16,264,128]{2,1,0:T(8,128)} custom-call(f32[32,32,512]{2,1,0:T(8,128)} %in_ref.1, s32[1,16]{1,0:T(1,128)} %bitcast.10, s32[1,8]{1,0:T(1,128)} %bitcast.11), custom_call_target="tpu_custom_call" | custom-call | bytes 8388608 | tf_op jit(solution)/shard_map/split_rows/pallas_call | solution.py:92
  3.9 0.0 copy-start.3
  3.9 0.0 copy-start.1
  3.9 8.1 %all-to-all-start = ((f32[16,264,128]{2,1,0:T(8,128)}), f32[16,264,128]{2,1,0:T(8,128)}, u32[]{:S(2)}, u32[]{:S(2)}) async-start(f32[16,264,128]{2,1,0:T(8,128)} %split_rows.1), calls=%async_computation | async-start | bytes 4325376 | tf_op jit(solution)/shard_map/all_to_all | solution.py:626
  12.1 0.0 copy-done.3
  12.1 0.0 copy-done.1
  12.1 4.9 %fusion.in_ref = f32[512,512]{1,0:T(8,128)} fusion(f32[1024,512]{1,0:T(8,128)S(1)} %copy-done.1, f32[1024]{0:T(1024)S(1)} %maximum_multiply_fusion), kind=kOutput, calls=%fused_computation.1 | convolution fusion | flops 3221749760 | bytes 3149824 | tf_op jit(solution)/shard_map/dot_general | solution.py:632
  17.0 2.3 %bf16_pair.1 = (bf16[512,512]{1,0:T(8,128)(2,1)}, bf16[512,512]{1,0:T(8,128)(2,1)}) custom-call(f32[512,512]{1,0:T(8,128)} %fusion.in_ref), custom_call_target="tpu_custom_call" | custom-call | bytes 2097152 | tf_op jit(solution)/shard_map/bf16_pair/pallas_call | solution.py:146
  19.3 24.0 %all-to-all-done.in_ref.extra_ref = f32[16,264,128]{2,1,0:T(8,128)} async-done(((f32[16,264,128]{2,1,0:T(8,128)}), f32[16,264,128]{2,1,0:T(8,128)}, u32[]{:S(2)}, u32[]{:S(2)}) %all-to-all-start) | async-done | bytes 2162720 | tf_op jit(solution)/shard_map/all_to_all | solution.py:626
  43.3 5.4 %filter_exp.1 = (f32[16,256,128]{2,1,0:T(8,128)}, f32[4,512,128]{2,1,0:T(8,128)}, f32[4,512,128]{2,1,0:T(8,128)}, s32[2,16,128]{2,1,0:T(8,128)}) custom-call(s32[1]{0:T(128)} %bitcast.odd_ref, bf16[512,512]{1,0:T(8,128)(2,1)} %get-tuple-element.10.high_ref, bf16[512,512]{1,0:T(8,128)(2,1)} %get-tuple-element.11.low_ref, ...), custom_call_target="tpu_custom_call" | custom-call | flops 1610612736 | bytes 8388608 | tf_op jit(solution)/shard_map/filter_exp/pallas_call | solution.py:183
  48.7 3.7 %all-to-all-start.1 = ((f32[16,256,128]{2,1,0:T(8,128)}), f32[16,256,128]{2,1,0:T(8,128)S(1)}, u32[]{:S(2)}, u32[]{:S(2)}) async-start(f32[16,256,128]{2,1,0:T(8,128)} %get-tuple-element.15), calls=%async_computation.1 | async-start | bytes 4194304 | tf_op jit(solution)/shard_map/all_to_all | solution.py:626
  52.5 0.7 collective-permute-start
  53.2 3.0 %collective-permute-start.1 = (f32[4,512,128]{2,1,0:T(8,128)}, f32[4,512,128]{2,1,0:T(8,128)}, u32[]{:S(2)}, u32[]{:S(2)}) collective-permute-start(f32[4,512,128]{2,1,0:T(8,128)} %get-tuple-element.14.refs_1_), channel_id=1, source_target_pairs={{0,1},{1,0},{2,3},{3,2},{4,5},{5,4},{6,7},{7,6},{8,9},{9,8},{10,11... | collective-permute-start | bytes 3145736 | tf_op jit(solution)/shard_map/ppermute | solution.py:647
  56.2 5.8 %patch_windows.2.refs_2_ = f32[16,144,384]{2,1,0:T(8,128)} custom-call(s32[2,16,128]{2,1,0:T(8,128)} %get-tuple-element.12.table_ref, s32[1]{0:T(128)} %bitcast.odd_ref, f32[4,512,128]{2,1,0:T(8,128)} %get-tuple-element.13.refs_0_, f32[4,512,128]{2,1,0:T(8,128)} %get-tuple-element.14.refs_1_), custom_call_target="tpu_custom_call" | custom-call | bytes 12582912 | tf_op jit(solution)/shard_map/patch_windows/pallas_call | solution.py:277
  62.0 0.0 collective-permute-done.refs_0_
  62.0 0.0 copy-start.2
  62.0 0.0 collective-permute-done.1.refs_1_
  62.0 1.0 copy-done.2
  63.0 4.9 %patch_windows.3 = f32[16,144,384]{2,1,0:T(8,128)} custom-call(s32[2,16,128]{2,1,0:T(8,128)} %get-tuple-element.12.table_ref, s32[1]{0:T(128)} %bitcast.odd_ref, f32[4,512,128]{2,1,0:T(8,128)} %copy-done.2, f32[4,512,128]{2,1,0:T(8,128)} %collective-permute-done.1.refs_1_, f32[16,144,384]{2,1,0:T(8,128)} %patch_windows.2.refs_2_), custom_call_target="tpu_custom_call", output_to_operand_aliasing={{}: (4, {})} | custom-call | bytes 6291456 | tf_op jit(solution)/shard_map/patch_windows/pallas_call | solution.py:277
  67.9 0.0 copy-start.4
  68.0 0.0 copy-start
  68.0 12.2 %all-to-all-done.1.low_ref.high_ref = f32[16,256,128]{2,1,0:T(8,128)S(1)} async-done(((f32[16,256,128]{2,1,0:T(8,128)}), f32[16,256,128]{2,1,0:T(8,128)S(1)}, u32[]{:S(2)}, u32[]{:S(2)}) %all-to-all-start.1) | async-done | bytes 2097184 | tf_op jit(solution)/shard_map/all_to_all | solution.py:626
  80.1 4.7 %all-to-all-start.2 = ((f32[16,144,384]{2,1,0:T(8,128)}), f32[16,144,384]{2,1,0:T(8,128)}, u32[]{:S(2)}, u32[]{:S(2)}) async-start(f32[16,144,384]{2,1,0:T(8,128)} %patch_windows.3), calls=%async_computation.2 | async-start | bytes 7077888 | tf_op jit(solution)/shard_map/all_to_all | solution.py:626
  84.8 0.0 copy-done.4
  84.9 0.0 copy-done
  84.9 0.6 gather_fusion
  85.5 0.1 broadcast_in_dim.9
  85.6 0.1 reshape_reshape.3.later_ref
  85.7 2.1 %join_rows.1 = f32[32,32,512]{2,1,0:T(8,128)} custom-call(f32[16,256,128]{2,1,0:T(8,128)S(1)} %all-to-all-done.1.low_ref.high_ref, f32[16,256,128]{2,1,0:T(8,128)S(1)} %all-to-all-done.1.low_ref.high_ref), custom_call_target="tpu_custom_call" | custom-call | bytes 8388608 | tf_op jit(solution)/shard_map/join_rows/pallas_call | solution.py:123
  87.8 41.2 %all-to-all-done.2.half_ref = f32[16,144,384]{2,1,0:T(8,128)} async-done(((f32[16,144,384]{2,1,0:T(8,128)}), f32[16,144,384]{2,1,0:T(8,128)}, u32[]{:S(2)}, u32[]{:S(2)}) %all-to-all-start.2) | async-done | bytes 3538976 | tf_op jit(solution)/shard_map/all_to_all | solution.py:626
  129.1 14.3 %solve_patches.1 = f32[8,48,2304]{2,1,0:T(8,128)} custom-call(f32[16,144,384]{2,1,0:T(8,128)} %all-to-all-done.2.half_ref, s32[1,384]{1,0:T(1,128)S(1)} %reshape_reshape.3.later_ref), custom_call_target="tpu_custom_call" | custom-call | flops 53084160 | bytes 33554432 | tf_op jit(solution)/shard_map/solve_patches/pallas_call | solution.py:593
  (3 shorter events, 0.0 us)
Async XLA Ops:
  3.9 8.2 %copy-start.3 = (f32[512]{0:T(512)S(1)}, f32[512]{0:T(512)}, u32[]{:S(2)}) copy-start(f32[512]{0:T(512)} %param.6) | copy-start | bytes 6148
  3.9 8.2 %copy-start.1 = (f32[1024,512]{1,0:T(8,128)S(1)}, f32[1024,512]{1,0:T(8,128)}, u32[]{:S(2)}) copy-start(f32[1024,512]{1,0:T(8,128)} %constant.27.clone) | copy-start | bytes 6291460
  3.9 39.4 %all-to-all-start = ((f32[16,264,128]{2,1,0:T(8,128)}), f32[16,264,128]{2,1,0:T(8,128)}, u32[]{:S(2)}, u32[]{:S(2)}) async-start(f32[16,264,128]{2,1,0:T(8,128)} %split_rows.1), calls=%async_computation | async-start | bytes 4325376 | tf_op jit(solution)/shard_map/all_to_all | solution.py:626
  48.7 31.4 %all-to-all-start.1 = ((f32[16,256,128]{2,1,0:T(8,128)}), f32[16,256,128]{2,1,0:T(8,128)S(1)}, u32[]{:S(2)}, u32[]{:S(2)}) async-start(f32[16,256,128]{2,1,0:T(8,128)} %get-tuple-element.15), calls=%async_computation.1 | async-start | bytes 4194304 | tf_op jit(solution)/shard_map/all_to_all | solution.py:626
  52.5 9.5 %collective-permute-start = (f32[4,512,128]{2,1,0:T(8,128)}, f32[4,512,128]{2,1,0:T(8,128)S(1)}, u32[]{:S(2)}, u32[]{:S(2)}) collective-permute-start(f32[4,512,128]{2,1,0:T(8,128)} %get-tuple-element.13.refs_0_), channel_id=1, source_target_pairs={{1,2},{2,1},{3,4},{4,3},{5,6},{6,5},{9,10},{10,9},{11,12},{12,11},... | collective-permute-start | bytes 3145736 | tf_op jit(solution)/shard_map/ppermute | solution.py:646
  53.2 8.8 %collective-permute-start.1 = (f32[4,512,128]{2,1,0:T(8,128)}, f32[4,512,128]{2,1,0:T(8,128)}, u32[]{:S(2)}, u32[]{:S(2)}) collective-permute-start(f32[4,512,128]{2,1,0:T(8,128)} %get-tuple-element.14.refs_1_), channel_id=1, source_target_pairs={{0,1},{1,0},{2,3},{3,2},{4,5},{5,4},{6,7},{7,6},{8,9},{9,8},{10,11... | collective-permute-start | bytes 3145736 | tf_op jit(solution)/shard_map/ppermute | solution.py:647
  62.0 1.0 copy-start.2
  67.9 16.9 %copy-start.4 = (s32[1,1,8]{2,1,0:T(1,128)S(1)}, s32[1,1,8]{2,1,0:T(1,128)}, u32[]{:S(2)}) copy-start(s32[1,1,8]{2,1,0:T(1,128)} %param.8) | copy-start | bytes 100
  68.0 16.9 %copy-start = (s32[2,16,128]{2,1,0:T(8,128)S(1)}, s32[2,16,128]{2,1,0:T(8,128)}, u32[]{:S(2)}) copy-start(s32[2,16,128]{2,1,0:T(8,128)} %get-tuple-element.12.table_ref) | copy-start | bytes 49156
  80.1 48.9 %all-to-all-start.2 = ((f32[16,144,384]{2,1,0:T(8,128)}), f32[16,144,384]{2,1,0:T(8,128)}, u32[]{:S(2)}, u32[]{:S(2)}) async-start(f32[16,144,384]{2,1,0:T(8,128)} %patch_windows.3), calls=%async_computation.2 | async-start | bytes 7077888 | tf_op jit(solution)/shard_map/all_to_all | solution.py:626

commit v12 on v11

--- a/solution.py
+++ b/solution.py
@@ -24,7 +24,7 @@
 TILES = NZ // SIDE
 ROWS = 2 * TILES * CX
 OWNERS = 8
-UNROLL = 2
+UNROLL = 4
 TINY = 1e-06
 F32 = jnp.float32
 

time: 144 us -> 144 us (level)
  transfers between devices with their start and end apart: 5 -> 5, of which waited for: 3 -> 3; matrix products, arithmetic and copies ran while one was open for 4% -> 4% of each run, Pallas kernels for 11% -> 10%
where the time goes in v12:
time: 144 us; the launch traced here: 143 us
  waiting for transfers between devices  77.7 us (54%)
  Pallas kernels  37.4 us (26%)
  starting transfers between devices  20.2 us (14%)
  matrix products  4.92 us (3%)
  local copies, waits for them, and re-layouts  1.8 us (1%)
    all_to_all x3, waiting for transfers between devices, on_device(): swap = lambda v: lax.all_to_all(v, 'wide', split_axis=0, concat_axis=0)  77.7 us
    all_to_all x3, starting transfers between devices, on_device(): swap = lambda v: lax.all_to_all(v, 'wide', split_axis=0, concat_axis=0)  16.6 us
    pallas_call x1, Pallas kernels, solve(): pl.pallas_call(solve_kernel, in_specs=[pl.BlockSpec(memory_space=pl.ANY),...  14.3 us
    pallas_call x2, Pallas kernels, windows(): pl.pallas_call(functools.partial(window_kernel, slots), grid_spec=pltpu.P...  10.1 us
    pallas_call x1, Pallas kernels, filter_exp(): pl.pallas_call(filter_kernel, grid_spec=pltpu.PrefetchScalarGridSpec(num_...  5.44 us
    dot_general x1, matrix products, on_device(): lax.dot_general(waves, waves * weights, (((0,), (0,)), ((), ())), precisi...  4.92 us
    pallas_call x1, Pallas kernels, split_rows(): pl.pallas_call(split_kernel, in_specs=[pl.BlockSpec(memory_space=pl.ANY),...  3.24 us
    ppermute x1, starting transfers between devices, on_device(): stayed = lax.ppermute(staying, 'mid', pairs(0))  2.95 us
  transfers between devices with their start and end apart: 5, of which 3 were waited for; matrix products, arithmetic and copies ran while one was open for 4% of the time, Pallas kernels for 10%

profile of v12, /device:TPU:0, one launch (start us, length us, event | category | flops | bytes accessed | tf_op | source)
XLA Modules:
  0.0 143.1 jit_solution(13059913104098108506)
XLA Ops:
  0.6 3.2 %split_rows.1 = f32[16,264,128]{2,1,0:T(8,128)} custom-call(f32[32,32,512]{2,1,0:T(8,128)} %in_ref.1, s32[1,16]{1,0:T(1,128)} %bitcast.10, s32[1,8]{1,0:T(1,128)} %bitcast.11), custom_call_target="tpu_custom_call" | custom-call | bytes 8388608 | tf_op jit(solution)/shard_map/split_rows/pallas_call | solution.py:92
  3.9 0.0 copy-start.3
  3.9 0.0 copy-start.1
  3.9 8.1 %all-to-all-start = ((f32[16,264,128]{2,1,0:T(8,128)}), f32[16,264,128]{2,1,0:T(8,128)}, u32[]{:S(2)}, u32[]{:S(2)}) async-start(f32[16,264,128]{2,1,0:T(8,128)} %split_rows.1), calls=%async_computation | async-start | bytes 4325376 | tf_op jit(solution)/shard_map/all_to_all | solution.py:626
  12.1 0.0 copy-done.3
  12.1 0.0 copy-done.1
  12.1 4.9 %fusion.in_ref = f32[512,512]{1,0:T(8,128)} fusion(f32[1024,512]{1,0:T(8,128)S(1)} %copy-done.1, f32[1024]{0:T(1024)S(1)} %maximum_multiply_fusion), kind=kOutput, calls=%fused_computation.1 | convolution fusion | flops 3221749760 | bytes 3149824 | tf_op jit(solution)/shard_map/dot_general | solution.py:632
  17.0 2.3 %bf16_pair.1 = (bf16[512,512]{1,0:T(8,128)(2,1)}, bf16[512,512]{1,0:T(8,128)(2,1)}) custom-call(f32[512,512]{1,0:T(8,128)} %fusion.in_ref), custom_call_target="tpu_custom_call" | custom-call | bytes 2097152 | tf_op jit(solution)/shard_map/bf16_pair/pallas_call | solution.py:146
  19.3 24.0 %all-to-all-done.in_ref.extra_ref = f32[16,264,128]{2,1,0:T(8,128)} async-done(((f32[16,264,128]{2,1,0:T(8,128)}), f32[16,264,128]{2,1,0:T(8,128)}, u32[]{:S(2)}, u32[]{:S(2)}) %all-to-all-start) | async-done | bytes 2162720 | tf_op jit(solution)/shard_map/all_to_all | solution.py:626
  43.3 5.4 %filter_exp.1 = (f32[16,256,128]{2,1,0:T(8,128)}, f32[4,512,128]{2,1,0:T(8,128)}, f32[4,512,128]{2,1,0:T(8,128)}, s32[2,16,128]{2,1,0:T(8,128)}) custom-call(s32[1]{0:T(128)} %bitcast.odd_ref, bf16[512,512]{1,0:T(8,128)(2,1)} %get-tuple-element.10.high_ref, bf16[512,512]{1,0:T(8,128)(2,1)} %get-tuple-element.11.low_ref, ...), custom_call_target="tpu_custom_call" | custom-call | flops 1610612736 | bytes 8388608 | tf_op jit(solution)/shard_map/filter_exp/pallas_call | solution.py:183
  48.7 3.7 %all-to-all-start.1 = ((f32[16,256,128]{2,1,0:T(8,128)}), f32[16,256,128]{2,1,0:T(8,128)S(1)}, u32[]{:S(2)}, u32[]{:S(2)}) async-start(f32[16,256,128]{2,1,0:T(8,128)} %get-tuple-element.15), calls=%async_computation.1 | async-start | bytes 4194304 | tf_op jit(solution)/shard_map/all_to_all | solution.py:626
  52.5 0.7 collective-permute-start
  53.2 3.0 %collective-permute-start.1 = (f32[4,512,128]{2,1,0:T(8,128)}, f32[4,512,128]{2,1,0:T(8,128)}, u32[]{:S(2)}, u32[]{:S(2)}) collective-permute-start(f32[4,512,128]{2,1,0:T(8,128)} %get-tuple-element.14.refs_1_), channel_id=1, source_target_pairs={{0,1},{1,0},{2,3},{3,2},{4,5},{5,4},{6,7},{7,6},{8,9},{9,8},{10,11... | collective-permute-start | bytes 3145736 | tf_op jit(solution)/shard_map/ppermute | solution.py:647
  56.2 5.5 %patch_windows.2.refs_2_ = f32[16,144,384]{2,1,0:T(8,128)} custom-call(s32[2,16,128]{2,1,0:T(8,128)} %get-tuple-element.12.table_ref, s32[1]{0:T(128)} %bitcast.odd_ref, f32[4,512,128]{2,1,0:T(8,128)} %get-tuple-element.13.refs_0_, f32[4,512,128]{2,1,0:T(8,128)} %get-tuple-element.14.refs_1_), custom_call_target="tpu_custom_call" | custom-call | bytes 12582912 | tf_op jit(solution)/shard_map/patch_windows/pallas_call | solution.py:277
  61.7 0.0 collective-permute-done.refs_0_
  61.7 0.0 copy-start.2
  61.7 0.0 collective-permute-done.1.refs_1_
  61.7 1.0 copy-done.2
  62.7 4.6 %patch_windows.3 = f32[16,144,384]{2,1,0:T(8,128)} custom-call(s32[2,16,128]{2,1,0:T(8,128)} %get-tuple-element.12.table_ref, s32[1]{0:T(128)} %bitcast.odd_ref, f32[4,512,128]{2,1,0:T(8,128)} %copy-done.2, f32[4,512,128]{2,1,0:T(8,128)} %collective-permute-done.1.refs_1_, f32[16,144,384]{2,1,0:T(8,128)} %patch_windows.2.refs_2_), custom_call_target="tpu_custom_call", output_to_operand_aliasing={{}: (4, {})} | custom-call | bytes 6291456 | tf_op jit(solution)/shard_map/patch_windows/pallas_call | solution.py:277
  67.3 0.0 copy-start.4
  67.3 0.0 copy-start
  67.3 12.8 %all-to-all-done.1.low_ref.high_ref = f32[16,256,128]{2,1,0:T(8,128)S(1)} async-done(((f32[16,256,128]{2,1,0:T(8,128)}), f32[16,256,128]{2,1,0:T(8,128)S(1)}, u32[]{:S(2)}, u32[]{:S(2)}) %all-to-all-start.1) | async-done | bytes 2097184 | tf_op jit(solution)/shard_map/all_to_all | solution.py:626
  80.1 4.7 %all-to-all-start.2 = ((f32[16,144,384]{2,1,0:T(8,128)}), f32[16,144,384]{2,1,0:T(8,128)}, u32[]{:S(2)}, u32[]{:S(2)}) async-start(f32[16,144,384]{2,1,0:T(8,128)} %patch_windows.3), calls=%async_computation.2 | async-start | bytes 7077888 | tf_op jit(solution)/shard_map/all_to_all | solution.py:626
  84.8 0.0 copy-done.4
  84.9 0.0 copy-done
  84.9 0.6 gather_fusion
  85.5 0.1 broadcast_in_dim.9
  85.6 0.1 reshape_reshape.3.later_ref
  85.7 2.1 %join_rows.1 = f32[32,32,512]{2,1,0:T(8,128)} custom-call(f32[16,256,128]{2,1,0:T(8,128)S(1)} %all-to-all-done.1.low_ref.high_ref, f32[16,256,128]{2,1,0:T(8,128)S(1)} %all-to-all-done.1.low_ref.high_ref), custom_call_target="tpu_custom_call" | custom-call | bytes 8388608 | tf_op jit(solution)/shard_map/join_rows/pallas_call | solution.py:123
  87.8 40.9 %all-to-all-done.2.half_ref = f32[16,144,384]{2,1,0:T(8,128)} async-done(((f32[16,144,384]{2,1,0:T(8,128)}), f32[16,144,384]{2,1,0:T(8,128)}, u32[]{:S(2)}, u32[]{:S(2)}) %all-to-all-start.2) | async-done | bytes 3538976 | tf_op jit(solution)/shard_map/all_to_all | solution.py:626
  128.7 14.3 %solve_patches.1 = f32[8,48,2304]{2,1,0:T(8,128)} custom-call(f32[16,144,384]{2,1,0:T(8,128)} %all-to-all-done.2.half_ref, s32[1,384]{1,0:T(1,128)S(1)} %reshape_reshape.3.later_ref), custom_call_target="tpu_custom_call" | custom-call | flops 53084160 | bytes 33554432 | tf_op jit(solution)/shard_map/solve_patches/pallas_call | solution.py:593
  (3 shorter events, 0.0 us)
Async XLA Ops:
  3.9 8.2 %copy-start.3 = (f32[512]{0:T(512)S(1)}, f32[512]{0:T(512)}, u32[]{:S(2)}) copy-start(f32[512]{0:T(512)} %param.6) | copy-start | bytes 6148
  3.9 8.2 %copy-start.1 = (f32[1024,512]{1,0:T(8,128)S(1)}, f32[1024,512]{1,0:T(8,128)}, u32[]{:S(2)}) copy-start(f32[1024,512]{1,0:T(8,128)} %constant.27.clone) | copy-start | bytes 6291460
  3.9 39.4 %all-to-all-start = ((f32[16,264,128]{2,1,0:T(8,128)}), f32[16,264,128]{2,1,0:T(8,128)}, u32[]{:S(2)}, u32[]{:S(2)}) async-start(f32[16,264,128]{2,1,0:T(8,128)} %split_rows.1), calls=%async_computation | async-start | bytes 4325376 | tf_op jit(solution)/shard_map/all_to_all | solution.py:626
  48.7 31.4 %all-to-all-start.1 = ((f32[16,256,128]{2,1,0:T(8,128)}), f32[16,256,128]{2,1,0:T(8,128)S(1)}, u32[]{:S(2)}, u32[]{:S(2)}) async-start(f32[16,256,128]{2,1,0:T(8,128)} %get-tuple-element.15), calls=%async_computation.1 | async-start | bytes 4194304 | tf_op jit(solution)/shard_map/all_to_all | solution.py:626
  52.5 9.2 %collective-permute-start = (f32[4,512,128]{2,1,0:T(8,128)}, f32[4,512,128]{2,1,0:T(8,128)S(1)}, u32[]{:S(2)}, u32[]{:S(2)}) collective-permute-start(f32[4,512,128]{2,1,0:T(8,128)} %get-tuple-element.13.refs_0_), channel_id=1, source_target_pairs={{1,2},{2,1},{3,4},{4,3},{5,6},{6,5},{9,10},{10,9},{11,12},{12,11},... | collective-permute-start | bytes 3145736 | tf_op jit(solution)/shard_map/ppermute | solution.py:646
  53.2 8.5 %collective-permute-start.1 = (f32[4,512,128]{2,1,0:T(8,128)}, f32[4,512,128]{2,1,0:T(8,128)}, u32[]{:S(2)}, u32[]{:S(2)}) collective-permute-start(f32[4,512,128]{2,1,0:T(8,128)} %get-tuple-element.14.refs_1_), channel_id=1, source_target_pairs={{0,1},{1,0},{2,3},{3,2},{4,5},{5,4},{6,7},{7,6},{8,9},{9,8},{10,11... | collective-permute-start | bytes 3145736 | tf_op jit(solution)/shard_map/ppermute | solution.py:647
  61.7 1.0 copy-start.2
  67.3 17.6 %copy-start.4 = (s32[1,1,8]{2,1,0:T(1,128)S(1)}, s32[1,1,8]{2,1,0:T(1,128)}, u32[]{:S(2)}) copy-start(s32[1,1,8]{2,1,0:T(1,128)} %param.8) | copy-start | bytes 100
  67.3 17.6 %copy-start = (s32[2,16,128]{2,1,0:T(8,128)S(1)}, s32[2,16,128]{2,1,0:T(8,128)}, u32[]{:S(2)}) copy-start(s32[2,16,128]{2,1,0:T(8,128)} %get-tuple-element.12.table_ref) | copy-start | bytes 49156
  80.1 48.6 %all-to-all-start.2 = ((f32[16,144,384]{2,1,0:T(8,128)}), f32[16,144,384]{2,1,0:T(8,128)}, u32[]{:S(2)}, u32[]{:S(2)}) async-start(f32[16,144,384]{2,1,0:T(8,128)} %patch_windows.3), calls=%async_computation.2 | async-start | bytes 7077888 | tf_op jit(solution)/shard_map/all_to_all | solution.py:626
